TPU v7x, 256 devices: a whole 4x4x8 slice. The times are simulated.
256 devices in a mesh: space: 64 (over x, z, core), tm: 4 (over y).
Axes of the slice: x: 4, y: 4, z: 8, core: 2. Of those that a mesh axis runs over, the one named last changes fastest.
Arguments:
- previous: bfloat16 [64, 384, 256, 128], P('tm', 'space'), may hold values from 0 to 1
- initial: float32 [384, 256, 128], P('space'), may hold values from 0 to 1
- rates: float32 [384, 256], P('space'), may hold values from 0.005 to 0.3
- transitions: float32 [64, 128, 128], replicated, may hold values from -0.02 to 0.99, as said below
Outputs:
- trajectory: bfloat16 [64, 384, 256, 128], P('tm', 'space')
Inputs may be any that keep to these rules, and one draw needn't show every extreme that they name: `transitions`: each matrix has its diagonal in 0.88 to 0.99 and small entries off it.
All inputs are finite; a program needn't handle non-finite values.
Results may differ from a plain program's by a relative error of at most 0.0015.
Values may be sent and summed in bfloat16 or wider, within the bound.
No kernel may reach another device: no remote copies, remote signals or barrier semaphores. Data moves between devices by JAX's collectives and lax.ppermute only.
A program may use at most 128 MiB of HBM per device.

v0:
```python
import jax
import jax.numpy as jnp
from jax import lax
from jax.sharding import PartitionSpec as P


def padded_2(value, sides, width):
    for axis, dim in sides:
        peers, length = (lax.axis_size(axis), value.shape[dim])
        up = [(i, (i + 1) % peers) for i in range(peers - 1)]
        down = [(j, i) for i, j in up]
        last = lax.slice_in_dim(value, length - width, length, axis=dim)
        initial = lax.slice_in_dim(value, 0, width, axis=dim)
        before = lax.ppermute(last, axis, up)
        after = lax.ppermute(initial, axis, down)
        value = jnp.concatenate([before, value, after], axis=dim)
    return value


def carried_in(part, axis, combine, identity):
    place = lax.axis_index(axis)
    gathered = jax.tree.map(lambda a: lax.all_gather(a, axis), part)
    state = jax.tree.map(lambda a, e: jnp.zeros_like(a) + jnp.asarray(e, a.dtype), part, identity)

    def one(step, state):
        return combine(
            state, jax.tree.map(lambda a: lax.dynamic_index_in_dim(a, step, 0, False), gathered)
        )

    return lax.fori_loop(0, place, one, state)


def column_sum(padded_rows):
    middle = padded_rows[1:-1]
    sides = jnp.pad(middle, ((0, 0), (1, 1), (0, 0)))
    return padded_rows[:-2] + padded_rows[2:] + sides[:, :-2] + sides[:, 2:]


def combine(earlier, later):
    high = lax.Precision.HIGHEST
    joined_map = jnp.dot(earlier[0], later[0], precision=high, preferred_element_type=jnp.float32)
    joined_decay = earlier[1] * later[1]
    carried = later[1] * jnp.dot(
        earlier[2], later[0], precision=high, preferred_element_type=jnp.float32
    )
    return (joined_map, joined_decay, carried + later[2])


def local(previous, initial, rates, transitions):
    steps = previous.shape[0]
    rows = previous.shape[1]
    columns = previous.shape[2]
    bins = previous.shape[3]
    cells = rows * columns
    high = lax.Precision.HIGHEST
    keep = (1.0 - rates)[:, :, None]
    weight = (rates * 0.25)[None, :, :, None]
    scaled = (previous.astype(jnp.float32) * weight).astype(jnp.bfloat16)
    start_index = lax.axis_index("tm") * steps
    matrices = lax.dynamic_slice_in_dim(transitions, start_index, steps, 0)
    first = jnp.where(lax.axis_index("tm") == 0, initial, jnp.zeros_like(initial))
    padded = padded_2(scaled, (("space", 1),), 1)

    def advance(state, inputs):
        rim_rows, matrix = inputs
        mixed = keep * state + column_sum(rim_rows.astype(jnp.float32))
        state = jnp.dot(
            mixed.reshape(cells, bins), matrix, precision=high, preferred_element_type=jnp.float32
        ).reshape(rows, columns, bins)
        return (state, state)

    final, local_states = lax.scan(advance, first, (padded, matrices))

    def multiply(product, matrix):
        product = jnp.dot(product, matrix, precision=high, preferred_element_type=jnp.float32)
        return (product, product)

    total_map, partial_maps = lax.scan(multiply, jnp.eye(bins, dtype=jnp.float32), matrices)
    decay = keep.reshape(cells, 1) ** steps
    own = (total_map, decay, final.reshape(cells, bins))
    identity = (
        jnp.eye(bins, dtype=jnp.float32),
        jnp.ones((cells, 1), jnp.float32),
        jnp.zeros((cells, bins), jnp.float32),
    )
    entering = carried_in(own, "tm", combine, identity)[2]
    powers = keep.reshape(1, cells, 1) ** jnp.arange(1, steps + 1, dtype=jnp.float32)[:, None, None]
    spread = jnp.einsum(
        "cb,tbd->tcd", entering, partial_maps, precision=high, preferred_element_type=jnp.float32
    )
    result = local_states.reshape(steps, cells, bins) + powers * spread
    return result.reshape(steps, rows, columns, bins).astype(jnp.bfloat16)


def solution(mesh):
    in_specs = (P("tm", "space", None, None), P("space", None, None), P("space", None), P())
    out_specs = P("tm", "space", None, None)
    return jax.shard_map(local, mesh=mesh, in_specs=in_specs, out_specs=out_specs, check_vma=False)
```

profile of v0, /device:TPU:30, one launch (start us, length us, event | category | flops | bytes accessed | tf_op | source)
XLA Modules:
  0.0 188.1 jit_solution(17396750167421872332)
XLA Ops:
  7.2 4.7 %multiply_convert_fusion = bf16[16,6,256,128]{3,2,1,0:T(8,128)(2,1)S(1)} fusion(bf16[16,6,256,128]{3,2,1,0:T(8,128)(2,1)} %param.10, f32[6,256]{1,0:T(8,128)S(1)} %get-tuple-element.216), kind=kLoop, calls=%fused_computation.27 | loop fusion | flops 9437184 | bytes 12589056 | tf_op jit(solution)/shard_map/convert_element_type | solution.py:58
  12.0 2.7 %copy-done.1 = bf16[16,6,256,128]{3,2,1,0:T(8,128)(2,1)} copy-done((bf16[16,6,256,128]{3,2,1,0:T(8,128)(2,1)}, bf16[16,6,256,128]{3,2,1,0:T(8,128)(2,1)S(1)}, u32[]{:S(2)}) %copy-start.1) | copy-done | bytes 6291480
  14.7 1.4 fusion.21
  16.1 1.9 %collective-permute-start = (bf16[16,1,256,128]{3,2,1,0:T(8,128)(2,1)}, bf16[16,1,256,128]{3,2,1,0:T(8,128)(2,1)S(1)}, u32[]{:S(2)}, u32[]{:S(2)}) collective-permute-start(bf16[16,1,256,128]{3,2,1,0:T(8,128)(2,1)} %get-tuple-element.212), channel_id=1, source_target_pairs={{0,4},{4,8},{8,12},{12,16},{16,20},{20,24},{24,28},{28,32},{32,36}... | collective-permute-start | bytes 3145736 | tf_op jit(solution)/shard_map/ppermute | solution.py:14
  18.1 7.5 %collective-permute-start.1 = (bf16[16,1,256,128]{3,2,1,0:T(8,128)(2,1)}, bf16[16,1,256,128]{3,2,1,0:T(8,128)(2,1)}, u32[]{:S(2)}, u32[]{:S(2)}) collective-permute-start(bf16[16,1,256,128]{3,2,1,0:T(8,128)(2,1)} %get-tuple-element.213), channel_id=1, source_target_pairs={{4,0},{8,4},{12,8},{16,12},{20,16},{24,20},{28,24},{32,28},{36,32}... | collective-permute-start | bytes 3145736 | tf_op jit(solution)/shard_map/ppermute | solution.py:15
  25.6 1.3 constant_dynamic-slice_fusion.1
  26.9 9.3 %collective-permute-done = bf16[16,1,256,128]{3,2,1,0:T(8,128)(2,1)S(1)} collective-permute-done((bf16[16,1,256,128]{3,2,1,0:T(8,128)(2,1)}, bf16[16,1,256,128]{3,2,1,0:T(8,128)(2,1)S(1)}, u32[]{:S(2)}, u32[]{:S(2)}) %collective-permute-start) | collective-permute-done | bytes 1048608 | tf_op jit(solution)/shard_map/ppermute | solution.py:14
  36.3 1.9 collective-permute-done.1
  38.1 6.9 %pad_maximum_fusion = bf16[16,8,256,128]{3,2,1,0:T(8,128)(2,1)} fusion(bf16[16,1,256,128]{3,2,1,0:T(8,128)(2,1)} %collective-permute-done.1, bf16[16,6,256,128]{3,2,1,0:T(8,128)(2,1)} %copy-done.1, bf16[16,1,256,128]{3,2,1,0:T(8,128)(2,1)S(1)} %collective-permute-done), kind=kLoop, calls=%fused_computation.28 | loop fusion | flops 8388608 | bytes 16777216 | tf_op jit(solution)/shard_map/concatenate | solution.py:16
  45.1 51.6 %while.39 = (s32[]{:T(128)}, f32[6,256,128]{2,1,0:T(8,128)S(1)}, f32[16,6,256,128]{3,2,1,0:T(8,128)}, f32[6,256,1]{1,0,2:T(8,128)S(1)}, bf16[16,8,256,128]{3,2,1...) while((s32[]{:T(128)}, f32[6,256,128]{2,1,0:T(8,128)S(1)}, f32[16,6,256,128]{3,2,1,0:T(8,128)}, ...), condition=%wide.region_1.2_spmd, body=%wide.region_0.1_spmd.sunk | while | flops 303235072 | bytes 10295893 | solution.py:72
  45.1 1.1 dynamic-slice_convert_fusion.2
  47.3 1.0 constant_dynamic-update-slice_fusion.2
  48.3 1.1 dynamic-slice_convert_fusion.2
  50.6 1.0 constant_dynamic-update-slice_fusion.2
  51.6 1.1 dynamic-slice_convert_fusion.2
  53.8 1.0 constant_dynamic-update-slice_fusion.2
  54.8 1.1 dynamic-slice_convert_fusion.2
  57.1 0.9 constant_dynamic-update-slice_fusion.2
  58.0 1.1 dynamic-slice_convert_fusion.2
  60.3 1.0 constant_dynamic-update-slice_fusion.2
  61.3 1.1 dynamic-slice_convert_fusion.2
  63.6 0.9 constant_dynamic-update-slice_fusion.2
  64.5 1.1 dynamic-slice_convert_fusion.2
  66.8 1.0 constant_dynamic-update-slice_fusion.2
  67.7 1.1 dynamic-slice_convert_fusion.2
  70.0 1.0 constant_dynamic-update-slice_fusion.2
  70.9 1.1 dynamic-slice_convert_fusion.2
  74.2 1.1 dynamic-slice_convert_fusion.2
  76.4 0.9 constant_dynamic-update-slice_fusion.2
  77.4 1.1 dynamic-slice_convert_fusion.2
  80.6 1.1 dynamic-slice_convert_fusion.2
  83.8 1.1 dynamic-slice_convert_fusion.2
  86.0 1.0 constant_dynamic-update-slice_fusion.2
  87.0 1.1 dynamic-slice_convert_fusion.2
  89.3 0.9 constant_dynamic-update-slice_fusion.2
  90.2 1.1 dynamic-slice_convert_fusion.2
  93.4 1.1 dynamic-slice_convert_fusion.2
  95.7 1.0 constant_dynamic-update-slice_fusion.2
  97.6 14.8 %while.40 = (s32[]{:T(128)}, f32[128,128]{0,1:T(8,128)S(1)}, f32[16,128,128]{1,2,0:T(8,128)}, f32[16,128,128]{2,1,0:T(8,128)S(1)}, s32[]{:T(128)}) while((s32[]{:T(128)}, f32[128,128]{0,1:T(8,128)S(1)}, f32[16,128,128]{1,2,0:T(8,128)}, f32[16,128,128]{2,1,0:T(8,128)S(1)}, s32[]{:T(128)}) %tuple.75), condition=%wide.region_3.4_spmd, body=%wide.region_2.3_spmd.sunk | while | flops 25165824 | bytes 394301 | solution.py:78
  112.5 13.3 %all-gather = f32[512,128]{0,1:T(8,128)S(1)} all-gather(f32[128,128]{0,1:T(8,128)S(1)} %get-tuple-element.163), channel_id=2, replica_groups=mesh['space'=64,'tm'=4] {'tm'}, dimensions={0}, use_global_device_ids=true | all-gather | bytes 327680 | tf_op jit(solution)/shard_map/all_gather | solution.py:22
  125.9 12.0 %all_gather.13 = f32[4,1536,1]{1,2,0:T(1,128)S(1)} all-gather(f32[1,1536,1]{1,2,0:T(1,128)S(1)} %mul.129), channel_id=1, replica_groups=mesh['space'=64,'tm'=4] {'tm'}, dimensions={0}, use_global_device_ids=true | all-gather | bytes 30720 | tf_op jit(solution)/shard_map/all_gather | solution.py:22
  138.1 12.6 %copy.18 = f32[16,1536,128]{1,2,0:T(8,128)} copy(f32[16,1536,128]{2,1,0:T(8,128)} %bitcast.88) | data formatting | bytes 25165824 | tf_op jit(solution)/shard_map/reshape | solution.py:91
  150.8 7.3 %while.41 = (s32[]{:T(128)}, f32[1536,128]{0,1:T(8,128)S(1)}, s32[]{:T(128)}, f32[4,1536,1]{1,2,0:T(1,128)S(1)}, f32[4,128,128]{2,1,0:T(8,128)S(1)}, /*index=5*/...) while((s32[]{:T(128)}, f32[1536,128]{0,1:T(8,128)S(1)}, s32[]{:T(128)}, f32[4,1536,1]{1,2,0:T(1,128)S(1)}, ...), condition=%wide.region_5.6_spmd, body=%wide.region_4.5_spmd.sunk | while | flops 302383104 | bytes 7164043 | solution.py:30
  150.8 1.2 constant_dynamic-slice_fusion.3
  153.3 1.2 constant_dynamic-slice_fusion.3
  155.7 1.2 constant_dynamic-slice_fusion.3
  158.1 14.5 %fusion.17 = bf16[16,1536,128]{1,2,0:T(8,128)(2,1)} fusion(f32[16,1536,128]{1,2,0:T(8,128)} %copy.18, f32[16,128,128]{1,2,0:T(8,128)} %get-tuple-element.162, f32[16,1536]{1,0:T(8,128)S(1)} %broadcast_power_fusion, f32[1536,128]{0,1:T(8,128)S(1)} %get-tuple-element.165), kind=kOutput, calls=%fused_computation.26 | convolution fusion | flops 4841275392 | bytes 20807680 | tf_op jit(solution)/shard_map/cb,tbd->tcd/dot_general | solution.py:88
  172.6 8.6 %copy.19 = bf16[16,1536,128]{2,1,0:T(8,128)(2,1)} copy(bf16[16,1536,128]{1,2,0:T(8,128)(2,1)} %fusion.17) | data formatting | bytes 12582912 | tf_op jit(solution)/shard_map/convert_element_type | solution.py:92
  (113 shorter events, 42.4 us)
Async XLA Ops:
  6.5 144.2 %all-gather.3.cloned.1.call-start = ((), (), s32[]{:S(2)}) async-start(), calls=%async_computation | async-start | bytes 3932160 | tf_op jit(solution)/shard_map/all_gather | solution.py:22
  12.0 2.7 %copy-start.1 = (bf16[16,6,256,128]{3,2,1,0:T(8,128)(2,1)}, bf16[16,6,256,128]{3,2,1,0:T(8,128)(2,1)S(1)}, u32[]{:S(2)}) copy-start(bf16[16,6,256,128]{3,2,1,0:T(8,128)(2,1)S(1)} %multiply_convert_fusion) | copy-start | bytes 18874372
  16.1 20.1 %collective-permute-start = (bf16[16,1,256,128]{3,2,1,0:T(8,128)(2,1)}, bf16[16,1,256,128]{3,2,1,0:T(8,128)(2,1)S(1)}, u32[]{:S(2)}, u32[]{:S(2)}) collective-permute-start(bf16[16,1,256,128]{3,2,1,0:T(8,128)(2,1)} %get-tuple-element.212), channel_id=1, source_target_pairs={{0,4},{4,8},{8,12},{12,16},{16,20},{20,24},{24,28},{28,32},{32,36}... | collective-permute-start | bytes 3145736 | tf_op jit(solution)/shard_map/ppermute | solution.py:14
  18.1 20.1 %collective-permute-start.1 = (bf16[16,1,256,128]{3,2,1,0:T(8,128)(2,1)}, bf16[16,1,256,128]{3,2,1,0:T(8,128)(2,1)}, u32[]{:S(2)}, u32[]{:S(2)}) collective-permute-start(bf16[16,1,256,128]{3,2,1,0:T(8,128)(2,1)} %get-tuple-element.213), channel_id=1, source_target_pairs={{4,0},{8,4},{12,8},{16,12},{20,16},{24,20},{28,24},{32,28},{36,32}... | collective-permute-start | bytes 3145736 | tf_op jit(solution)/shard_map/ppermute | solution.py:15
  96.7 0.9 copy-start
Sparse Core Ops, SparseCore 0:
  97.7 43.0 all-gather.2
where the time goes:
time: 190 us; the launch traced here: 188 us
  local copies, waits for them, and re-layouts  48.7 us (26%)
  matrix products  44.1 us (23%)
  other arithmetic  35.2 us (19%)
  blocking collectives  25.3 us (13%)
  between operations  13.5 us (7%)
  waiting for transfers between devices  11.2 us (6%)
  starting transfers between devices  9.38 us (5%)
    all_gather x2, blocking collectives, carried_in(): gathered = jax.tree.map(lambda a: lax.all_gather(a, axis), part)  25.3 us
    convert_element_type x16, other arithmetic, advance(): mixed = keep * state + column_sum(rim_rows.astype(jnp.float32))  17.8 us
    dynamic_update_slice x16, local copies, waits for them, and re-layouts, local(): final, local_states = lax.scan(advance, first, (padded, matrices))  15.3 us
    dot_general x16, matrix products, multiply(): jnp.dot(product, matrix, precision=high, preferred_element_type=jnp.float32)  14.7 us
    dot_general x1, matrix products, local(): jnp.einsum('cb,tbd->tcd', entering, partial_maps, precision=high, preferr...  14.5 us
    reshape x1, local copies, waits for them, and re-layouts, local(): result = local_states.reshape(steps, cells, bins) + powers * spread  12.6 us
    dot_general x16, matrix products, advance(): jnp.dot(mixed.reshape(cells, bins), matrix, precision=high, preferred_ele...  12.4 us
    ppermute x1, waiting for transfers between devices, padded_2(): before = lax.ppermute(last, axis, up)  9.35 us
  transfers between devices with their start and end apart: 3, of which 2 were waited for; matrix products, arithmetic and copies ran while one was open for 15% of the time, Pallas kernels for 0%

commit v1 on v0

v1 whole, which is shorter than its diff:
```python
import functools

import jax
import jax.numpy as jnp
from jax import lax
from jax.experimental import pallas as pl
from jax.experimental.pallas import tpu as pltpu
from jax.sharding import PartitionSpec as P

F32, BF16 = jnp.float32, jnp.bfloat16
PEAK = 2.0**15.5
CHUNK = 128
MIB = 1 << 20


def split(value):
    high = value.astype(BF16)
    low = (value - high.astype(F32)).astype(BF16)
    return high, low


def left(value):
    return jnp.concatenate(split(value), axis=1)


def right(matrix):
    both = jnp.concatenate(split(matrix), axis=1)
    return jnp.concatenate([both, both], axis=0)


def times(value, matrix):
    n = matrix.shape[1] // 2
    both = jnp.dot(left(value), matrix, preferred_element_type=F32)
    return both[:, :n] + both[:, n:]


def column(rates_ref, row, bins):
    line = rates_ref[pl.ds(row, 1), :]
    return jnp.broadcast_to(line, (bins, line.shape[1])).T


def place(q, rows, odd):
    return q + odd * (rows - 1 - 2 * q)


def encode(value, scale):
    u = value * (PEAK / scale)
    g = u * u
    g = g * g
    g = g * g
    return jnp.where(value < 0, -g, g).astype(BF16)


def decode(code, scale):
    g = code.astype(F32)
    root = jnp.exp(jnp.log(jnp.abs(g)) * 0.125) * (scale * (1.0 / PEAK))
    return jnp.where(g < 0, -root, root)


def sweep_kernel(
    own, calc, halo_q, steps, rows,
    prev_ref, halo_ref, init_ref, rates_ref, trans_ref,
    loc_ref, code_ref,
    pbuf, hbuf, ibuf, tbuf, grid, weight, keep, rhs, psem, hsem, isem, tsem,
):
    odd = lax.rem(lax.axis_index("space"), 2)
    block = lax.axis_index("tm")
    columns, bins = pbuf.shape[2], pbuf.shape[3]
    base = min(min(own), halo_q)
    whole = len(own) == rows

    def fetch(t):
        if whole:
            return [pltpu.make_async_copy(prev_ref.at[t], pbuf.at[t], psem.at[t])]
        return [
            pltpu.make_async_copy(prev_ref.at[t, place(q, rows, odd)], pbuf.at[t, i], psem.at[t])
            for i, q in enumerate(own)
        ]

    matrices = pltpu.make_async_copy(trans_ref.at[pl.ds(block * steps, steps)], tbuf, tsem)
    start = pltpu.make_async_copy(init_ref, ibuf, isem)
    halo = pltpu.make_async_copy(halo_ref, hbuf, hsem)
    matrices.start()
    start.start()
    for t in range(steps):
        for copy in fetch(t):
            copy.start()
    halo.start()

    for i, q in enumerate(own):
        share = column(rates_ref, place(q, rows, odd), bins)
        weight[i] = share * 0.25
        if q in calc:
            keep[q - calc[0]] = 1.0 - share
    for i in range(grid.shape[0]):
        grid[i, 0:8] = jnp.zeros((8, bins), F32)
        grid[i, columns + 8 : columns + 16] = jnp.zeros((8, bins), F32)
    matrices.wait()
    for t in range(steps):
        rhs[t] = right(tbuf[t])
    start.wait()
    for n, q in enumerate(calc):
        first = ibuf[place(q, rows, odd)]
        loc_ref[0, n] = jnp.where(block == 0, first, jnp.zeros_like(first))
    halo.wait()

    def step(t, carry):
        for copy in fetch(t):
            copy.wait()
        for i, q in enumerate(own):
            source = pbuf[t, place(q, rows, odd) if whole else i].astype(F32)
            grid[q - base, 8 : 8 + columns] = (source * weight[i]).astype(BF16).astype(F32)
        grid[halo_q - base, 8 : 8 + columns] = hbuf[t].astype(F32)
        matrix = rhs[t]
        for n, q in enumerate(calc):
            g = q - base
            for c in range(0, columns, CHUNK):
                at = slice(8 + c, 8 + c + CHUNK)
                inflow = (grid[g - 1, at] + grid[g + 1, at]) + (
                    grid[g, 7 + c : 7 + c + CHUNK] + grid[g, 9 + c : 9 + c + CHUNK]
                )
                cells = slice(c, c + CHUNK)
                mixed = keep[n, cells] * loc_ref[t, n, cells] + inflow
                loc_ref[t + 1, n, cells] = times(mixed, matrix)
        return carry

    lax.fori_loop(0, steps, step, 0)

    top = jnp.zeros((columns, bins), F32)
    for n in range(len(calc)):
        top = jnp.maximum(top, jnp.abs(loc_ref[steps, n]))
    scale = (jnp.max(top, keepdims=True) * 1.01 + 1e-30).astype(BF16).astype(F32)
    for n in range(len(calc)):
        code_ref[n * columns : (n + 1) * columns] = encode(loc_ref[steps, n], scale)
    code_ref[len(calc) * columns :] = jnp.broadcast_to(scale, (16, bins)).astype(BF16)


def sweep(previous, halo, initial, rates, transitions, own, calc, halo_q):
    steps, rows, columns, bins = previous.shape
    n = len(calc)
    anywhere = pl.BlockSpec(memory_space=pl.ANY)
    vmem = pl.BlockSpec(memory_space=pltpu.VMEM)
    return pl.pallas_call(
        functools.partial(sweep_kernel, own, calc, halo_q, steps, rows),
        out_shape=[
            pltpu.VMEM((steps + 1, n, columns, bins), F32),
            jax.ShapeDtypeStruct((n * columns + 16, bins), BF16),
        ],
        in_specs=[anywhere, anywhere, anywhere, vmem, anywhere],
        out_specs=[vmem, vmem],
        scratch_shapes=[
            pltpu.VMEM((steps, len(own), columns, bins), BF16),
            pltpu.VMEM((steps, columns, bins), BF16),
            pltpu.VMEM((rows, columns, bins), F32),
            pltpu.VMEM((steps, bins, bins), F32),
            pltpu.VMEM((len(own) + 1, columns + 16, bins), F32),
            pltpu.VMEM((len(own), columns, bins), F32),
            pltpu.VMEM((n, columns, bins), F32),
            pltpu.VMEM((steps, 2 * bins, 2 * bins), BF16),
            pltpu.SemaphoreType.DMA((steps,)),
            pltpu.SemaphoreType.DMA,
            pltpu.SemaphoreType.DMA,
            pltpu.SemaphoreType.DMA,
        ],
        compiler_params=pltpu.CompilerParams(vmem_limit_bytes=24 * MIB),
        cost_estimate=pl.CostEstimate(
            flops=8 * steps * n * columns * bins * bins,
            bytes_accessed=steps * len(own) * columns * bins * 2,
            transcendentals=0,
        ),
        name=f"sweep{n}",
    )(previous, halo, initial, rates, transitions)


def product_kernel(steps, trans_ref, prefix_ref, total_ref, tbuf, work, sems):
    block = lax.axis_index("tm")
    bins = tbuf.shape[2]
    copies = []
    for back in range(3):
        at = pl.ds(jnp.maximum(block - back, 0) * steps, steps)
        copies.append(
            pltpu.make_async_copy(
                trans_ref.at[at], tbuf.at[pl.ds(back * steps, steps)], sems.at[back]
            )
        )
        copies[-1].start()
    for copy in copies:
        copy.wait()
    for back in range(3):
        work[back] = tbuf[back * steps]
    prefix_ref[0] = right(tbuf[0])

    def step(t, carry):
        for back in range(3):
            work[back] = times(work[back], right(tbuf[back * steps + t]))
        prefix_ref[t] = right(work[0])
        return carry

    lax.fori_loop(1, steps, step, 0)
    total_ref[0] = right(work[1])
    total_ref[1] = right(work[2])


def products(transitions, steps):
    bins = transitions.shape[1]
    vmem = pl.BlockSpec(memory_space=pltpu.VMEM)
    return pl.pallas_call(
        functools.partial(product_kernel, steps),
        out_shape=[
            pltpu.VMEM((steps, 2 * bins, 2 * bins), BF16),
            pltpu.VMEM((2, 2 * bins, 2 * bins), BF16),
        ],
        in_specs=[pl.BlockSpec(memory_space=pl.ANY)],
        out_specs=[vmem, vmem],
        scratch_shapes=[
            pltpu.VMEM((3 * steps, bins, bins), F32),
            pltpu.VMEM((3, bins, bins), F32),
            pltpu.SemaphoreType.DMA((3,)),
        ],
        compiler_params=pltpu.CompilerParams(vmem_limit_bytes=16 * MIB),
        cost_estimate=pl.CostEstimate(
            flops=24 * steps * bins**3 * 4, bytes_accessed=4 * MIB, transcendentals=0
        ),
        name="products",
    )(transitions)


def spread_kernel(
    chunks, rows,
    a1_ref, b1_ref, c1_ref, a0_ref, b0_ref, c0_ref, loc1_ref, loc0_ref, rates_ref, prefix_ref, total_ref,
    out_ref,
    entering, keep, power, stage, sems,
):
    odd = lax.rem(lax.axis_index("space"), 2)
    steps, _, columns, bins = stage.shape
    codes = ((a1_ref, b1_ref, c1_ref), (a0_ref, b0_ref, c0_ref))
    locs = (loc1_ref, loc0_ref)

    for calc, refs in zip(chunks, codes):
        last = len(calc) * columns
        scales = [ref[last : last + 16].astype(F32)[0:1, 0:1] for ref in refs]
        for n, q in enumerate(calc):
            held = 1.0 - column(rates_ref, place(q, rows, odd), bins)
            keep[q] = held
            power[q] = jnp.ones_like(held)
            for _ in range(4):
                held = held * held
            at = slice(n * columns, (n + 1) * columns)
            near, mid, far = [decode(ref[at], scale) for ref, scale in zip(refs, scales)]
            state = mid + held * times(far, total_ref[1])
            state = near + held * times(state, total_ref[0])
            entering[q] = left(state)

    def step(t, carry):
        matrix = prefix_ref[t]
        for calc, loc_ref in zip(chunks, locs):
            for n, q in enumerate(calc):
                row = place(q, rows, odd)
                for c in range(0, columns, CHUNK):
                    cells = slice(c, c + CHUNK)
                    both = jnp.dot(entering[q, cells], matrix, preferred_element_type=F32)
                    factor = power[q, cells] * keep[q, cells]
                    power[q, cells] = factor
                    share = factor * (both[:, :bins] + both[:, bins:])
                    stage[t, row, cells] = (loc_ref[t + 1, n, cells] + share).astype(BF16)
        pltpu.make_async_copy(stage.at[t], out_ref.at[t], sems.at[t]).start()
        return carry

    lax.fori_loop(0, steps, step, 0)
    for t in range(steps):
        pltpu.make_async_copy(stage.at[t], out_ref.at[t], sems.at[t]).wait()


def spread(chunks, codes1, codes0, loc1, loc0, rates, prefix, total):
    steps, columns, bins = loc1.shape[0] - 1, loc1.shape[2], loc1.shape[3]
    rows = rates.shape[0]
    vmem = pl.BlockSpec(memory_space=pltpu.VMEM)
    return pl.pallas_call(
        functools.partial(spread_kernel, chunks, rows),
        out_shape=jax.ShapeDtypeStruct((steps, rows, columns, bins), BF16),
        in_specs=[vmem] * 11,
        out_specs=pl.BlockSpec(memory_space=pl.ANY),
        scratch_shapes=[
            pltpu.VMEM((rows, columns, 2 * bins), BF16),
            pltpu.VMEM((rows, columns, bins), F32),
            pltpu.VMEM((rows, columns, bins), F32),
            pltpu.VMEM((steps, rows, columns, bins), BF16),
            pltpu.SemaphoreType.DMA((steps,)),
        ],
        compiler_params=pltpu.CompilerParams(vmem_limit_bytes=24 * MIB),
        cost_estimate=pl.CostEstimate(
            flops=8 * steps * rows * columns * bins * bins,
            bytes_accessed=steps * rows * columns * bins * 2,
            transcendentals=0,
        ),
        name="spread",
    )(*codes1, *codes0, loc1, loc0, rates, prefix, total)


def local(previous, initial, rates, transitions):
    steps, rows, columns, bins = previous.shape
    strips, blocks = lax.axis_size("space"), lax.axis_size("tm")
    odd = lax.rem(lax.axis_index("space"), 2)

    def edge(row):
        taken = lax.dynamic_index_in_dim(previous, row, 1, False).astype(F32)
        share = lax.dynamic_index_in_dim(rates, row, 0, False) * 0.25
        return (taken * share[None, :, None]).astype(BF16)

    between = [(i, i + 1) for i in range(1, strips - 1, 2)]
    within = [(i, i + 1) for i in range(0, strips, 2)]
    outer = lax.ppermute(edge(place(0, rows, odd)), "space", between + [(j, i) for i, j in between])
    inner = lax.ppermute(edge(place(rows - 1, rows, odd)), "space", within + [(j, i) for i, j in within])

    def send(code):
        return [
            lax.ppermute(code, "tm", [(i, i + hop) for i in range(blocks - hop)])
            for hop in range(1, blocks)
        ]

    most, rest = tuple(range(1, rows)), (0,)
    loc1, code1 = sweep(previous, inner, initial, rates, transitions, tuple(range(rows)), most, rows)
    codes1 = send(code1)
    prefix, total = products(transitions, steps)
    loc0, code0 = sweep(previous, outer, initial, rates, transitions, (0, 1), rest, -1)
    codes0 = send(code0)
    return spread((most, rest), codes1, codes0, loc1, loc0, rates, prefix, total)


def solution(mesh):
    in_specs = (P("tm", "space", None, None), P("space", None, None), P("space", None), P())
    out_specs = P("tm", "space", None, None)
    return jax.shard_map(local, mesh=mesh, in_specs=in_specs, out_specs=out_specs, check_vma=False)
```

time: 190 us -> 78.4 us (0.41)
  the two profiles are of different devices: /device:TPU:30 before, /device:TPU:14 now
where the time goes in v1:
time: 78.4 us; the launch traced here: 77.7 us
  Pallas kernels  31.7 us (40%)
  starting transfers between devices  19.5 us (25%)
  waiting for transfers between devices  19.3 us (25%)
  local copies, waits for them, and re-layouts  3.93 us (5%)
  other arithmetic  3.09 us (4%)
    pallas_call x2, Pallas kernels, sweep(): pl.pallas_call(functools.partial(sweep_kernel, own, calc, halo_q, steps,...  19.4 us
    ppermute x1, waiting for transfers between devices, local(): lax.ppermute(edge(place(0, rows, odd)), 'space', between + [(j, i) for i,...  12.4 us
    ppermute x6, starting transfers between devices, send(): lax.ppermute(code, 'tm', [(i, i + hop) for i in range(blocks - hop)])  11.9 us
    pallas_call x1, Pallas kernels, spread(): pl.pallas_call(functools.partial(spread_kernel, chunks, rows), out_shape=...  8.61 us
    ppermute x1, starting transfers between devices, local(): lax.ppermute(edge(place(0, rows, odd)), 'space', between + [(j, i) for i,...  7.47 us
    ppermute x6, waiting for transfers between devices, send(): lax.ppermute(code, 'tm', [(i, i + hop) for i in range(blocks - hop)])  6.96 us
    unnamed x10, local copies, waits for them, and re-layouts  3.93 us
    pallas_call x1, Pallas kernels, products(): pl.pallas_call(functools.partial(product_kernel, steps), out_shape=[pltpu...  3.64 us
  transfers between devices with their start and end apart: 8, of which 2 were waited for; matrix products, arithmetic and copies ran while one was open for 0% of the time, Pallas kernels for 30%

profile of v1, /device:TPU:14, one launch (start us, length us, event | category | flops | bytes accessed | tf_op | source)
XLA Modules:
  0.0 77.7 jit_solution(800938800342444192)
XLA Ops:
  0.0 0.0 copy-start.4
  0.0 0.8 %dynamic-slice_multiply_fusion = (f32[1,256]{1,0:T(1,128)S(1)}, f32[1,256]{1,0:T(1,128)S(1)}) fusion(f32[6,256]{1,0:T(8,128)} %rates_ref.5, s32[]{:T(128)S(6)} %select_n.11, s32[]{:T(128)S(6)} %select_n.10), kind=kLoop, calls=%fused_computation.4 | loop fusion | flops 512 | bytes 4104 | tf_op jit(solution)/shard_map/mul | solution.py:307
  0.8 0.0 copy-start.2
  0.8 2.3 %fusion = (bf16[16,256,128]{2,1,0:T(8,128)(2,1)S(1)}, bf16[16,256,128]{2,1,0:T(8,128)(2,1)S(1)}) fusion(f32[256]{0:T(256)S(1)} %bitcast.12, bf16[16,6,256,128]{3,2,1,0:T(8,128)(2,1)} %prev_ref.3, s32[]{:T(128)S(6)} %select_n.11, f32[256]{0:T(256)S(1)} %bitcast.13, s32[]{:T(128)S(6)} %select_n.10), kind=kLoop, calls=%fused_computation.1 | loop fusion | flops 3145728 | bytes 4196360 | tf_op jit(solution)/shard_map/convert_element_type | solution.py:308
  3.1 7.5 %collective-permute-start.4 = (bf16[16,256,128]{2,1,0:T(8,128)(2,1)S(1)}, bf16[16,256,128]{2,1,0:T(8,128)(2,1)S(1)}, u32[]{:S(2)}, u32[]{:S(2)}) collective-permute-start(bf16[16,256,128]{2,1,0:T(8,128)(2,1)S(1)} %get-tuple-element.17), channel_id=1, source_target_pairs={{4,8},{12,16},{20,24},{28,32},{36,40},{44,48},{52,56},{60,64},{68,... | collective-permute-start | bytes 3145736 | tf_op jit(solution)/shard_map/ppermute | solution.py:312
  10.6 0.1 collective-permute-start
  10.7 12.4 %collective-permute-done.4.halo_ref = bf16[16,256,128]{2,1,0:T(8,128)(2,1)S(1)} collective-permute-done((bf16[16,256,128]{2,1,0:T(8,128)(2,1)S(1)}, bf16[16,256,128]{2,1,0:T(8,128)(2,1)S(1)}, u32[]{:S(2)}, u32[]{:S(2)}) %collective-permute-start.4) | collective-permute-done | bytes 1048608 | tf_op jit(solution)/shard_map/ppermute | solution.py:312
  23.1 0.0 copy-done.4
  23.1 0.0 copy-done.2
  23.1 0.0 copy-start
  23.1 2.8 %copy-done = bf16[16,6,256,128]{3,2,1,0:T(8,128)(2,1)S(1)} copy-done((bf16[16,6,256,128]{3,2,1,0:T(8,128)(2,1)S(1)}, bf16[16,6,256,128]{3,2,1,0:T(8,128)(2,1)}, u32[]{:S(2)}) %copy-start) | copy-done | bytes 6291480
  25.8 0.0 copy-start.3
  25.8 1.1 %copy-done.3 = f32[6,256,128]{2,1,0:T(8,128)S(1)} copy-done((f32[6,256,128]{2,1,0:T(8,128)S(1)}, f32[6,256,128]{2,1,0:T(8,128)}, u32[]{:S(2)}) %copy-start.3) | copy-done | bytes 786456
  27.0 0.0 copy-start.1
  27.0 7.3 %sweep1.1 = (f32[17,1,256,128]{3,2,1,0:T(8,128)S(1)}, bf16[272,128]{1,0:T(8,128)(2,1)S(1)}) custom-call(bf16[16,6,256,128]{3,2,1,0:T(8,128)(2,1)S(1)} %copy-done, bf16[16,256,128]{2,1,0:T(8,128)(2,1)S(1)} %collective-permute-done.4.halo_ref, f32[6,256,128]{2,1,0:T(8,128)S(1)} %copy-done.3, f32[6,256]{1,0:T(8,128)S(1)} %copy-done.4, f32[64,128,128]{2,1,0:T(8,128)S(1)} %copy-done.2), custom_call_target="tpu_custom_call" | custom-call | flops 536870912 | bytes 2097152 | tf_op jit(solution)/shard_map/sweep1/pallas_call | solution.py:143
  34.3 0.7 collective-permute-start.7
  35.0 0.0 collective-permute-done.halo_ref
  35.0 0.0 copy-done.1
  35.0 12.1 %sweep5.1 = (f32[17,5,256,128]{3,2,1,0:T(8,128)S(1)}, bf16[1296,128]{1,0:T(8,128)(2,1)S(1)}) custom-call(bf16[16,6,256,128]{3,2,1,0:T(8,128)(2,1)S(1)} %copy-done.1, bf16[16,256,128]{2,1,0:T(8,128)(2,1)S(1)} %collective-permute-done.halo_ref, f32[6,256,128]{2,1,0:T(8,128)S(1)} %copy-done.3, f32[6,256]{1,0:T(8,128)S(1)} %copy-done.4, ...), custom_call_target="tpu_custom_call" | custom-call | flops 2684354560 | bytes 6291456 | tf_op jit(solution)/shard_map/sweep5/pallas_call | solution.py:143
  47.1 0.7 collective-permute-start.3
  47.8 5.5 %collective-permute-start.2 = (bf16[1296,128]{1,0:T(8,128)(2,1)S(1)}, bf16[1296,128]{1,0:T(8,128)(2,1)S(1)}, u32[]{:S(2)}, u32[]{:S(2)}) collective-permute-start(bf16[1296,128]{1,0:T(8,128)(2,1)S(1)} %get-tuple-element.11), channel_id=1, source_target_pairs={{0,2},{1,3},{4,6},{5,7},{8,10},{9,11},{12,14},{13,15},{16,18},{17,... | collective-permute-start | bytes 995336 | tf_op jit(solution)/shard_map/ppermute | solution.py:317
  53.3 1.9 %collective-permute-start.1 = (bf16[1296,128]{1,0:T(8,128)(2,1)S(1)}, bf16[1296,128]{1,0:T(8,128)(2,1)S(1)}, u32[]{:S(2)}, u32[]{:S(2)}) collective-permute-start(bf16[1296,128]{1,0:T(8,128)(2,1)S(1)} %get-tuple-element.11), channel_id=1, source_target_pairs={{0,1},{1,2},{2,3},{4,5},{5,6},{6,7},{8,9},{9,10},{10,11},{12,13},{... | collective-permute-start | bytes 995336 | tf_op jit(solution)/shard_map/ppermute | solution.py:317
  55.2 1.3 %collective-permute-start.6 = (bf16[272,128]{1,0:T(8,128)(2,1)S(1)}, bf16[272,128]{1,0:T(8,128)(2,1)S(1)}, u32[]{:S(2)}, u32[]{:S(2)}) collective-permute-start(bf16[272,128]{1,0:T(8,128)(2,1)S(1)} %get-tuple-element.12), channel_id=1, source_target_pairs={{0,2},{1,3},{4,6},{5,7},{8,10},{9,11},{12,14},{13,15},{16,18},{17,... | collective-permute-start | bytes 208904 | tf_op jit(solution)/shard_map/ppermute | solution.py:317
  56.5 0.0 collective-permute-done.7.c0_ref
  56.5 1.9 %collective-permute-start.5 = (bf16[272,128]{1,0:T(8,128)(2,1)S(1)}, bf16[272,128]{1,0:T(8,128)(2,1)S(1)}, u32[]{:S(2)}, u32[]{:S(2)}) collective-permute-start(bf16[272,128]{1,0:T(8,128)(2,1)S(1)} %get-tuple-element.12), channel_id=1, source_target_pairs={{0,1},{1,2},{2,3},{4,5},{5,6},{6,7},{8,9},{9,10},{10,11},{12,13},{... | collective-permute-start | bytes 208904 | tf_op jit(solution)/shard_map/ppermute | solution.py:317
  58.4 3.6 %products.1 = (bf16[16,256,256]{2,1,0:T(8,128)(2,1)S(1)}, bf16[2,256,256]{2,1,0:T(8,128)(2,1)S(1)}) custom-call(f32[64,128,128]{2,1,0:T(8,128)S(1)} %copy-done.2), custom_call_target="tpu_custom_call" | custom-call | flops 3221225472 | bytes 4194304 | tf_op jit(solution)/shard_map/products/pallas_call | solution.py:207
  62.1 0.0 collective-permute-done.6.b0_ref
  62.1 6.9 %collective-permute-done.5.a0_ref = bf16[272,128]{1,0:T(8,128)(2,1)S(1)} collective-permute-done((bf16[272,128]{1,0:T(8,128)(2,1)S(1)}, bf16[272,128]{1,0:T(8,128)(2,1)S(1)}, u32[]{:S(2)}, u32[]{:S(2)}) %collective-permute-start.5) | collective-permute-done | bytes 69664 | tf_op jit(solution)/shard_map/ppermute | solution.py:317
  69.1 0.0 collective-permute-done.3.c1_ref
  69.1 0.0 collective-permute-done.2.b1_ref
  69.1 0.0 collective-permute-done.1.a1_ref
  69.1 8.6 %spread.1 = bf16[16,6,256,128]{3,2,1,0:T(8,128)(2,1)} custom-call(bf16[1296,128]{1,0:T(8,128)(2,1)S(1)} %collective-permute-done.1.a1_ref, bf16[1296,128]{1,0:T(8,128)(2,1)S(1)} %collective-permute-done.2.b1_ref, bf16[1296,128]{1,0:T(8,128)(2,1)S(1)} %collective-permute-done.3.c1_ref, bf16[272,128]{1,0:T(8,128)(2,1)S(1)} %collective-permute-done.5.a0_ref, ...), custom_call_target="tpu_custom_call" | custom-call | flops 3221225472 | bytes 6291456 | tf_op jit(solution)/shard_map/spread/pallas_call | solution.py:278
Async XLA Ops:
  0.0 23.1 %copy-start.4 = (f32[6,256]{1,0:T(8,128)S(1)}, f32[6,256]{1,0:T(8,128)}, u32[]{:S(2)}) copy-start(f32[6,256]{1,0:T(8,128)} %rates_ref.5) | copy-start | bytes 18436
  0.8 22.2 %copy-start.2 = (f32[64,128,128]{2,1,0:T(8,128)S(1)}, f32[64,128,128]{2,1,0:T(8,128)}, u32[]{:S(2)}) copy-start(f32[64,128,128]{2,1,0:T(8,128)} %trans_ref.5) | copy-start | bytes 12582916
  3.1 19.9 %collective-permute-start.4 = (bf16[16,256,128]{2,1,0:T(8,128)(2,1)S(1)}, bf16[16,256,128]{2,1,0:T(8,128)(2,1)S(1)}, u32[]{:S(2)}, u32[]{:S(2)}) collective-permute-start(bf16[16,256,128]{2,1,0:T(8,128)(2,1)S(1)} %get-tuple-element.17), channel_id=1, source_target_pairs={{4,8},{12,16},{20,24},{28,32},{36,40},{44,48},{52,56},{60,64},{68,... | collective-permute-start | bytes 3145736 | tf_op jit(solution)/shard_map/ppermute | solution.py:312
  10.6 24.4 %collective-permute-start = (bf16[16,256,128]{2,1,0:T(8,128)(2,1)S(1)}, bf16[16,256,128]{2,1,0:T(8,128)(2,1)S(1)}, u32[]{:S(2)}, u32[]{:S(2)}) collective-permute-start(bf16[16,256,128]{2,1,0:T(8,128)(2,1)S(1)} %get-tuple-element.18), channel_id=1, source_target_pairs={{0,4},{8,12},{16,20},{24,28},{32,36},{40,44},{48,52},{56,60},{64,6... | collective-permute-start | bytes 3145736 | tf_op jit(solution)/shard_map/ppermute | solution.py:313
  23.1 2.8 %copy-start = (bf16[16,6,256,128]{3,2,1,0:T(8,128)(2,1)S(1)}, bf16[16,6,256,128]{3,2,1,0:T(8,128)(2,1)}, u32[]{:S(2)}) copy-start(bf16[16,6,256,128]{3,2,1,0:T(8,128)(2,1)} %prev_ref.3) | copy-start | bytes 18874372
  25.8 1.1 %copy-start.3 = (f32[6,256,128]{2,1,0:T(8,128)S(1)}, f32[6,256,128]{2,1,0:T(8,128)}, u32[]{:S(2)}) copy-start(f32[6,256,128]{2,1,0:T(8,128)} %init_ref.3) | copy-start | bytes 2359300
  27.0 8.0 %copy-start.1 = (bf16[16,6,256,128]{3,2,1,0:T(8,128)(2,1)S(1)}, bf16[16,6,256,128]{3,2,1,0:T(8,128)(2,1)}, u32[]{:S(2)}) copy-start(bf16[16,6,256,128]{3,2,1,0:T(8,128)(2,1)} %prev_ref.3) | copy-start | bytes 18874372
  34.3 22.2 %collective-permute-start.7 = (bf16[272,128]{1,0:T(8,128)(2,1)S(1)}, bf16[272,128]{1,0:T(8,128)(2,1)S(1)}, u32[]{:S(2)}, u32[]{:S(2)}) collective-permute-start(bf16[272,128]{1,0:T(8,128)(2,1)S(1)} %get-tuple-element.12), channel_id=1, source_target_pairs={{0,3},{4,7},{8,11},{12,15},{16,19},{20,23},{24,27},{28,31},{32,35}... | collective-permute-start | bytes 208904 | tf_op jit(solution)/shard_map/ppermute | solution.py:317
  47.1 21.9 %collective-permute-start.3 = (bf16[1296,128]{1,0:T(8,128)(2,1)S(1)}, bf16[1296,128]{1,0:T(8,128)(2,1)S(1)}, u32[]{:S(2)}, u32[]{:S(2)}) collective-permute-start(bf16[1296,128]{1,0:T(8,128)(2,1)S(1)} %get-tuple-element.11), channel_id=1, source_target_pairs={{0,3},{4,7},{8,11},{12,15},{16,19},{20,23},{24,27},{28,31},{32,35}... | collective-permute-start | bytes 995336 | tf_op jit(solution)/shard_map/ppermute | solution.py:317
  47.8 21.2 %collective-permute-start.2 = (bf16[1296,128]{1,0:T(8,128)(2,1)S(1)}, bf16[1296,128]{1,0:T(8,128)(2,1)S(1)}, u32[]{:S(2)}, u32[]{:S(2)}) collective-permute-start(bf16[1296,128]{1,0:T(8,128)(2,1)S(1)} %get-tuple-element.11), channel_id=1, source_target_pairs={{0,2},{1,3},{4,6},{5,7},{8,10},{9,11},{12,14},{13,15},{16,18},{17,... | collective-permute-start | bytes 995336 | tf_op jit(solution)/shard_map/ppermute | solution.py:317
  53.3 15.8 %collective-permute-start.1 = (bf16[1296,128]{1,0:T(8,128)(2,1)S(1)}, bf16[1296,128]{1,0:T(8,128)(2,1)S(1)}, u32[]{:S(2)}, u32[]{:S(2)}) collective-permute-start(bf16[1296,128]{1,0:T(8,128)(2,1)S(1)} %get-tuple-element.11), channel_id=1, source_target_pairs={{0,1},{1,2},{2,3},{4,5},{5,6},{6,7},{8,9},{9,10},{10,11},{12,13},{... | collective-permute-start | bytes 995336 | tf_op jit(solution)/shard_map/ppermute | solution.py:317
  55.2 6.9 %collective-permute-start.6 = (bf16[272,128]{1,0:T(8,128)(2,1)S(1)}, bf16[272,128]{1,0:T(8,128)(2,1)S(1)}, u32[]{:S(2)}, u32[]{:S(2)}) collective-permute-start(bf16[272,128]{1,0:T(8,128)(2,1)S(1)} %get-tuple-element.12), channel_id=1, source_target_pairs={{0,2},{1,3},{4,6},{5,7},{8,10},{9,11},{12,14},{13,15},{16,18},{17,... | collective-permute-start | bytes 208904 | tf_op jit(solution)/shard_map/ppermute | solution.py:317
  56.5 12.5 %collective-permute-start.5 = (bf16[272,128]{1,0:T(8,128)(2,1)S(1)}, bf16[272,128]{1,0:T(8,128)(2,1)S(1)}, u32[]{:S(2)}, u32[]{:S(2)}) collective-permute-start(bf16[272,128]{1,0:T(8,128)(2,1)S(1)} %get-tuple-element.12), channel_id=1, source_target_pairs={{0,1},{1,2},{2,3},{4,5},{5,6},{6,7},{8,9},{9,10},{10,11},{12,13},{... | collective-permute-start | bytes 208904 | tf_op jit(solution)/shard_map/ppermute | solution.py:317

commit v2 on v1

v2 whole, which is shorter than its diff:
```python
import functools

import jax
import jax.numpy as jnp
from jax import lax
from jax.experimental import pallas as pl
from jax.experimental.pallas import tpu as pltpu
from jax.sharding import PartitionSpec as P

F32, BF16 = jnp.float32, jnp.bfloat16
PEAK = 2.0**15.5
CHUNK = 64
MIB = 1 << 20


def split(value):
    high = value.astype(BF16)
    low = (value - high.astype(F32)).astype(BF16)
    return high, low


def left(value):
    return jnp.concatenate(split(value), axis=1)


def right(matrix):
    both = jnp.concatenate(split(matrix), axis=1)
    return jnp.concatenate([both, both], axis=0)


def times(value, matrix):
    n = matrix.shape[1] // 2
    both = jnp.dot(left(value), matrix, preferred_element_type=F32)
    return both[:, :n] + both[:, n:]


def shares(rates_ref, which, bins):
    lines = [rates_ref[pl.ds(row, 1), :] for row in which]
    lines += [jnp.zeros_like(lines[0])] * (8 - len(lines))
    turned = jnp.concatenate(lines, axis=0).T
    return [jnp.broadcast_to(turned[:, i : i + 1], (turned.shape[0], bins)) for i in range(len(which))]


def place(q, rows, odd):
    return q + odd * (rows - 1 - 2 * q)


def encode(value, scale):
    u = value * (PEAK / scale)
    g = u * u
    g = g * g
    g = g * g
    return jnp.where(value < 0, -g, g).astype(BF16)


def decode(code, scale):
    g = code.astype(F32)
    root = jnp.exp(jnp.log(jnp.abs(g)) * 0.125) * (scale * (1.0 / PEAK))
    return jnp.where(g < 0, -root, root)


def stream(steps, count, matrix_of, left_of, store, beside=None):
    lag = max(n for n in range(2, 13, 2) if count % n == 0)

    def push(t):
        matrix = matrix_of(t)
        pltpu.matmul_push_rhs(matrix, 0, 0)
        pltpu.matmul_push_rhs(matrix, 0, 1)

    def run(*accs):
        def emit(t, first, last, slot):
            for i in range(count):
                acc = accs[i % lag]
                if i >= lag:
                    store(t, i - lag, pltpu.matmul_pop(acc))
                elif not first:
                    store(t - 1, count - lag + i, pltpu.matmul_pop(acc))
                pltpu.matmul_acc_lhs(acc, left_of(t, i, slot), load_staged_rhs=0 if i < 2 else None)
                if i == 1 and not last:
                    push(t + 1)
                if beside is not None:
                    beside(t, i, slot)

        push(0)
        emit(0, True, steps == 1, 0)

        def pair(k, carry):
            emit(2 * k + 1, False, False, 1)
            emit(2 * k + 2, False, False, 0)
            return carry

        pairs = max(steps - 2, 0) // 2
        lax.fori_loop(0, pairs, pair, 0)
        for t in range(2 * pairs + 1, steps):
            emit(t, False, t == steps - 1, t % 2)
        for i in range(lag):
            store(steps - 1, count - lag + i, pltpu.matmul_pop(accs[i]))

    pl.run_scoped(run, *[pltpu.ACC(i % 2)((CHUNK, 256), F32) for i in range(lag)])


def halves(both):
    n = both.shape[1] // 2
    return both[:, :n] + both[:, n:]


def finish(loc_ref, code_ref, steps):
    rows, columns, bins = loc_ref.shape[1:]
    top = jnp.zeros((columns, bins), F32)
    for n in range(rows):
        top = jnp.maximum(top, jnp.abs(loc_ref[steps - 1, n]))
    scale = (jnp.max(top, keepdims=True) * 1.01 + 1e-30).astype(BF16).astype(F32)
    for n in range(rows):
        code_ref[n * columns : (n + 1) * columns] = encode(loc_ref[steps - 1, n], scale)
    code_ref[rows * columns :] = jnp.broadcast_to(scale, (16, bins)).astype(BF16)


def edge_kernel(steps, rows, prev_ref, line_ref, outer_ref, inner_ref, buf, rates_ref, sems, rsem):
    odd = lax.rem(lax.axis_index("space"), 2)
    bins = buf.shape[3]
    order = [place(0, rows, odd), place(rows - 1, rows, odd)]
    group = steps // sems.shape[1]

    def fetch(side, k):
        at = pl.ds(k * group, group)
        return pltpu.make_async_copy(
            prev_ref.at[at, order[side]], buf.at[side, at], sems.at[side, k]
        )

    parts = [(side, k) for side in range(2) for k in range(sems.shape[1])]
    lines = pltpu.make_async_copy(line_ref, rates_ref, rsem)
    lines.start()
    for part in parts:
        fetch(*part).start()
    lines.wait()
    weights = [share * 0.25 for share in shares(rates_ref, order, bins)]
    for side, k in parts:
        fetch(side, k).wait()
        out_ref = (outer_ref, inner_ref)[side]
        for t in range(k * group, (k + 1) * group):
            out_ref[t] = (buf[side, t].astype(F32) * weights[side]).astype(BF16)


def edges(previous, rates):
    steps, rows, columns, bins = previous.shape
    vmem = pl.BlockSpec(memory_space=pltpu.VMEM)
    return pl.pallas_call(
        functools.partial(edge_kernel, steps, rows),
        out_shape=[jax.ShapeDtypeStruct((steps, columns, bins), BF16)] * 2,
        in_specs=[pl.BlockSpec(memory_space=pl.ANY)] * 2,
        out_specs=[vmem] * 2,
        scratch_shapes=[
            pltpu.VMEM((2, steps, columns, bins), BF16),
            pltpu.VMEM((rows, columns), F32),
            pltpu.SemaphoreType.DMA((2, 4)),
            pltpu.SemaphoreType.DMA,
        ],
        compiler_params=pltpu.CompilerParams(vmem_limit_bytes=8 * MIB),
        cost_estimate=pl.CostEstimate(flops=0, bytes_accessed=0, transcendentals=0),
        name="edges",
    )(*[pltpu.with_memory_space_constraint(a, pltpu.HBM) for a in (previous, rates)])


def inner_kernel(
    steps, rows,
    prev_ref, halo_ref, init_ref, line_ref, trans_ref,
    loc_ref, code_ref, part_ref, first_ref, keep_ref, rhs_ref,
    pbuf, ibuf, tbuf, even, odds, weight, state, rates_ref, psem, isem, tsem, rsem,
):
    odd = lax.rem(lax.axis_index("space"), 2)
    block = lax.axis_index("tm")
    columns, bins = pbuf.shape[2], pbuf.shape[3]

    def fetch(t):
        return pltpu.make_async_copy(prev_ref.at[t], pbuf.at[t], psem.at[t])

    matrices = pltpu.make_async_copy(trans_ref.at[pl.ds(block * steps, steps)], tbuf, tsem)
    start = pltpu.make_async_copy(init_ref, ibuf, isem)
    lines = pltpu.make_async_copy(line_ref, rates_ref, rsem)
    lines.start()
    matrices.start()
    start.start()
    for t in range(steps):
        fetch(t).start()
    lines.wait()
    for q, share in enumerate(shares(rates_ref, [place(q, rows, odd) for q in range(rows)], bins)):
        weight[q] = share * 0.25
        keep_ref[q] = 1.0 - share
    grids = (even, odds)
    for grid in grids:
        for i in range(rows + 1):
            grid[i, 0:8] = jnp.zeros((8, bins), F32)
            grid[i, columns + 8 :] = jnp.zeros((8, bins), F32)
    matrices.wait()
    for t in range(steps):
        rhs_ref[t] = right(tbuf[t])
    start.wait()
    for q in range(rows):
        value = ibuf[place(q, rows, odd)]
        value = jnp.where(block == 0, value, jnp.zeros_like(value))
        if q == 0:
            first_ref[...] = value
        else:
            state[q - 1] = value

    pieces = [(q, c) for q in range(1, rows) for c in range(0, columns, CHUNK)]

    units = [(q, c) for q in range(rows + 1) for c in range(0, columns, CHUNK)]

    def fill(t, unit, slot):
        q, c = unit
        if q == rows:
            value = halo_ref[t, c : c + CHUNK].astype(F32)
        else:
            value = pbuf[t, place(q, rows, odd), c : c + CHUNK].astype(F32)
            value = (value * weight[q, c : c + CHUNK]).astype(BF16).astype(F32)
        grids[slot][q, 8 + c : 8 + c + CHUNK] = value

    def sides(grid, q, c):
        return grid[q, 7 + c : 7 + c + CHUNK] + grid[q, 9 + c : 9 + c + CHUNK]

    def left_of(t, i, slot):
        q, c = pieces[i]
        grid, inside, cells = grids[slot], slice(8 + c, 8 + c + CHUNK), slice(c, c + CHUNK)
        inflow = (grid[q - 1, inside] + grid[q + 1, inside]) + sides(grid, q, c)
        return left(keep_ref[q, cells] * state[q - 1, cells] + inflow)

    def store(t, i, both):
        q, c = pieces[i]
        value = halves(both)
        state[q - 1, c : c + CHUNK] = value
        loc_ref[t, q - 1, c : c + CHUNK] = value

    def beside(t, i, slot):
        if i % rows == 0 and i // rows < columns // CHUNK:
            c = i // rows * CHUNK
            grid = grids[slot]
            part_ref[t, c : c + CHUNK] = grid[1, 8 + c : 8 + c + CHUNK] + sides(grid, 0, c)
        if isinstance(t, int) and t == steps - 1:
            return
        if i == 0:
            fetch(t + 1).wait()
        for unit in units[len(units) * i // len(pieces) : len(units) * (i + 1) // len(pieces)]:
            fill(t + 1, unit, 1 - slot)

    fetch(0).wait()
    for unit in units:
        fill(0, unit, 0)
    stream(steps, len(pieces), lambda t: rhs_ref[t], left_of, store, beside)
    finish(loc_ref, code_ref, steps)


def inner_rows(previous, halo, initial, rates, transitions):
    steps, rows, columns, bins = previous.shape
    anywhere = pl.BlockSpec(memory_space=pl.ANY)
    vmem = pl.BlockSpec(memory_space=pltpu.VMEM)
    previous, initial, rates, transitions = [
        pltpu.with_memory_space_constraint(a, pltpu.HBM)
        for a in (previous, initial, rates, transitions)
    ]
    return pl.pallas_call(
        functools.partial(inner_kernel, steps, rows),
        out_shape=[
            pltpu.VMEM((steps, rows - 1, columns, bins), F32),
            jax.ShapeDtypeStruct(((rows - 1) * columns + 16, bins), BF16),
            pltpu.VMEM((steps, columns, bins), F32),
            pltpu.VMEM((columns, bins), F32),
            pltpu.VMEM((rows, columns, bins), F32),
            pltpu.VMEM((steps, 2 * bins, 2 * bins), BF16),
        ],
        in_specs=[anywhere, vmem, anywhere, anywhere, anywhere],
        out_specs=[vmem] * 6,
        scratch_shapes=[
            pltpu.VMEM((steps, rows, columns, bins), BF16),
            pltpu.VMEM((rows, columns, bins), F32),
            pltpu.VMEM((steps, bins, bins), F32),
            pltpu.VMEM((rows + 1, columns + 16, bins), F32),
            pltpu.VMEM((rows + 1, columns + 16, bins), F32),
            pltpu.VMEM((rows, columns, bins), F32),
            pltpu.VMEM((rows - 1, columns, bins), F32),
            pltpu.VMEM((rows, columns), F32),
            pltpu.SemaphoreType.DMA((steps,)),
            pltpu.SemaphoreType.DMA,
            pltpu.SemaphoreType.DMA,
            pltpu.SemaphoreType.DMA,
        ],
        compiler_params=pltpu.CompilerParams(vmem_limit_bytes=16 * MIB),
        cost_estimate=pl.CostEstimate(
            flops=8 * steps * rows * columns * bins * bins,
            bytes_accessed=steps * rows * columns * bins * 2,
            transcendentals=0,
        ),
        name="inner_rows",
    )(previous, halo, initial, rates, transitions)


def outer_kernel(
    steps, halo_ref, part_ref, first_ref, keep_ref, rhs_ref, most_ref, loc_ref, code_ref, all_ref, state, sem
):
    columns = first_ref.shape[0]
    joined = most_ref.shape[0]
    copy = pltpu.make_async_copy(most_ref, all_ref.at[pl.ds(0, joined)], sem)
    copy.start()
    state[...] = first_ref[...]

    def left_of(t, i, _):
        cells = slice(i * CHUNK, (i + 1) * CHUNK)
        inflow = part_ref[t, cells] + halo_ref[t, cells].astype(F32)
        return left(keep_ref[0, cells] * state[cells] + inflow)

    def store(t, i, both):
        cells = slice(i * CHUNK, (i + 1) * CHUNK)
        state[cells] = loc_ref[t, 0, cells] = halves(both)

    stream(steps, columns // CHUNK, lambda t: rhs_ref[t], left_of, store)
    finish(loc_ref, code_ref, steps)
    all_ref[joined:] = code_ref[...]
    copy.wait()


def outer_row(halo, part, first, keep, rhs, most):
    steps, columns, bins = part.shape
    vmem = pl.BlockSpec(memory_space=pltpu.VMEM)
    return pl.pallas_call(
        functools.partial(outer_kernel, steps),
        out_shape=[
            pltpu.VMEM((steps, 1, columns, bins), F32),
            jax.ShapeDtypeStruct((columns + 16, bins), BF16),
            jax.ShapeDtypeStruct((most.shape[0] + columns + 16, bins), BF16),
        ],
        in_specs=[vmem] * 6,
        out_specs=[vmem] * 3,
        scratch_shapes=[pltpu.VMEM((columns, bins), F32), pltpu.SemaphoreType.DMA],
        compiler_params=pltpu.CompilerParams(vmem_limit_bytes=4 * MIB),
        cost_estimate=pl.CostEstimate(
            flops=0, bytes_accessed=0, transcendentals=0
        ),
        name="outer_row",
    )(halo, part, first, keep, rhs, most)


def product_kernel(steps, trans_ref, prefix_ref, total_ref, tbuf, work, sems):
    block = lax.axis_index("tm")
    bins = tbuf.shape[2]
    copies = []
    for back in range(3):
        at = pl.ds(jnp.maximum(block - back, 0) * steps, steps)
        copies.append(
            pltpu.make_async_copy(
                trans_ref.at[at], tbuf.at[pl.ds(back * steps, steps)], sems.at[back]
            )
        )
        copies[-1].start()
    for copy in copies:
        copy.wait()
    for back in range(3):
        work[back] = tbuf[back * steps]
    prefix_ref[0] = right(tbuf[0])

    def step(t, carry):
        for back in range(3):
            work[back] = times(work[back], right(tbuf[back * steps + t]))
        prefix_ref[t] = right(work[0])
        return carry

    lax.fori_loop(1, steps, step, 0)
    total_ref[0] = right(work[1])
    total_ref[1] = right(work[2])


def products(transitions, steps):
    bins = transitions.shape[1]
    transitions = pltpu.with_memory_space_constraint(transitions, pltpu.HBM)
    vmem = pl.BlockSpec(memory_space=pltpu.VMEM)
    return pl.pallas_call(
        functools.partial(product_kernel, steps),
        out_shape=[
            pltpu.VMEM((steps, 2 * bins, 2 * bins), BF16),
            pltpu.VMEM((2, 2 * bins, 2 * bins), BF16),
        ],
        in_specs=[pl.BlockSpec(memory_space=pl.ANY)],
        out_specs=[vmem, vmem],
        scratch_shapes=[
            pltpu.VMEM((3 * steps, bins, bins), F32),
            pltpu.VMEM((3, bins, bins), F32),
            pltpu.SemaphoreType.DMA((3,)),
        ],
        compiler_params=pltpu.CompilerParams(vmem_limit_bytes=16 * MIB),
        cost_estimate=pl.CostEstimate(
            flops=0, bytes_accessed=0, transcendentals=0
        ),
        name="products",
    )(transitions)


def scale_of(ref, last):
    return ref[last : last + 16].astype(F32)[0:1, 0:1]


def decay(held):
    for _ in range(4):
        held = held * held
    return held


def ready_kernel(
    chunks, near1_ref, near0_ref, far1_ref, far0_ref, keep_ref, total_ref, near_ref, far_ref
):
    columns = keep_ref.shape[1]
    pieces = [(k, n, q, c) for k, calc in enumerate(chunks) for n, q in enumerate(calc) for c in range(0, columns, CHUNK)]
    refs = ((near1_ref, far1_ref), (near0_ref, far0_ref))
    scales = [[scale_of(ref, len(calc) * columns) for ref in pair] for calc, pair in zip(chunks, refs)]

    def carried(i, which):
        k, n, _, c = pieces[i]
        at = n * columns + c
        return decode(refs[k][which][at : at + CHUNK], scales[k][which])

    def store(_, i, both):
        _, _, q, c = pieces[i]
        cells = slice(c, c + CHUNK)
        near_ref[q, cells] = carried(i, 0)
        far_ref[q, cells] = decay(keep_ref[q, cells]) * halves(both)

    stream(1, len(pieces), lambda _: total_ref[1], lambda _, i, s: left(carried(i, 1)), store)


def ready(chunks, codes, keep, total):
    vmem = pl.BlockSpec(memory_space=pltpu.VMEM)
    return pl.pallas_call(
        functools.partial(ready_kernel, chunks),
        out_shape=[pltpu.VMEM(keep.shape, F32)] * 2,
        in_specs=[vmem] * 6,
        out_specs=[vmem] * 2,
        compiler_params=pltpu.CompilerParams(vmem_limit_bytes=4 * MIB),
        cost_estimate=pl.CostEstimate(flops=4000000000, bytes_accessed=8000000, transcendentals=0),
        name="ready",
    )(*codes, keep, total)


def spread_kernel(
    chunks, rows,
    near_ref, far_ref, mid_ref, loc1_ref, loc0_ref, keep_ref, prefix_ref, total_ref,
    out_ref,
    entering, power, stage, sems,
):
    odd = lax.rem(lax.axis_index("space"), 2)
    steps, _, columns, bins = stage.shape
    locs = (loc1_ref, loc0_ref)
    pieces, at, scales = [], 0, []
    for k, calc in enumerate(chunks):
        for n, q in enumerate(calc):
            pieces += [(k, n, q, c, at + c) for c in range(0, columns, CHUNK)]
            at += columns
        scales.append(scale_of(mid_ref, at))
        at += 16
    count = len(pieces)

    def cells_of(i):
        return pieces[i][2], slice(pieces[i][3], pieces[i][3] + CHUNK)

    def left_mid(_, i, slot):
        k, n, q, c, at = pieces[i]
        return left(decode(mid_ref[at : at + CHUNK], scales[k]) + far_ref[cells_of(i)])

    def store_mid(_, i, both):
        state = near_ref[cells_of(i)] + decay(keep_ref[cells_of(i)]) * halves(both)
        entering[cells_of(i)] = left(state)
        power[cells_of(i)] = jnp.ones((CHUNK, bins), F32)

    stream(1, count, lambda _: total_ref[0], left_mid, store_mid)

    def store(t, i, both):
        k, n, q, c, _ = pieces[i]
        factor = power[cells_of(i)] * keep_ref[cells_of(i)]
        power[cells_of(i)] = factor
        value = locs[k][t, n, c : c + CHUNK] + factor * halves(both)
        stage[t, place(q, rows, odd), c : c + CHUNK] = value.astype(BF16)
        if i == count - 1:
            pltpu.make_async_copy(stage.at[t], out_ref.at[t], sems.at[t]).start()

    stream(steps, count, lambda t: prefix_ref[t], lambda t, i, slot: entering[cells_of(i)], store)
    for t in range(steps):
        pltpu.make_async_copy(stage.at[t], out_ref.at[t], sems.at[t]).wait()


def spread(chunks, near, far, mid, loc1, loc0, keep, prefix, total):
    steps, _, columns, bins = loc1.shape
    rows = keep.shape[0]
    vmem = pl.BlockSpec(memory_space=pltpu.VMEM)
    return pl.pallas_call(
        functools.partial(spread_kernel, chunks, rows),
        out_shape=jax.ShapeDtypeStruct((steps, rows, columns, bins), BF16),
        in_specs=[vmem] * 8,
        out_specs=pl.BlockSpec(memory_space=pl.ANY),
        scratch_shapes=[
            pltpu.VMEM((rows, columns, 2 * bins), BF16),
            pltpu.VMEM((rows, columns, bins), F32),
            pltpu.VMEM((steps, rows, columns, bins), BF16),
            pltpu.SemaphoreType.DMA((steps,)),
        ],
        compiler_params=pltpu.CompilerParams(vmem_limit_bytes=16 * MIB),
        cost_estimate=pl.CostEstimate(
            flops=8 * steps * rows * columns * bins * bins,
            bytes_accessed=steps * rows * columns * bins * 2,
            transcendentals=0,
        ),
        name="spread",
    )(near, far, mid, loc1, loc0, keep, prefix, total)


def local(previous, initial, rates, transitions):
    steps, rows, columns, bins = previous.shape
    strips, blocks = lax.axis_size("space"), lax.axis_size("tm")
    outer_edge, inner_edge = edges(previous, rates)
    between = [(i, i + 1) for i in range(1, strips - 1, 2)]
    within = [(i, i + 1) for i in range(0, strips, 2)]
    outer = lax.ppermute(outer_edge, "space", between + [(j, i) for i, j in between])
    inner = lax.ppermute(inner_edge, "space", within + [(j, i) for i, j in within])

    def send(code, hop):
        return lax.ppermute(code, "tm", [(i, i + hop) for i in range(blocks - hop)])

    most, rest = tuple(range(1, rows)), (0,)
    loc1, code1, part, first, keep, rhs = inner_rows(previous, inner, initial, rates, transitions)
    near1, far1 = send(code1, 1), send(code1, 3)
    loc0, code0, code = outer_row(outer, part, first, keep, rhs, code1)
    mid, near0, far0 = send(code, 2), send(code0, 1), send(code0, 3)
    prefix, total = products(transitions, steps)
    chunks = (most, rest)
    near, far = ready(chunks, [near1, near0, far1, far0], keep, total)
    return spread(chunks, near, far, mid, loc1, loc0, keep, prefix, total)


def solution(mesh):
    in_specs = (P("tm", "space", None, None), P("space", None, None), P("space", None), P())
    out_specs = P("tm", "space", None, None)
    return jax.shard_map(local, mesh=mesh, in_specs=in_specs, out_specs=out_specs, check_vma=False)
```

time: 78.4 us -> 48.4 us (0.62)
  the two profiles are of different devices: /device:TPU:14 before, /device:TPU:22 now
where the time goes in v2:
time: 48.4 us; the launch traced here: 48.1 us
  Pallas kernels  26.9 us (56%)
  starting transfers between devices  16.5 us (34%)
  waiting for transfers between devices  4.6 us (10%)
    pallas_call x1, Pallas kernels, inner_rows(): pl.pallas_call(functools.partial(inner_kernel, steps, rows), out_shape=[p...  10.1 us
    ppermute x5, starting transfers between devices, send(): return lax.ppermute(code, 'tm', [(i, i + hop) for i in range(blocks - hop)])  8.29 us
    ppermute x1, starting transfers between devices, local(): lax.ppermute(outer_edge, 'space', between + [(j, i) for i, j in between])  8.12 us
    pallas_call x1, Pallas kernels, spread(): pl.pallas_call(functools.partial(spread_kernel, chunks, rows), out_shape=...  5.93 us
    pallas_call x1, Pallas kernels, products(): pl.pallas_call(functools.partial(product_kernel, steps), out_shape=[pltpu...  5.28 us
    ppermute x5, waiting for transfers between devices, send(): return lax.ppermute(code, 'tm', [(i, i + hop) for i in range(blocks - hop)])  4.6 us
    pallas_call x1, Pallas kernels, outer_row(): pl.pallas_call(functools.partial(outer_kernel, steps), out_shape=[pltpu.V...  2.47 us
    pallas_call x1, Pallas kernels, edges(): pl.pallas_call(functools.partial(edge_kernel, steps, rows), out_shape=[ja...  2.13 us
  transfers between devices with their start and end apart: 7, of which 1 were waited for; matrix products, arithmetic and copies ran while one was open for 0% of the time, Pallas kernels for 39%

profile of v2, /device:TPU:22, one launch (start us, length us, event | category | flops | bytes accessed | tf_op | source)
XLA Modules:
  0.0 48.1 jit_solution(17069009369365470775)
XLA Ops:
  0.0 2.1 %edges.1 = (bf16[16,256,128]{2,1,0:T(8,128)(2,1)S(1)}, bf16[16,256,128]{2,1,0:T(8,128)(2,1)S(1)}) custom-call(bf16[16,6,256,128]{3,2,1,0:T(8,128)(2,1)} %prev_ref.3, f32[6,256]{1,0:T(8,128)} %line_ref.3), custom_call_target="tpu_custom_call" | custom-call | tf_op jit(solution)/shard_map/edges/pallas_call | solution.py:147
  2.1 0.1 collective-permute-start
  2.2 8.1 %collective-permute-start.2 = (bf16[16,256,128]{2,1,0:T(8,128)(2,1)S(1)}, bf16[16,256,128]{2,1,0:T(8,128)(2,1)S(1)}, u32[]{:S(2)}, u32[]{:S(2)}) collective-permute-start(bf16[16,256,128]{2,1,0:T(8,128)(2,1)S(1)} %get-tuple-element.22), channel_id=1, source_target_pairs={{4,8},{12,16},{20,24},{28,32},{36,40},{44,48},{52,56},{60,64},{68,... | collective-permute-start | bytes 3145736 | tf_op jit(solution)/shard_map/ppermute | solution.py:518
  10.4 0.0 collective-permute-done.halo_ref
  10.4 10.1 %inner_rows.1 = (f32[16,5,256,128]{3,2,1,0:T(8,128)S(1)}, bf16[1296,128]{1,0:T(8,128)(2,1)S(1)}, f32[16,256,128]{2,1,0:T(8,128)S(1)}, f32[256,128]{1,0:T(8,128)S...) custom-call(bf16[16,6,256,128]{3,2,1,0:T(8,128)(2,1)} %prev_ref.3, ...), custom_call_target="tpu_custom_call" | custom-call | flops 3221225472 | bytes 6291456 | tf_op jit(solution)/shard_map/inner_rows/pallas_call | solution.py:261
  20.5 0.7 %collective-permute-start.4 = (bf16[1296,128]{1,0:T(8,128)(2,1)S(1)}, bf16[1296,128]{1,0:T(8,128)(2,1)S(1)}, u32[]{:S(2)}, u32[]{:S(2)}) collective-permute-start(bf16[1296,128]{1,0:T(8,128)(2,1)S(1)} %get-tuple-element.21.most_ref), channel_id=1, source_target_pairs={{0,3},{4,7},{8,11},{12,15},{16,19},{20,23},{24,27},{28,31},{32,35}... | collective-permute-start | bytes 995336 | tf_op jit(solution)/shard_map/ppermute | solution.py:522
  21.2 3.7 %collective-permute-start.1 = (bf16[1296,128]{1,0:T(8,128)(2,1)S(1)}, bf16[1296,128]{1,0:T(8,128)(2,1)S(1)}, u32[]{:S(2)}, u32[]{:S(2)}) collective-permute-start(bf16[1296,128]{1,0:T(8,128)(2,1)S(1)} %get-tuple-element.21.most_ref), channel_id=1, source_target_pairs={{0,1},{1,2},{2,3},{4,5},{5,6},{6,7},{8,9},{9,10},{10,11},{12,13},{... | collective-permute-start | bytes 995336 | tf_op jit(solution)/shard_map/ppermute | solution.py:522
  24.9 0.0 collective-permute-done.2.halo_ref
  25.0 2.5 %outer_row.1 = (f32[16,1,256,128]{3,2,1,0:T(8,128)S(1)}, bf16[272,128]{1,0:T(8,128)(2,1)S(1)}, bf16[1568,128]{1,0:T(8,128)(2,1)S(1)}) custom-call(bf16[16,256,128]{2,1,0:T(8,128)(2,1)S(1)} %collective-permute-done.2.halo_ref, f32[16,256,128]{2,1,0:T(8,128)S(1)} %get-tuple-element.23.part_ref, f32[256,128]{1,0:T(8,128)S(1)} %get-tuple-element.24.first_ref, ...), custom_call_target="tpu_custom_call" | custom-call | tf_op jit(solution)/shard_map/outer_row/pallas_call | solution.py:324
  27.4 0.7 %collective-permute-start.5 = (bf16[272,128]{1,0:T(8,128)(2,1)S(1)}, bf16[272,128]{1,0:T(8,128)(2,1)S(1)}, u32[]{:S(2)}, u32[]{:S(2)}) collective-permute-start(bf16[272,128]{1,0:T(8,128)(2,1)S(1)} %get-tuple-element.27), channel_id=1, source_target_pairs={{0,3},{4,7},{8,11},{12,15},{16,19},{20,23},{24,27},{28,31},{32,35}... | collective-permute-start | bytes 208904 | tf_op jit(solution)/shard_map/ppermute | solution.py:522
  28.1 1.9 %collective-permute-start.3 = (bf16[272,128]{1,0:T(8,128)(2,1)S(1)}, bf16[272,128]{1,0:T(8,128)(2,1)S(1)}, u32[]{:S(2)}, u32[]{:S(2)}) collective-permute-start(bf16[272,128]{1,0:T(8,128)(2,1)S(1)} %get-tuple-element.27), channel_id=1, source_target_pairs={{0,1},{1,2},{2,3},{4,5},{5,6},{6,7},{8,9},{9,10},{10,11},{12,13},{... | collective-permute-start | bytes 208904 | tf_op jit(solution)/shard_map/ppermute | solution.py:522
  30.0 1.3 %collective-permute-start.6 = (bf16[1568,128]{1,0:T(8,128)(2,1)S(1)}, bf16[1568,128]{1,0:T(8,128)(2,1)S(1)}, u32[]{:S(2)}, u32[]{:S(2)}) collective-permute-start(bf16[1568,128]{1,0:T(8,128)(2,1)S(1)} %get-tuple-element.31), channel_id=1, source_target_pairs={{0,2},{1,3},{4,6},{5,7},{8,10},{9,11},{12,14},{13,15},{16,18},{17,... | collective-permute-start | bytes 1204232 | tf_op jit(solution)/shard_map/ppermute | solution.py:522
  31.3 5.3 %products.1 = (bf16[16,256,256]{2,1,0:T(8,128)(2,1)S(1)}, bf16[2,256,256]{2,1,0:T(8,128)(2,1)S(1)}) custom-call(f32[64,128,128]{2,1,0:T(8,128)} %trans_ref.3), custom_call_target="tpu_custom_call" | custom-call | tf_op jit(solution)/shard_map/products/pallas_call | solution.py:375
  36.6 0.0 collective-permute-done.5.far0_ref
  36.6 0.0 collective-permute-done.3.near0_ref
  36.6 0.0 collective-permute-done.4.far1_ref
  36.7 0.0 collective-permute-done.1.near1_ref
  36.7 0.9 %ready.1 = (f32[6,256,128]{2,1,0:T(8,128)S(1)}, f32[6,256,128]{2,1,0:T(8,128)S(1)}) custom-call(bf16[1296,128]{1,0:T(8,128)(2,1)S(1)} %collective-permute-done.1.near1_ref, bf16[272,128]{1,0:T(8,128)(2,1)S(1)} %collective-permute-done.3.near0_ref, bf16[1296,128]{1,0:T(8,128)(2,1)S(1)} %collective-permute-done.4.far1_ref, ...), custom_call_target="tpu_custom_call" | custom-call | flops 4000000000 | bytes 8000000 | tf_op jit(solution)/shard_map/ready/pallas_call | solution.py:430
  37.6 4.6 %collective-permute-done.6.mid_ref = bf16[1568,128]{1,0:T(8,128)(2,1)S(1)} collective-permute-done((bf16[1568,128]{1,0:T(8,128)(2,1)S(1)}, bf16[1568,128]{1,0:T(8,128)(2,1)S(1)}, u32[]{:S(2)}, u32[]{:S(2)}) %collective-permute-start.6) | collective-permute-done | bytes 401440 | tf_op jit(solution)/shard_map/ppermute | solution.py:522
  42.2 5.9 %spread.1 = bf16[16,6,256,128]{3,2,1,0:T(8,128)(2,1)} custom-call(f32[6,256,128]{2,1,0:T(8,128)S(1)} %get-tuple-element.29.near_ref, f32[6,256,128]{2,1,0:T(8,128)S(1)} %get-tuple-element.30.far_ref, bf16[1568,128]{1,0:T(8,128)(2,1)S(1)} %collective-permute-done.6.mid_ref, f32[16,5,256,128]{3,2,1,0:T(8,128)S(1)} %get-tuple-element.32.loc1_ref, ...), custom_call_target="tpu_custom_call" | custom-call | flops 3221225472 | bytes 6291456 | tf_op jit(solution)/shard_map/spread/pallas_call | solution.py:491
Async XLA Ops:
  2.1 8.2 %collective-permute-start = (bf16[16,256,128]{2,1,0:T(8,128)(2,1)S(1)}, bf16[16,256,128]{2,1,0:T(8,128)(2,1)S(1)}, u32[]{:S(2)}, u32[]{:S(2)}) collective-permute-start(bf16[16,256,128]{2,1,0:T(8,128)(2,1)S(1)} %get-tuple-element.20), channel_id=1, source_target_pairs={{0,4},{8,12},{16,20},{24,28},{32,36},{40,44},{48,52},{56,60},{64,6... | collective-permute-start | bytes 3145736 | tf_op jit(solution)/shard_map/ppermute | solution.py:519
  2.2 22.7 %collective-permute-start.2 = (bf16[16,256,128]{2,1,0:T(8,128)(2,1)S(1)}, bf16[16,256,128]{2,1,0:T(8,128)(2,1)S(1)}, u32[]{:S(2)}, u32[]{:S(2)}) collective-permute-start(bf16[16,256,128]{2,1,0:T(8,128)(2,1)S(1)} %get-tuple-element.22), channel_id=1, source_target_pairs={{4,8},{12,16},{20,24},{28,32},{36,40},{44,48},{52,56},{60,64},{68,... | collective-permute-start | bytes 3145736 | tf_op jit(solution)/shard_map/ppermute | solution.py:518
  20.5 16.1 %collective-permute-start.4 = (bf16[1296,128]{1,0:T(8,128)(2,1)S(1)}, bf16[1296,128]{1,0:T(8,128)(2,1)S(1)}, u32[]{:S(2)}, u32[]{:S(2)}) collective-permute-start(bf16[1296,128]{1,0:T(8,128)(2,1)S(1)} %get-tuple-element.21.most_ref), channel_id=1, source_target_pairs={{0,3},{4,7},{8,11},{12,15},{16,19},{20,23},{24,27},{28,31},{32,35}... | collective-permute-start | bytes 995336 | tf_op jit(solution)/shard_map/ppermute | solution.py:522
  21.2 15.4 %collective-permute-start.1 = (bf16[1296,128]{1,0:T(8,128)(2,1)S(1)}, bf16[1296,128]{1,0:T(8,128)(2,1)S(1)}, u32[]{:S(2)}, u32[]{:S(2)}) collective-permute-start(bf16[1296,128]{1,0:T(8,128)(2,1)S(1)} %get-tuple-element.21.most_ref), channel_id=1, source_target_pairs={{0,1},{1,2},{2,3},{4,5},{5,6},{6,7},{8,9},{9,10},{10,11},{12,13},{... | collective-permute-start | bytes 995336 | tf_op jit(solution)/shard_map/ppermute | solution.py:522
  27.4 9.2 %collective-permute-start.5 = (bf16[272,128]{1,0:T(8,128)(2,1)S(1)}, bf16[272,128]{1,0:T(8,128)(2,1)S(1)}, u32[]{:S(2)}, u32[]{:S(2)}) collective-permute-start(bf16[272,128]{1,0:T(8,128)(2,1)S(1)} %get-tuple-element.27), channel_id=1, source_target_pairs={{0,3},{4,7},{8,11},{12,15},{16,19},{20,23},{24,27},{28,31},{32,35}... | collective-permute-start | bytes 208904 | tf_op jit(solution)/shard_map/ppermute | solution.py:522
  28.1 8.5 %collective-permute-start.3 = (bf16[272,128]{1,0:T(8,128)(2,1)S(1)}, bf16[272,128]{1,0:T(8,128)(2,1)S(1)}, u32[]{:S(2)}, u32[]{:S(2)}) collective-permute-start(bf16[272,128]{1,0:T(8,128)(2,1)S(1)} %get-tuple-element.27), channel_id=1, source_target_pairs={{0,1},{1,2},{2,3},{4,5},{5,6},{6,7},{8,9},{9,10},{10,11},{12,13},{... | collective-permute-start | bytes 208904 | tf_op jit(solution)/shard_map/ppermute | solution.py:522
  30.0 12.2 %collective-permute-start.6 = (bf16[1568,128]{1,0:T(8,128)(2,1)S(1)}, bf16[1568,128]{1,0:T(8,128)(2,1)S(1)}, u32[]{:S(2)}, u32[]{:S(2)}) collective-permute-start(bf16[1568,128]{1,0:T(8,128)(2,1)S(1)} %get-tuple-element.31), channel_id=1, source_target_pairs={{0,2},{1,3},{4,6},{5,7},{8,10},{9,11},{12,14},{13,15},{16,18},{17,... | collective-permute-start | bytes 1204232 | tf_op jit(solution)/shard_map/ppermute | solution.py:522

commit v3 on v2

--- a/solution.py
+++ b/solution.py
@@ -76,7 +76,7 @@
                 elif not first:
                     store(t - 1, count - lag + i, pltpu.matmul_pop(acc))
                 pltpu.matmul_acc_lhs(acc, left_of(t, i, slot), load_staged_rhs=0 if i < 2 else None)
-                if i == 1 and not last:
+                if i == count // 2 and not last:
                     push(t + 1)
                 if beside is not None:
                     beside(t, i, slot)
@@ -174,14 +174,15 @@
     def fetch(t):
         return pltpu.make_async_copy(prev_ref.at[t], pbuf.at[t], psem.at[t])
 
-    matrices = pltpu.make_async_copy(trans_ref.at[pl.ds(block * steps, steps)], tbuf, tsem)
+    def matrix(t):
+        return pltpu.make_async_copy(trans_ref.at[block * steps + t], tbuf.at[t], tsem.at[t])
+
     start = pltpu.make_async_copy(init_ref, ibuf, isem)
     lines = pltpu.make_async_copy(line_ref, rates_ref, rsem)
     lines.start()
-    matrices.start()
+    matrix(0).start()
+    fetch(0).start()
     start.start()
-    for t in range(steps):
-        fetch(t).start()
     lines.wait()
     for q, share in enumerate(shares(rates_ref, [place(q, rows, odd) for q in range(rows)], bins)):
         weight[q] = share * 0.25
@@ -191,9 +192,11 @@
         for i in range(rows + 1):
             grid[i, 0:8] = jnp.zeros((8, bins), F32)
             grid[i, columns + 8 :] = jnp.zeros((8, bins), F32)
-    matrices.wait()
-    for t in range(steps):
-        rhs_ref[t] = right(tbuf[t])
+    for t in range(1, steps):
+        matrix(t).start()
+        fetch(t).start()
+    matrix(0).wait()
+    rhs_ref[0] = right(tbuf[0])
     start.wait()
     for q in range(rows):
         value = ibuf[place(q, rows, odd)]
@@ -240,6 +243,9 @@
             return
         if i == 0:
             fetch(t + 1).wait()
+        if i == 2:
+            matrix(t + 1).wait()
+            rhs_ref[t + 1] = right(tbuf[t + 1])
         for unit in units[len(units) * i // len(pieces) : len(units) * (i + 1) // len(pieces)]:
             fill(t + 1, unit, 1 - slot)
 
@@ -281,7 +287,7 @@
             pltpu.VMEM((rows, columns), F32),
             pltpu.SemaphoreType.DMA((steps,)),
             pltpu.SemaphoreType.DMA,
-            pltpu.SemaphoreType.DMA,
+            pltpu.SemaphoreType.DMA((steps,)),
             pltpu.SemaphoreType.DMA,
         ],
         compiler_params=pltpu.CompilerParams(vmem_limit_bytes=16 * MIB),
@@ -339,33 +345,32 @@
     )(halo, part, first, keep, rhs, most)
 
 
-def product_kernel(steps, trans_ref, prefix_ref, total_ref, tbuf, work, sems):
+def product_kernel(steps, trans_ref, prefix_ref, total_ref, work, sems):
     block = lax.axis_index("tm")
-    bins = tbuf.shape[2]
     copies = []
     for back in range(3):
         at = pl.ds(jnp.maximum(block - back, 0) * steps, steps)
         copies.append(
             pltpu.make_async_copy(
-                trans_ref.at[at], tbuf.at[pl.ds(back * steps, steps)], sems.at[back]
+                trans_ref.at[at], work.at[pl.ds(back * steps, steps)], sems.at[back]
             )
         )
         copies[-1].start()
     for copy in copies:
         copy.wait()
-    for back in range(3):
-        work[back] = tbuf[back * steps]
-    prefix_ref[0] = right(tbuf[0])
-
-    def step(t, carry):
-        for back in range(3):
-            work[back] = times(work[back], right(tbuf[back * steps + t]))
-        prefix_ref[t] = right(work[0])
-        return carry
-
-    lax.fori_loop(1, steps, step, 0)
-    total_ref[0] = right(work[1])
-    total_ref[1] = right(work[2])
+    span = 1
+    while span < steps:
+        pairs = [(i // span * span - 1, i) for i in range(steps) if i & span]
+        for back in (1, 2):
+            pairs += [(k, k + span) for k in range(back * steps, (back + 1) * steps, 2 * span)]
+        for first, second in pairs:
+            product = times(work[first], right(work[second]))
+            work[second if second < steps else first] = product
+        span *= 2
+    for t in range(steps):
+        prefix_ref[t] = right(work[t])
+    total_ref[0] = right(work[steps])
+    total_ref[1] = right(work[2 * steps])
 
 
 def products(transitions, steps):
@@ -382,7 +387,6 @@
         out_specs=[vmem, vmem],
         scratch_shapes=[
             pltpu.VMEM((3 * steps, bins, bins), F32),
-            pltpu.VMEM((3, bins, bins), F32),
             pltpu.SemaphoreType.DMA((3,)),
         ],
         compiler_params=pltpu.CompilerParams(vmem_limit_bytes=16 * MIB),
@@ -403,46 +407,47 @@
     return held
 
 
-def ready_kernel(
-    chunks, near1_ref, near0_ref, far1_ref, far0_ref, keep_ref, total_ref, near_ref, far_ref
-):
+def ready_kernel(calc, near_code, far_code, keep_ref, total_ref, near_ref, far_ref):
     columns = keep_ref.shape[1]
-    pieces = [(k, n, q, c) for k, calc in enumerate(chunks) for n, q in enumerate(calc) for c in range(0, columns, CHUNK)]
-    refs = ((near1_ref, far1_ref), (near0_ref, far0_ref))
-    scales = [[scale_of(ref, len(calc) * columns) for ref in pair] for calc, pair in zip(chunks, refs)]
-
-    def carried(i, which):
-        k, n, _, c = pieces[i]
+    pieces = [(n, q, c) for n, q in enumerate(calc) for c in range(0, columns, CHUNK)]
+    last = len(calc) * columns
+    near_scale, far_scale = scale_of(near_code, last), scale_of(far_code, last)
+
+    def left_far(_, i, slot):
+        n, _, c = pieces[i]
+        return left(decode(far_code[n * columns + c : n * columns + c + CHUNK], far_scale))
+
+    def store(_, i, both):
+        n, q, c = pieces[i]
+        cells = slice(c, c + CHUNK)
         at = n * columns + c
-        return decode(refs[k][which][at : at + CHUNK], scales[k][which])
-
-    def store(_, i, both):
-        _, _, q, c = pieces[i]
-        cells = slice(c, c + CHUNK)
-        near_ref[q, cells] = carried(i, 0)
-        far_ref[q, cells] = decay(keep_ref[q, cells]) * halves(both)
-
-    stream(1, len(pieces), lambda _: total_ref[1], lambda _, i, s: left(carried(i, 1)), store)
-
-
-def ready(chunks, codes, keep, total):
+        near_ref[n, cells] = decode(near_code[at : at + CHUNK], near_scale)
+        far_ref[n, cells] = decay(keep_ref[q, cells]) * halves(both)
+
+    stream(1, len(pieces), lambda _: total_ref[1], left_far, store)
+
+
+def ready(calc, near, far, keep, total):
+    _, columns, bins = keep.shape
     vmem = pl.BlockSpec(memory_space=pltpu.VMEM)
     return pl.pallas_call(
-        functools.partial(ready_kernel, chunks),
-        out_shape=[pltpu.VMEM(keep.shape, F32)] * 2,
-        in_specs=[vmem] * 6,
+        functools.partial(ready_kernel, calc),
+        out_shape=[pltpu.VMEM((len(calc), columns, bins), F32)] * 2,
+        in_specs=[vmem] * 4,
         out_specs=[vmem] * 2,
         compiler_params=pltpu.CompilerParams(vmem_limit_bytes=4 * MIB),
-        cost_estimate=pl.CostEstimate(flops=4000000000, bytes_accessed=8000000, transcendentals=0),
+        cost_estimate=pl.CostEstimate(
+            flops=4_000_000_000, bytes_accessed=8_000_000, transcendentals=0
+        ),
         name="ready",
-    )(*codes, keep, total)
+    )(near, far, keep, total)
 
 
 def spread_kernel(
     chunks, rows,
-    near_ref, far_ref, mid_ref, loc1_ref, loc0_ref, keep_ref, prefix_ref, total_ref,
+    near1_ref, far1_ref, near0_code, far0_code, mid_ref, loc1_ref, loc0_ref, keep_ref, prefix_ref, total_ref,
     out_ref,
-    entering, power, stage, sems,
+    entering, power, near0_ref, far0_ref, stage, sems,
 ):
     odd = lax.rem(lax.axis_index("space"), 2)
     steps, _, columns, bins = stage.shape
@@ -455,16 +460,19 @@
         scales.append(scale_of(mid_ref, at))
         at += 16
     count = len(pieces)
+    nears, fars = (near1_ref, near0_ref), (far1_ref, far0_ref)
+    ready_kernel(chunks[1], near0_code, far0_code, keep_ref, total_ref, near0_ref, far0_ref)
 
     def cells_of(i):
         return pieces[i][2], slice(pieces[i][3], pieces[i][3] + CHUNK)
 
     def left_mid(_, i, slot):
         k, n, q, c, at = pieces[i]
-        return left(decode(mid_ref[at : at + CHUNK], scales[k]) + far_ref[cells_of(i)])
+        return left(decode(mid_ref[at : at + CHUNK], scales[k]) + fars[k][n, c : c + CHUNK])
 
     def store_mid(_, i, both):
-        state = near_ref[cells_of(i)] + decay(keep_ref[cells_of(i)]) * halves(both)
+        k, n, _, c, _ = pieces[i]
+        state = nears[k][n, c : c + CHUNK] + decay(keep_ref[cells_of(i)]) * halves(both)
         entering[cells_of(i)] = left(state)
         power[cells_of(i)] = jnp.ones((CHUNK, bins), F32)
 
@@ -484,18 +492,20 @@
         pltpu.make_async_copy(stage.at[t], out_ref.at[t], sems.at[t]).wait()
 
 
-def spread(chunks, near, far, mid, loc1, loc0, keep, prefix, total):
+def spread(chunks, near1, far1, near0, far0, mid, loc1, loc0, keep, prefix, total):
     steps, _, columns, bins = loc1.shape
     rows = keep.shape[0]
     vmem = pl.BlockSpec(memory_space=pltpu.VMEM)
     return pl.pallas_call(
         functools.partial(spread_kernel, chunks, rows),
         out_shape=jax.ShapeDtypeStruct((steps, rows, columns, bins), BF16),
-        in_specs=[vmem] * 8,
+        in_specs=[vmem] * 10,
         out_specs=pl.BlockSpec(memory_space=pl.ANY),
         scratch_shapes=[
             pltpu.VMEM((rows, columns, 2 * bins), BF16),
             pltpu.VMEM((rows, columns, bins), F32),
+            pltpu.VMEM((1, columns, bins), F32),
+            pltpu.VMEM((1, columns, bins), F32),
             pltpu.VMEM((steps, rows, columns, bins), BF16),
             pltpu.SemaphoreType.DMA((steps,)),
         ],
@@ -506,7 +516,7 @@
             transcendentals=0,
         ),
         name="spread",
-    )(near, far, mid, loc1, loc0, keep, prefix, total)
+    )(near1, far1, near0, far0, mid, loc1, loc0, keep, prefix, total)
 
 
 def local(previous, initial, rates, transitions):
@@ -528,8 +538,8 @@
     mid, near0, far0 = send(code, 2), send(code0, 1), send(code0, 3)
     prefix, total = products(transitions, steps)
     chunks = (most, rest)
-    near, far = ready(chunks, [near1, near0, far1, far0], keep, total)
-    return spread(chunks, near, far, mid, loc1, loc0, keep, prefix, total)
+    ready1 = ready(most, near1, far1, keep, total)
+    return spread(chunks, *ready1, near0, far0, mid, loc1, loc0, keep, prefix, total)
 
 
 def solution(mesh):

time: 48.4 us -> 46.8 us (0.967)
  the two profiles are of different devices: /device:TPU:22 before, /device:TPU:14 now
where the time goes in v3:
time: 46.8 us; the launch traced here: 46.5 us
  Pallas kernels  22.9 us (49%)
  starting transfers between devices  18.9 us (40%)
  waiting for transfers between devices  4.69 us (10%)
    ppermute x5, starting transfers between devices, send(): return lax.ppermute(code, 'tm', [(i, i + hop) for i in range(blocks - hop)])  10.6 us
    pallas_call x1, Pallas kernels, inner_rows(): pl.pallas_call(functools.partial(inner_kernel, steps, rows), out_shape=[p...  8.58 us
    ppermute x1, starting transfers between devices, local(): lax.ppermute(outer_edge, 'space', between + [(j, i) for i, j in between])  8.12 us
    pallas_call x1, Pallas kernels, spread(): pl.pallas_call(functools.partial(spread_kernel, chunks, rows), out_shape=...  5.7 us
    ppermute x5, waiting for transfers between devices, send(): return lax.ppermute(code, 'tm', [(i, i + hop) for i in range(blocks - hop)])  4.68 us
    pallas_call x1, Pallas kernels, products(): pl.pallas_call(functools.partial(product_kernel, steps), out_shape=[pltpu...  3.22 us
    pallas_call x1, Pallas kernels, outer_row(): pl.pallas_call(functools.partial(outer_kernel, steps), out_shape=[pltpu.V...  2.46 us
    pallas_call x1, Pallas kernels, edges(): pl.pallas_call(functools.partial(edge_kernel, steps, rows), out_shape=[ja...  2.13 us
  transfers between devices with their start and end apart: 7, of which 1 were waited for; matrix products, arithmetic and copies ran while one was open for 0% of the time, Pallas kernels for 32%

profile of v3, /device:TPU:14, one launch (start us, length us, event | category | flops | bytes accessed | tf_op | source)
XLA Modules:
  0.0 46.5 jit_solution(16251061595527648688)
XLA Ops:
  0.0 2.1 %edges.1 = (bf16[16,256,128]{2,1,0:T(8,128)(2,1)S(1)}, bf16[16,256,128]{2,1,0:T(8,128)(2,1)S(1)}) custom-call(bf16[16,6,256,128]{3,2,1,0:T(8,128)(2,1)} %prev_ref.3, f32[6,256]{1,0:T(8,128)} %line_ref.3), custom_call_target="tpu_custom_call" | custom-call | tf_op jit(solution)/shard_map/edges/pallas_call | solution.py:147
  2.1 0.1 collective-permute-start
  2.2 8.1 %collective-permute-start.3 = (bf16[16,256,128]{2,1,0:T(8,128)(2,1)S(1)}, bf16[16,256,128]{2,1,0:T(8,128)(2,1)S(1)}, u32[]{:S(2)}, u32[]{:S(2)}) collective-permute-start(bf16[16,256,128]{2,1,0:T(8,128)(2,1)S(1)} %get-tuple-element.26), channel_id=1, source_target_pairs={{4,8},{12,16},{20,24},{28,32},{36,40},{44,48},{52,56},{60,64},{68,... | collective-permute-start | bytes 3145736 | tf_op jit(solution)/shard_map/ppermute | solution.py:528
  10.4 0.0 collective-permute-done.halo_ref
  10.4 8.6 %inner_rows.1 = (f32[16,5,256,128]{3,2,1,0:T(8,128)S(1)}, bf16[1296,128]{1,0:T(8,128)(2,1)S(1)}, f32[16,256,128]{2,1,0:T(8,128)S(1)}, f32[256,128]{1,0:T(8,128)S...) custom-call(bf16[16,6,256,128]{3,2,1,0:T(8,128)(2,1)} %prev_ref.3, ...), custom_call_target="tpu_custom_call" | custom-call | flops 3221225472 | bytes 6291456 | tf_op jit(solution)/shard_map/inner_rows/pallas_call | solution.py:267
  19.0 0.7 %collective-permute-start.2 = (bf16[1296,128]{1,0:T(8,128)(2,1)S(1)}, bf16[1296,128]{1,0:T(8,128)(2,1)S(1)}, u32[]{:S(2)}, u32[]{:S(2)}) collective-permute-start(bf16[1296,128]{1,0:T(8,128)(2,1)S(1)} %get-tuple-element.21.most_ref), channel_id=1, source_target_pairs={{0,3},{4,7},{8,11},{12,15},{16,19},{20,23},{24,27},{28,31},{32,35}... | collective-permute-start | bytes 995336 | tf_op jit(solution)/shard_map/ppermute | solution.py:532
  19.7 3.5 %collective-permute-start.1 = (bf16[1296,128]{1,0:T(8,128)(2,1)S(1)}, bf16[1296,128]{1,0:T(8,128)(2,1)S(1)}, u32[]{:S(2)}, u32[]{:S(2)}) collective-permute-start(bf16[1296,128]{1,0:T(8,128)(2,1)S(1)} %get-tuple-element.21.most_ref), channel_id=1, source_target_pairs={{0,1},{1,2},{2,3},{4,5},{5,6},{6,7},{8,9},{9,10},{10,11},{12,13},{... | collective-permute-start | bytes 995336 | tf_op jit(solution)/shard_map/ppermute | solution.py:532
  23.2 0.0 collective-permute-done.3.halo_ref
  23.2 2.5 %outer_row.1 = (f32[16,1,256,128]{3,2,1,0:T(8,128)S(1)}, bf16[272,128]{1,0:T(8,128)(2,1)S(1)}, bf16[1568,128]{1,0:T(8,128)(2,1)S(1)}) custom-call(bf16[16,256,128]{2,1,0:T(8,128)(2,1)S(1)} %collective-permute-done.3.halo_ref, f32[16,256,128]{2,1,0:T(8,128)S(1)} %get-tuple-element.27.part_ref, f32[256,128]{1,0:T(8,128)S(1)} %get-tuple-element.28.first_ref, ...), custom_call_target="tpu_custom_call" | custom-call | tf_op jit(solution)/shard_map/outer_row/pallas_call | solution.py:330
  25.6 3.9 %collective-permute-start.6 = (bf16[1568,128]{1,0:T(8,128)(2,1)S(1)}, bf16[1568,128]{1,0:T(8,128)(2,1)S(1)}, u32[]{:S(2)}, u32[]{:S(2)}) collective-permute-start(bf16[1568,128]{1,0:T(8,128)(2,1)S(1)} %get-tuple-element.31), channel_id=1, source_target_pairs={{0,2},{1,3},{4,6},{5,7},{8,10},{9,11},{12,14},{13,15},{16,18},{17,... | collective-permute-start | bytes 1204232 | tf_op jit(solution)/shard_map/ppermute | solution.py:532
  29.5 3.2 %products.1 = (bf16[16,256,256]{2,1,0:T(8,128)(2,1)S(1)}, bf16[2,256,256]{2,1,0:T(8,128)(2,1)S(1)}) custom-call(f32[64,128,128]{2,1,0:T(8,128)} %trans_ref.3), custom_call_target="tpu_custom_call" | custom-call | tf_op jit(solution)/shard_map/products/pallas_call | solution.py:380
  32.8 0.7 %collective-permute-start.5 = (bf16[272,128]{1,0:T(8,128)(2,1)S(1)}, bf16[272,128]{1,0:T(8,128)(2,1)S(1)}, u32[]{:S(2)}, u32[]{:S(2)}) collective-permute-start(bf16[272,128]{1,0:T(8,128)(2,1)S(1)} %get-tuple-element.30), channel_id=1, source_target_pairs={{0,3},{4,7},{8,11},{12,15},{16,19},{20,23},{24,27},{28,31},{32,35}... | collective-permute-start | bytes 208904 | tf_op jit(solution)/shard_map/ppermute | solution.py:532
  33.4 1.9 %collective-permute-start.4 = (bf16[272,128]{1,0:T(8,128)(2,1)S(1)}, bf16[272,128]{1,0:T(8,128)(2,1)S(1)}, u32[]{:S(2)}, u32[]{:S(2)}) collective-permute-start(bf16[272,128]{1,0:T(8,128)(2,1)S(1)} %get-tuple-element.30), channel_id=1, source_target_pairs={{0,1},{1,2},{2,3},{4,5},{5,6},{6,7},{8,9},{9,10},{10,11},{12,13},{... | collective-permute-start | bytes 208904 | tf_op jit(solution)/shard_map/ppermute | solution.py:532
  35.4 0.0 collective-permute-done.2.far_code
  35.4 0.0 collective-permute-done.1.near_code
  35.4 0.8 %ready.1 = (f32[5,256,128]{2,1,0:T(8,128)S(1)}, f32[5,256,128]{2,1,0:T(8,128)S(1)}) custom-call(bf16[1296,128]{1,0:T(8,128)(2,1)S(1)} %collective-permute-done.1.near_code, bf16[1296,128]{1,0:T(8,128)(2,1)S(1)} %collective-permute-done.2.far_code, f32[6,256,128]{2,1,0:T(8,128)S(1)} %get-tuple-element.22.keep_ref, ...), custom_call_target="tpu_custom_call" | custom-call | flops 4000000000 | bytes 8000000 | tf_op jit(solution)/shard_map/ready/pallas_call | solution.py:433
  36.2 0.0 collective-permute-done.5.far0_code
  36.2 4.7 %collective-permute-done.4.near0_code = bf16[272,128]{1,0:T(8,128)(2,1)S(1)} collective-permute-done((bf16[272,128]{1,0:T(8,128)(2,1)S(1)}, bf16[272,128]{1,0:T(8,128)(2,1)S(1)}, u32[]{:S(2)}, u32[]{:S(2)}) %collective-permute-start.4) | collective-permute-done | bytes 69664 | tf_op jit(solution)/shard_map/ppermute | solution.py:532
  40.8 0.0 collective-permute-done.6.mid_ref
  40.8 5.7 %spread.1 = bf16[16,6,256,128]{3,2,1,0:T(8,128)(2,1)} custom-call(f32[5,256,128]{2,1,0:T(8,128)S(1)} %get-tuple-element.24.near1_ref, f32[5,256,128]{2,1,0:T(8,128)S(1)} %get-tuple-element.25.far1_ref, bf16[272,128]{1,0:T(8,128)(2,1)S(1)} %collective-permute-done.4.near0_code, bf16[272,128]{1,0:T(8,128)(2,1)S(1)} %collective-permute-done.5.far0_code, ...), custom_call_target="tpu_custom_call" | custom-call | flops 3221225472 | bytes 6291456 | tf_op jit(solution)/shard_map/spread/pallas_call | solution.py:499
Async XLA Ops:
  2.1 8.2 %collective-permute-start = (bf16[16,256,128]{2,1,0:T(8,128)(2,1)S(1)}, bf16[16,256,128]{2,1,0:T(8,128)(2,1)S(1)}, u32[]{:S(2)}, u32[]{:S(2)}) collective-permute-start(bf16[16,256,128]{2,1,0:T(8,128)(2,1)S(1)} %get-tuple-element.20), channel_id=1, source_target_pairs={{0,4},{8,12},{16,20},{24,28},{32,36},{40,44},{48,52},{56,60},{64,6... | collective-permute-start | bytes 3145736 | tf_op jit(solution)/shard_map/ppermute | solution.py:529
  2.2 20.9 %collective-permute-start.3 = (bf16[16,256,128]{2,1,0:T(8,128)(2,1)S(1)}, bf16[16,256,128]{2,1,0:T(8,128)(2,1)S(1)}, u32[]{:S(2)}, u32[]{:S(2)}) collective-permute-start(bf16[16,256,128]{2,1,0:T(8,128)(2,1)S(1)} %get-tuple-element.26), channel_id=1, source_target_pairs={{4,8},{12,16},{20,24},{28,32},{36,40},{44,48},{52,56},{60,64},{68,... | collective-permute-start | bytes 3145736 | tf_op jit(solution)/shard_map/ppermute | solution.py:528
  19.0 16.4 %collective-permute-start.2 = (bf16[1296,128]{1,0:T(8,128)(2,1)S(1)}, bf16[1296,128]{1,0:T(8,128)(2,1)S(1)}, u32[]{:S(2)}, u32[]{:S(2)}) collective-permute-start(bf16[1296,128]{1,0:T(8,128)(2,1)S(1)} %get-tuple-element.21.most_ref), channel_id=1, source_target_pairs={{0,3},{4,7},{8,11},{12,15},{16,19},{20,23},{24,27},{28,31},{32,35}... | collective-permute-start | bytes 995336 | tf_op jit(solution)/shard_map/ppermute | solution.py:532
  19.7 15.7 %collective-permute-start.1 = (bf16[1296,128]{1,0:T(8,128)(2,1)S(1)}, bf16[1296,128]{1,0:T(8,128)(2,1)S(1)}, u32[]{:S(2)}, u32[]{:S(2)}) collective-permute-start(bf16[1296,128]{1,0:T(8,128)(2,1)S(1)} %get-tuple-element.21.most_ref), channel_id=1, source_target_pairs={{0,1},{1,2},{2,3},{4,5},{5,6},{6,7},{8,9},{9,10},{10,11},{12,13},{... | collective-permute-start | bytes 995336 | tf_op jit(solution)/shard_map/ppermute | solution.py:532
  25.6 15.2 %collective-permute-start.6 = (bf16[1568,128]{1,0:T(8,128)(2,1)S(1)}, bf16[1568,128]{1,0:T(8,128)(2,1)S(1)}, u32[]{:S(2)}, u32[]{:S(2)}) collective-permute-start(bf16[1568,128]{1,0:T(8,128)(2,1)S(1)} %get-tuple-element.31), channel_id=1, source_target_pairs={{0,2},{1,3},{4,6},{5,7},{8,10},{9,11},{12,14},{13,15},{16,18},{17,... | collective-permute-start | bytes 1204232 | tf_op jit(solution)/shard_map/ppermute | solution.py:532
  32.8 3.4 %collective-permute-start.5 = (bf16[272,128]{1,0:T(8,128)(2,1)S(1)}, bf16[272,128]{1,0:T(8,128)(2,1)S(1)}, u32[]{:S(2)}, u32[]{:S(2)}) collective-permute-start(bf16[272,128]{1,0:T(8,128)(2,1)S(1)} %get-tuple-element.30), channel_id=1, source_target_pairs={{0,3},{4,7},{8,11},{12,15},{16,19},{20,23},{24,27},{28,31},{32,35}... | collective-permute-start | bytes 208904 | tf_op jit(solution)/shard_map/ppermute | solution.py:532
  33.4 7.4 %collective-permute-start.4 = (bf16[272,128]{1,0:T(8,128)(2,1)S(1)}, bf16[272,128]{1,0:T(8,128)(2,1)S(1)}, u32[]{:S(2)}, u32[]{:S(2)}) collective-permute-start(bf16[272,128]{1,0:T(8,128)(2,1)S(1)} %get-tuple-element.30), channel_id=1, source_target_pairs={{0,1},{1,2},{2,3},{4,5},{5,6},{6,7},{8,9},{9,10},{10,11},{12,13},{... | collective-permute-start | bytes 208904 | tf_op jit(solution)/shard_map/ppermute | solution.py:532

commit v4 on v3

--- a/solution.py
+++ b/solution.py
@@ -427,27 +427,35 @@
     stream(1, len(pieces), lambda _: total_ref[1], left_far, store)
 
 
-def ready(calc, near, far, keep, total):
+def chunks_kernel(
+    chunks, near1_code, far1_code, near0_code, far0_code, keep_ref, total_ref,
+    near1_ref, far1_ref, near0_ref, far0_ref,
+):
+    ready_kernel(chunks[0], near1_code, far1_code, keep_ref, total_ref, near1_ref, far1_ref)
+    ready_kernel(chunks[1], near0_code, far0_code, keep_ref, total_ref, near0_ref, far0_ref)
+
+
+def ready(chunks, codes, keep, total):
     _, columns, bins = keep.shape
     vmem = pl.BlockSpec(memory_space=pltpu.VMEM)
     return pl.pallas_call(
-        functools.partial(ready_kernel, calc),
-        out_shape=[pltpu.VMEM((len(calc), columns, bins), F32)] * 2,
-        in_specs=[vmem] * 4,
-        out_specs=[vmem] * 2,
+        functools.partial(chunks_kernel, chunks),
+        out_shape=[pltpu.VMEM((len(calc), columns, bins), F32) for calc in chunks for _ in range(2)],
+        in_specs=[vmem] * 6,
+        out_specs=[vmem] * 4,
         compiler_params=pltpu.CompilerParams(vmem_limit_bytes=4 * MIB),
         cost_estimate=pl.CostEstimate(
-            flops=4_000_000_000, bytes_accessed=8_000_000, transcendentals=0
+            flops=2000000000, bytes_accessed=4000000, transcendentals=0
         ),
         name="ready",
-    )(near, far, keep, total)
+    )(*codes, keep, total)
 
 
 def spread_kernel(
     chunks, rows,
-    near1_ref, far1_ref, near0_code, far0_code, mid_ref, loc1_ref, loc0_ref, keep_ref, prefix_ref, total_ref,
+    near1_ref, far1_ref, near0_ref, far0_ref, mid_ref, loc1_ref, loc0_ref, keep_ref, prefix_ref, total_ref,
     out_ref,
-    entering, power, near0_ref, far0_ref, stage, sems,
+    entering, power, stage, sems,
 ):
     odd = lax.rem(lax.axis_index("space"), 2)
     steps, _, columns, bins = stage.shape
@@ -461,7 +469,6 @@
         at += 16
     count = len(pieces)
     nears, fars = (near1_ref, near0_ref), (far1_ref, far0_ref)
-    ready_kernel(chunks[1], near0_code, far0_code, keep_ref, total_ref, near0_ref, far0_ref)
 
     def cells_of(i):
         return pieces[i][2], slice(pieces[i][3], pieces[i][3] + CHUNK)
@@ -504,8 +511,6 @@
         scratch_shapes=[
             pltpu.VMEM((rows, columns, 2 * bins), BF16),
             pltpu.VMEM((rows, columns, bins), F32),
-            pltpu.VMEM((1, columns, bins), F32),
-            pltpu.VMEM((1, columns, bins), F32),
             pltpu.VMEM((steps, rows, columns, bins), BF16),
             pltpu.SemaphoreType.DMA((steps,)),
         ],
@@ -531,15 +536,15 @@
     def send(code, hop):
         return lax.ppermute(code, "tm", [(i, i + hop) for i in range(blocks - hop)])
 
-    most, rest = tuple(range(1, rows)), (0,)
+    chunks = most, rest = tuple(range(1, rows)), (0,)
     loc1, code1, part, first, keep, rhs = inner_rows(previous, inner, initial, rates, transitions)
     near1, far1 = send(code1, 1), send(code1, 3)
     loc0, code0, code = outer_row(outer, part, first, keep, rhs, code1)
     mid, near0, far0 = send(code, 2), send(code0, 1), send(code0, 3)
     prefix, total = products(transitions, steps)
     chunks = (most, rest)
-    ready1 = ready(most, near1, far1, keep, total)
-    return spread(chunks, *ready1, near0, far0, mid, loc1, loc0, keep, prefix, total)
+    brought = ready(chunks, [near1, far1, near0, far0], keep, total)
+    return spread(chunks, *brought, mid, loc1, loc0, keep, prefix, total)
 
 
 def solution(mesh):

time: 46.8 us -> 48 us (1.026)
  waiting for transfers between devices: 4.69 us -> 5.52 us
    ppermute x5, waiting for transfers between devices: 4.68 us -> 5.51 us  [send(): return lax.ppermute(code, 'tm', [(i, i + hop) for i in range(blocks - hop)])]
where the time goes in v4:
time: 48 us; the launch traced here: 47.8 us
  Pallas kernels  23.3 us (49%)
  starting transfers between devices  18.8 us (39%)
  waiting for transfers between devices  5.52 us (12%)
    ppermute x5, starting transfers between devices, send(): return lax.ppermute(code, 'tm', [(i, i + hop) for i in range(blocks - hop)])  10.6 us
    pallas_call x1, Pallas kernels, inner_rows(): pl.pallas_call(functools.partial(inner_kernel, steps, rows), out_shape=[p...  8.62 us
    ppermute x1, starting transfers between devices, local(): lax.ppermute(outer_edge, 'space', between + [(j, i) for i, j in between])  8.12 us
    pallas_call x1, Pallas kernels, spread(): pl.pallas_call(functools.partial(spread_kernel, chunks, rows), out_shape=...  5.94 us
    ppermute x5, waiting for transfers between devices, send(): return lax.ppermute(code, 'tm', [(i, i + hop) for i in range(blocks - hop)])  5.51 us
    pallas_call x1, Pallas kernels, products(): pl.pallas_call(functools.partial(product_kernel, steps), out_shape=[pltpu...  3.21 us
    pallas_call x1, Pallas kernels, outer_row(): pl.pallas_call(functools.partial(outer_kernel, steps), out_shape=[pltpu.V...  2.47 us
    pallas_call x1, Pallas kernels, edges(): pl.pallas_call(functools.partial(edge_kernel, steps, rows), out_shape=[ja...  2.13 us
  transfers between devices with their start and end apart: 7, of which 1 were waited for; matrix products, arithmetic and copies ran while one was open for 0% of the time, Pallas kernels for 32%

profile of v4, /device:TPU:14, one launch (start us, length us, event | category | flops | bytes accessed | tf_op | source)
XLA Modules:
  0.0 47.8 jit_solution(16283974440627518492)
XLA Ops:
  0.0 2.1 %edges.1 = (bf16[16,256,128]{2,1,0:T(8,128)(2,1)S(1)}, bf16[16,256,128]{2,1,0:T(8,128)(2,1)S(1)}) custom-call(bf16[16,6,256,128]{3,2,1,0:T(8,128)(2,1)} %prev_ref.3, f32[6,256]{1,0:T(8,128)} %line_ref.3), custom_call_target="tpu_custom_call" | custom-call | tf_op jit(solution)/shard_map/edges/pallas_call | solution.py:147
  2.1 0.1 collective-permute-start
  2.2 8.1 %collective-permute-start.3 = (bf16[16,256,128]{2,1,0:T(8,128)(2,1)S(1)}, bf16[16,256,128]{2,1,0:T(8,128)(2,1)S(1)}, u32[]{:S(2)}, u32[]{:S(2)}) collective-permute-start(bf16[16,256,128]{2,1,0:T(8,128)(2,1)S(1)} %get-tuple-element.24), channel_id=1, source_target_pairs={{4,8},{12,16},{20,24},{28,32},{36,40},{44,48},{52,56},{60,64},{68,... | collective-permute-start | bytes 3145736 | tf_op jit(solution)/shard_map/ppermute | solution.py:533
  10.4 0.0 collective-permute-done.halo_ref
  10.4 8.6 %inner_rows.1 = (f32[16,5,256,128]{3,2,1,0:T(8,128)S(1)}, bf16[1296,128]{1,0:T(8,128)(2,1)S(1)}, f32[16,256,128]{2,1,0:T(8,128)S(1)}, f32[256,128]{1,0:T(8,128)S...) custom-call(bf16[16,6,256,128]{3,2,1,0:T(8,128)(2,1)} %prev_ref.3, ...), custom_call_target="tpu_custom_call" | custom-call | flops 3221225472 | bytes 6291456 | tf_op jit(solution)/shard_map/inner_rows/pallas_call | solution.py:267
  19.0 0.7 %collective-permute-start.2 = (bf16[1296,128]{1,0:T(8,128)(2,1)S(1)}, bf16[1296,128]{1,0:T(8,128)(2,1)S(1)}, u32[]{:S(2)}, u32[]{:S(2)}) collective-permute-start(bf16[1296,128]{1,0:T(8,128)(2,1)S(1)} %get-tuple-element.23.most_ref), channel_id=1, source_target_pairs={{0,3},{4,7},{8,11},{12,15},{16,19},{20,23},{24,27},{28,31},{32,35}... | collective-permute-start | bytes 995336 | tf_op jit(solution)/shard_map/ppermute | solution.py:537
  19.7 3.5 %collective-permute-start.1 = (bf16[1296,128]{1,0:T(8,128)(2,1)S(1)}, bf16[1296,128]{1,0:T(8,128)(2,1)S(1)}, u32[]{:S(2)}, u32[]{:S(2)}) collective-permute-start(bf16[1296,128]{1,0:T(8,128)(2,1)S(1)} %get-tuple-element.23.most_ref), channel_id=1, source_target_pairs={{0,1},{1,2},{2,3},{4,5},{5,6},{6,7},{8,9},{9,10},{10,11},{12,13},{... | collective-permute-start | bytes 995336 | tf_op jit(solution)/shard_map/ppermute | solution.py:537
  23.2 0.0 collective-permute-done.3.halo_ref
  23.2 2.5 %outer_row.1 = (f32[16,1,256,128]{3,2,1,0:T(8,128)S(1)}, bf16[272,128]{1,0:T(8,128)(2,1)S(1)}, bf16[1568,128]{1,0:T(8,128)(2,1)S(1)}) custom-call(bf16[16,256,128]{2,1,0:T(8,128)(2,1)S(1)} %collective-permute-done.3.halo_ref, f32[16,256,128]{2,1,0:T(8,128)S(1)} %get-tuple-element.25.part_ref, f32[256,128]{1,0:T(8,128)S(1)} %get-tuple-element.26.first_ref, ...), custom_call_target="tpu_custom_call" | custom-call | tf_op jit(solution)/shard_map/outer_row/pallas_call | solution.py:330
  25.7 3.8 %collective-permute-start.6 = (bf16[1568,128]{1,0:T(8,128)(2,1)S(1)}, bf16[1568,128]{1,0:T(8,128)(2,1)S(1)}, u32[]{:S(2)}, u32[]{:S(2)}) collective-permute-start(bf16[1568,128]{1,0:T(8,128)(2,1)S(1)} %get-tuple-element.35), channel_id=1, source_target_pairs={{0,2},{1,3},{4,6},{5,7},{8,10},{9,11},{12,14},{13,15},{16,18},{17,... | collective-permute-start | bytes 1204232 | tf_op jit(solution)/shard_map/ppermute | solution.py:537
  29.5 0.7 %collective-permute-start.5 = (bf16[272,128]{1,0:T(8,128)(2,1)S(1)}, bf16[272,128]{1,0:T(8,128)(2,1)S(1)}, u32[]{:S(2)}, u32[]{:S(2)}) collective-permute-start(bf16[272,128]{1,0:T(8,128)(2,1)S(1)} %get-tuple-element.29), channel_id=1, source_target_pairs={{0,3},{4,7},{8,11},{12,15},{16,19},{20,23},{24,27},{28,31},{32,35}... | collective-permute-start | bytes 208904 | tf_op jit(solution)/shard_map/ppermute | solution.py:537
  30.2 1.9 %collective-permute-start.4 = (bf16[272,128]{1,0:T(8,128)(2,1)S(1)}, bf16[272,128]{1,0:T(8,128)(2,1)S(1)}, u32[]{:S(2)}, u32[]{:S(2)}) collective-permute-start(bf16[272,128]{1,0:T(8,128)(2,1)S(1)} %get-tuple-element.29), channel_id=1, source_target_pairs={{0,1},{1,2},{2,3},{4,5},{5,6},{6,7},{8,9},{9,10},{10,11},{12,13},{... | collective-permute-start | bytes 208904 | tf_op jit(solution)/shard_map/ppermute | solution.py:537
  32.1 3.2 %products.1 = (bf16[16,256,256]{2,1,0:T(8,128)(2,1)S(1)}, bf16[2,256,256]{2,1,0:T(8,128)(2,1)S(1)}) custom-call(f32[64,128,128]{2,1,0:T(8,128)} %trans_ref.3), custom_call_target="tpu_custom_call" | custom-call | tf_op jit(solution)/shard_map/products/pallas_call | solution.py:380
  35.4 0.0 collective-permute-done.5.far0_code
  35.4 5.5 %collective-permute-done.4.near0_code = bf16[272,128]{1,0:T(8,128)(2,1)S(1)} collective-permute-done((bf16[272,128]{1,0:T(8,128)(2,1)S(1)}, bf16[272,128]{1,0:T(8,128)(2,1)S(1)}, u32[]{:S(2)}, u32[]{:S(2)}) %collective-permute-start.4) | collective-permute-done | bytes 69664 | tf_op jit(solution)/shard_map/ppermute | solution.py:537
  40.9 0.0 collective-permute-done.2.far1_code
  40.9 0.0 collective-permute-done.1.near1_code
  40.9 0.9 %ready.1 = (f32[5,256,128]{2,1,0:T(8,128)S(1)}, f32[5,256,128]{2,1,0:T(8,128)S(1)}, f32[1,256,128]{2,1,0:T(8,128)S(1)}, f32[1,256,128]{2,1,0:T(8,128)S(1)}) custom-call(bf16[1296,128]{1,0:T(8,128)(2,1)S(1)} %collective-permute-done.1.near1_code, bf16[1296,128]{1,0:T(8,128)(2,1)S(1)} %collective-permute-done.2.far1_code, ...), custom_call_target="tpu_custom_call" | custom-call | flops 2000000000 | bytes 4000000 | tf_op jit(solution)/shard_map/ready/pallas_call | solution.py:441
  41.8 0.0 collective-permute-done.6.mid_ref
  41.8 5.9 %spread.1 = bf16[16,6,256,128]{3,2,1,0:T(8,128)(2,1)} custom-call(f32[5,256,128]{2,1,0:T(8,128)S(1)} %get-tuple-element.31.near1_ref, f32[5,256,128]{2,1,0:T(8,128)S(1)} %get-tuple-element.32.far1_ref, f32[1,256,128]{2,1,0:T(8,128)S(1)} %get-tuple-element.33.near0_ref, f32[1,256,128]{2,1,0:T(8,128)S(1)} %get-tuple-element.34.far0_ref, ...), custom_call_target="tpu_custom_call" | custom-call | flops 3221225472 | bytes 6291456 | tf_op jit(solution)/shard_map/spread/pallas_call | solution.py:506
Async XLA Ops:
  2.1 8.2 %collective-permute-start = (bf16[16,256,128]{2,1,0:T(8,128)(2,1)S(1)}, bf16[16,256,128]{2,1,0:T(8,128)(2,1)S(1)}, u32[]{:S(2)}, u32[]{:S(2)}) collective-permute-start(bf16[16,256,128]{2,1,0:T(8,128)(2,1)S(1)} %get-tuple-element.22), channel_id=1, source_target_pairs={{0,4},{8,12},{16,20},{24,28},{32,36},{40,44},{48,52},{56,60},{64,6... | collective-permute-start | bytes 3145736 | tf_op jit(solution)/shard_map/ppermute | solution.py:534
  2.2 20.9 %collective-permute-start.3 = (bf16[16,256,128]{2,1,0:T(8,128)(2,1)S(1)}, bf16[16,256,128]{2,1,0:T(8,128)(2,1)S(1)}, u32[]{:S(2)}, u32[]{:S(2)}) collective-permute-start(bf16[16,256,128]{2,1,0:T(8,128)(2,1)S(1)} %get-tuple-element.24), channel_id=1, source_target_pairs={{4,8},{12,16},{20,24},{28,32},{36,40},{44,48},{52,56},{60,64},{68,... | collective-permute-start | bytes 3145736 | tf_op jit(solution)/shard_map/ppermute | solution.py:533
  19.0 21.9 %collective-permute-start.2 = (bf16[1296,128]{1,0:T(8,128)(2,1)S(1)}, bf16[1296,128]{1,0:T(8,128)(2,1)S(1)}, u32[]{:S(2)}, u32[]{:S(2)}) collective-permute-start(bf16[1296,128]{1,0:T(8,128)(2,1)S(1)} %get-tuple-element.23.most_ref), channel_id=1, source_target_pairs={{0,3},{4,7},{8,11},{12,15},{16,19},{20,23},{24,27},{28,31},{32,35}... | collective-permute-start | bytes 995336 | tf_op jit(solution)/shard_map/ppermute | solution.py:537
  19.7 21.2 %collective-permute-start.1 = (bf16[1296,128]{1,0:T(8,128)(2,1)S(1)}, bf16[1296,128]{1,0:T(8,128)(2,1)S(1)}, u32[]{:S(2)}, u32[]{:S(2)}) collective-permute-start(bf16[1296,128]{1,0:T(8,128)(2,1)S(1)} %get-tuple-element.23.most_ref), channel_id=1, source_target_pairs={{0,1},{1,2},{2,3},{4,5},{5,6},{6,7},{8,9},{9,10},{10,11},{12,13},{... | collective-permute-start | bytes 995336 | tf_op jit(solution)/shard_map/ppermute | solution.py:537
  25.7 16.1 %collective-permute-start.6 = (bf16[1568,128]{1,0:T(8,128)(2,1)S(1)}, bf16[1568,128]{1,0:T(8,128)(2,1)S(1)}, u32[]{:S(2)}, u32[]{:S(2)}) collective-permute-start(bf16[1568,128]{1,0:T(8,128)(2,1)S(1)} %get-tuple-element.35), channel_id=1, source_target_pairs={{0,2},{1,3},{4,6},{5,7},{8,10},{9,11},{12,14},{13,15},{16,18},{17,... | collective-permute-start | bytes 1204232 | tf_op jit(solution)/shard_map/ppermute | solution.py:537
  29.5 5.8 %collective-permute-start.5 = (bf16[272,128]{1,0:T(8,128)(2,1)S(1)}, bf16[272,128]{1,0:T(8,128)(2,1)S(1)}, u32[]{:S(2)}, u32[]{:S(2)}) collective-permute-start(bf16[272,128]{1,0:T(8,128)(2,1)S(1)} %get-tuple-element.29), channel_id=1, source_target_pairs={{0,3},{4,7},{8,11},{12,15},{16,19},{20,23},{24,27},{28,31},{32,35}... | collective-permute-start | bytes 208904 | tf_op jit(solution)/shard_map/ppermute | solution.py:537
  30.2 10.7 %collective-permute-start.4 = (bf16[272,128]{1,0:T(8,128)(2,1)S(1)}, bf16[272,128]{1,0:T(8,128)(2,1)S(1)}, u32[]{:S(2)}, u32[]{:S(2)}) collective-permute-start(bf16[272,128]{1,0:T(8,128)(2,1)S(1)} %get-tuple-element.29), channel_id=1, source_target_pairs={{0,1},{1,2},{2,3},{4,5},{5,6},{6,7},{8,9},{9,10},{10,11},{12,13},{... | collective-permute-start | bytes 208904 | tf_op jit(solution)/shard_map/ppermute | solution.py:537

commit v5 on v3

--- a/solution.py
+++ b/solution.py
@@ -164,7 +164,7 @@
 def inner_kernel(
     steps, rows,
     prev_ref, halo_ref, init_ref, line_ref, trans_ref,
-    loc_ref, code_ref, part_ref, first_ref, keep_ref, rhs_ref,
+    loc_ref, code_ref, tail_ref, part_ref, first_ref, keep_ref, rhs_ref,
     pbuf, ibuf, tbuf, even, odds, weight, state, rates_ref, psem, isem, tsem, rsem,
 ):
     odd = lax.rem(lax.axis_index("space"), 2)
@@ -254,6 +254,7 @@
         fill(0, unit, 0)
     stream(steps, len(pieces), lambda t: rhs_ref[t], left_of, store, beside)
     finish(loc_ref, code_ref, steps)
+    tail_ref[...] = code_ref[code_ref.shape[0] - tail_ref.shape[0] :]
 
 
 def inner_rows(previous, halo, initial, rates, transitions):
@@ -269,13 +270,14 @@
         out_shape=[
             pltpu.VMEM((steps, rows - 1, columns, bins), F32),
             jax.ShapeDtypeStruct(((rows - 1) * columns + 16, bins), BF16),
+            jax.ShapeDtypeStruct((rows // 2 * columns + 16, bins), BF16),
             pltpu.VMEM((steps, columns, bins), F32),
             pltpu.VMEM((columns, bins), F32),
             pltpu.VMEM((rows, columns, bins), F32),
             pltpu.VMEM((steps, 2 * bins, 2 * bins), BF16),
         ],
         in_specs=[anywhere, vmem, anywhere, anywhere, anywhere],
-        out_specs=[vmem] * 6,
+        out_specs=[vmem] * 7,
         scratch_shapes=[
             pltpu.VMEM((steps, rows, columns, bins), BF16),
             pltpu.VMEM((rows, columns, bins), F32),
@@ -301,11 +303,13 @@
 
 
 def outer_kernel(
-    steps, halo_ref, part_ref, first_ref, keep_ref, rhs_ref, most_ref, loc_ref, code_ref, all_ref, state, sem
+    steps, halo_ref, part_ref, first_ref, keep_ref, rhs_ref, most_ref, after_ref, loc_ref, code_ref, all_ref, state, sem
 ):
     columns = first_ref.shape[0]
-    joined = most_ref.shape[0]
-    copy = pltpu.make_async_copy(most_ref, all_ref.at[pl.ds(0, joined)], sem)
+    joined = all_ref.shape[0] - code_ref.shape[0]
+    copy = pltpu.make_async_copy(
+        most_ref.at[pl.ds(0, joined - 16)], all_ref.at[pl.ds(0, joined - 16)], sem
+    )
     copy.start()
     state[...] = first_ref[...]
 
@@ -320,21 +324,23 @@
 
     stream(steps, columns // CHUNK, lambda t: rhs_ref[t], left_of, store)
     finish(loc_ref, code_ref, steps)
+    all_ref[joined - 16 : joined] = most_ref[most_ref.shape[0] - 16 :]
     all_ref[joined:] = code_ref[...]
     copy.wait()
 
 
-def outer_row(halo, part, first, keep, rhs, most):
+def outer_row(halo, part, first, keep, rhs, most, after):
     steps, columns, bins = part.shape
+    rows = keep.shape[0]
     vmem = pl.BlockSpec(memory_space=pltpu.VMEM)
     return pl.pallas_call(
         functools.partial(outer_kernel, steps),
         out_shape=[
             pltpu.VMEM((steps, 1, columns, bins), F32),
             jax.ShapeDtypeStruct((columns + 16, bins), BF16),
-            jax.ShapeDtypeStruct((most.shape[0] + columns + 16, bins), BF16),
-        ],
-        in_specs=[vmem] * 6,
+            jax.ShapeDtypeStruct(((rows - rows // 2) * columns + 32, bins), BF16),
+        ],
+        in_specs=[vmem] * 6 + [pl.BlockSpec(memory_space=pl.ANY)],
         out_specs=[vmem] * 3,
         scratch_shapes=[pltpu.VMEM((columns, bins), F32), pltpu.SemaphoreType.DMA],
         compiler_params=pltpu.CompilerParams(vmem_limit_bytes=4 * MIB),
@@ -342,7 +348,7 @@
             flops=0, bytes_accessed=0, transcendentals=0
         ),
         name="outer_row",
-    )(halo, part, first, keep, rhs, most)
+    )(halo, part, first, keep, rhs, most, after)
 
 
 def product_kernel(steps, trans_ref, prefix_ref, total_ref, work, sems):
@@ -391,7 +397,7 @@
         ],
         compiler_params=pltpu.CompilerParams(vmem_limit_bytes=16 * MIB),
         cost_estimate=pl.CostEstimate(
-            flops=0, bytes_accessed=0, transcendentals=0
+            flops=1000000000, bytes_accessed=0, transcendentals=0
         ),
         name="products",
     )(transitions)
@@ -437,31 +443,35 @@
         out_specs=[vmem] * 2,
         compiler_params=pltpu.CompilerParams(vmem_limit_bytes=4 * MIB),
         cost_estimate=pl.CostEstimate(
-            flops=4_000_000_000, bytes_accessed=8_000_000, transcendentals=0
+            flops=1000000000, bytes_accessed=2000000, transcendentals=0
         ),
         name="ready",
     )(near, far, keep, total)
 
 
-def spread_kernel(
-    chunks, rows,
-    near1_ref, far1_ref, near0_code, far0_code, mid_ref, loc1_ref, loc0_ref, keep_ref, prefix_ref, total_ref,
-    out_ref,
-    entering, power, near0_ref, far0_ref, stage, sems,
-):
+def spread_kernel(chunks, rows, *refs):
+    sources, refs = len(chunks), list(refs)
+    nears, fars, locs = [[refs.pop(0) for _ in chunks] for _ in range(3)]
+    mid_ref, keep_ref, prefix_ref, total_ref = [refs.pop(0) for _ in range(4)]
+    *_, out_ref, entering, power, near0_ref, far0_ref, stage, sems = refs
     odd = lax.rem(lax.axis_index("space"), 2)
-    steps, _, columns, bins = stage.shape
-    locs = (loc1_ref, loc0_ref)
+    steps, held, columns, bins = stage.shape
+    picked = [q for calc in chunks for _, q in calc]
+    base = jnp.minimum(place(min(picked), rows, odd), place(max(picked), rows, odd))
     pieces, at, scales = [], 0, []
     for k, calc in enumerate(chunks):
-        for n, q in enumerate(calc):
+        for n, q in calc:
             pieces += [(k, n, q, c, at + c) for c in range(0, columns, CHUNK)]
             at += columns
         scales.append(scale_of(mid_ref, at))
         at += 16
     count = len(pieces)
-    nears, fars = (near1_ref, near0_ref), (far1_ref, far0_ref)
-    ready_kernel(chunks[1], near0_code, far0_code, keep_ref, total_ref, near0_ref, far0_ref)
+    if sources > 1:
+        ready_kernel((0,), nears[1], fars[1], keep_ref, total_ref, near0_ref, far0_ref)
+        nears[1], fars[1] = near0_ref, far0_ref
+
+    def copy(t):
+        return pltpu.make_async_copy(stage.at[t], out_ref.at[t, pl.ds(base, held)], sems.at[t])
 
     def cells_of(i):
         return pieces[i][2], slice(pieces[i][3], pieces[i][3] + CHUNK)
@@ -473,7 +483,7 @@
     def store_mid(_, i, both):
         k, n, _, c, _ = pieces[i]
         state = nears[k][n, c : c + CHUNK] + decay(keep_ref[cells_of(i)]) * halves(both)
-        entering[cells_of(i)] = left(state)
+        entering[pieces[i][2], cells_of(i)[1]] = left(state)
         power[cells_of(i)] = jnp.ones((CHUNK, bins), F32)
 
     stream(1, count, lambda _: total_ref[0], left_mid, store_mid)
@@ -483,40 +493,47 @@
         factor = power[cells_of(i)] * keep_ref[cells_of(i)]
         power[cells_of(i)] = factor
         value = locs[k][t, n, c : c + CHUNK] + factor * halves(both)
-        stage[t, place(q, rows, odd), c : c + CHUNK] = value.astype(BF16)
+        stage[t, place(q, rows, odd) - base, c : c + CHUNK] = value.astype(BF16)
         if i == count - 1:
-            pltpu.make_async_copy(stage.at[t], out_ref.at[t], sems.at[t]).start()
+            copy(t).start()
 
     stream(steps, count, lambda t: prefix_ref[t], lambda t, i, slot: entering[cells_of(i)], store)
     for t in range(steps):
-        pltpu.make_async_copy(stage.at[t], out_ref.at[t], sems.at[t]).wait()
-
-
-def spread(chunks, near1, far1, near0, far0, mid, loc1, loc0, keep, prefix, total):
-    steps, _, columns, bins = loc1.shape
+        copy(t).wait()
+
+
+def spread(chunks, nears, fars, locs, mid, keep, prefix, total, before=None):
+    steps, _, columns, bins = locs[0].shape
     rows = keep.shape[0]
-    vmem = pl.BlockSpec(memory_space=pltpu.VMEM)
+    held = sum(len(calc) for calc in chunks)
+    vmem, anywhere = pl.BlockSpec(memory_space=pltpu.VMEM), pl.BlockSpec(memory_space=pl.ANY)
+    arrays = [*nears, *fars, *locs, mid, keep, prefix, total]
+    specs = [vmem] * len(arrays)
+    aliases = {}
+    if before is not None:
+        aliases = {len(arrays): 0}
+        arrays, specs = arrays + [before], specs + [anywhere]
     return pl.pallas_call(
         functools.partial(spread_kernel, chunks, rows),
         out_shape=jax.ShapeDtypeStruct((steps, rows, columns, bins), BF16),
-        in_specs=[vmem] * 10,
-        out_specs=pl.BlockSpec(memory_space=pl.ANY),
+        in_specs=specs,
+        out_specs=anywhere,
         scratch_shapes=[
             pltpu.VMEM((rows, columns, 2 * bins), BF16),
             pltpu.VMEM((rows, columns, bins), F32),
             pltpu.VMEM((1, columns, bins), F32),
             pltpu.VMEM((1, columns, bins), F32),
-            pltpu.VMEM((steps, rows, columns, bins), BF16),
+            pltpu.VMEM((steps, held, columns, bins), BF16),
             pltpu.SemaphoreType.DMA((steps,)),
         ],
+        input_output_aliases=aliases,
         compiler_params=pltpu.CompilerParams(vmem_limit_bytes=16 * MIB),
         cost_estimate=pl.CostEstimate(
-            flops=8 * steps * rows * columns * bins * bins,
-            bytes_accessed=steps * rows * columns * bins * 2,
+            flops=1000000000, bytes_accessed=2000000,
             transcendentals=0,
         ),
-        name="spread",
-    )(near1, far1, near0, far0, mid, loc1, loc0, keep, prefix, total)
+        name=f"spread{len(chunks)}",
+    )(*arrays)
 
 
 def local(previous, initial, rates, transitions):
@@ -531,15 +548,21 @@
     def send(code, hop):
         return lax.ppermute(code, "tm", [(i, i + hop) for i in range(blocks - hop)])
 
-    most, rest = tuple(range(1, rows)), (0,)
-    loc1, code1, part, first, keep, rhs = inner_rows(previous, inner, initial, rates, transitions)
-    near1, far1 = send(code1, 1), send(code1, 3)
-    loc0, code0, code = outer_row(outer, part, first, keep, rhs, code1)
-    mid, near0, far0 = send(code, 2), send(code0, 1), send(code0, 3)
+    most, half = tuple(range(1, rows)), rows - rows // 2
+    loc1, code1, tail, part, first, keep, rhs = inner_rows(
+        previous, inner, initial, rates, transitions
+    )
+    near1, far1, mid1 = send(code1, 1), send(code1, 3), send(tail, 2)
     prefix, total = products(transitions, steps)
-    chunks = (most, rest)
-    ready1 = ready(most, near1, far1, keep, total)
-    return spread(chunks, *ready1, near0, far0, mid, loc1, loc0, keep, prefix, total)
+    loc0, code0, code = outer_row(outer, part, first, keep, rhs, code1, total)
+    mid0, near0, far0 = send(code, 2), send(code0, 1), send(code0, 3)
+    near1, far1 = ready(most, near1, far1, keep, total)
+    later = (tuple((q - 1, q) for q in range(half, rows)),)
+    early = (tuple((q - 1, q) for q in range(1, half)), ((0, 0),))
+    out = spread(later, [near1], [far1], [loc1], mid1, keep, prefix, total)
+    return spread(
+        early, [near1, near0], [far1, far0], [loc1, loc0], mid0, keep, prefix, total, out
+    )
 
 
 def solution(mesh):

time: 46.8 us -> 47.5 us (1.015)
  the two profiles are of different devices: /device:TPU:14 before, /device:TPU:117 now
where the time goes in v5:
time: 47.5 us; the launch traced here: 47.2 us
  Pallas kernels  23.9 us (50%)
  starting transfers between devices  23 us (48%)
    ppermute x6, starting transfers between devices, send(): return lax.ppermute(code, 'tm', [(i, i + hop) for i in range(blocks - hop)])  17.6 us
    pallas_call x1, Pallas kernels, inner_rows(): pl.pallas_call(functools.partial(inner_kernel, steps, rows), out_shape=[p...  8.56 us
    pallas_call x2, Pallas kernels, spread(): pl.pallas_call(functools.partial(spread_kernel, chunks, rows), out_shape=...  6.78 us
    ppermute x1, starting transfers between devices, local(): lax.ppermute(outer_edge, 'space', between + [(j, i) for i, j in between])  4.66 us
    pallas_call x1, Pallas kernels, products(): pl.pallas_call(functools.partial(product_kernel, steps), out_shape=[pltpu...  3.17 us
    pallas_call x1, Pallas kernels, outer_row(): pl.pallas_call(functools.partial(outer_kernel, steps), out_shape=[pltpu.V...  2.53 us
    pallas_call x1, Pallas kernels, edges(): pl.pallas_call(functools.partial(edge_kernel, steps, rows), out_shape=[ja...  2.13 us
  transfers between devices with their start and end apart: 8, of which 0 were waited for; matrix products, arithmetic and copies ran while one was open for 0% of the time, Pallas kernels for 39%

profile of v5, /device:TPU:117, one launch (start us, length us, event | category | flops | bytes accessed | tf_op | source)
XLA Modules:
  0.0 47.2 jit_solution(14469515959902992045)
XLA Ops:
  0.0 2.1 %edges.1 = (bf16[16,256,128]{2,1,0:T(8,128)(2,1)S(1)}, bf16[16,256,128]{2,1,0:T(8,128)(2,1)S(1)}) custom-call(bf16[16,6,256,128]{3,2,1,0:T(8,128)(2,1)} %prev_ref.3, f32[6,256]{1,0:T(8,128)} %line_ref.3), custom_call_target="tpu_custom_call" | custom-call | tf_op jit(solution)/shard_map/edges/pallas_call | solution.py:147
  2.1 0.8 %collective-permute-start = (bf16[16,256,128]{2,1,0:T(8,128)(2,1)S(1)}, bf16[16,256,128]{2,1,0:T(8,128)(2,1)S(1)}, u32[]{:S(2)}, u32[]{:S(2)}) collective-permute-start(bf16[16,256,128]{2,1,0:T(8,128)(2,1)S(1)} %get-tuple-element.21), channel_id=1, source_target_pairs={{0,4},{8,12},{16,20},{24,28},{32,36},{40,44},{48,52},{56,60},{64,6... | collective-permute-start | bytes 3145736 | tf_op jit(solution)/shard_map/ppermute | solution.py:546
  2.9 4.7 %collective-permute-start.3 = (bf16[16,256,128]{2,1,0:T(8,128)(2,1)S(1)}, bf16[16,256,128]{2,1,0:T(8,128)(2,1)S(1)}, u32[]{:S(2)}, u32[]{:S(2)}) collective-permute-start(bf16[16,256,128]{2,1,0:T(8,128)(2,1)S(1)} %get-tuple-element.26), channel_id=1, source_target_pairs={{4,8},{12,16},{20,24},{28,32},{36,40},{44,48},{52,56},{60,64},{68,... | collective-permute-start | bytes 3145736 | tf_op jit(solution)/shard_map/ppermute | solution.py:545
  7.6 0.0 collective-permute-done.halo_ref
  7.6 8.6 %inner_rows.1 = (f32[16,5,256,128]{3,2,1,0:T(8,128)S(1)}, bf16[1296,128]{1,0:T(8,128)(2,1)S(1)}, bf16[784,128]{1,0:T(8,128)(2,1)S(1)}, f32[16,256,128]{2,1,0:T(8...) custom-call(bf16[16,6,256,128]{3,2,1,0:T(8,128)(2,1)} %prev_ref.3, ...), custom_call_target="tpu_custom_call" | custom-call | flops 3221225472 | bytes 6291456 | tf_op jit(solution)/shard_map/inner_rows/pallas_call | solution.py:268
  16.1 0.7 %collective-permute-start.2 = (bf16[1296,128]{1,0:T(8,128)(2,1)S(1)}, bf16[1296,128]{1,0:T(8,128)(2,1)S(1)}, u32[]{:S(2)}, u32[]{:S(2)}) collective-permute-start(bf16[1296,128]{1,0:T(8,128)(2,1)S(1)} %get-tuple-element.22.most_ref), channel_id=1, source_target_pairs={{0,3},{4,7},{8,11},{12,15},{16,19},{20,23},{24,27},{28,31},{32,35}... | collective-permute-start | bytes 995336 | tf_op jit(solution)/shard_map/ppermute | solution.py:549
  16.8 3.5 %collective-permute-start.1 = (bf16[1296,128]{1,0:T(8,128)(2,1)S(1)}, bf16[1296,128]{1,0:T(8,128)(2,1)S(1)}, u32[]{:S(2)}, u32[]{:S(2)}) collective-permute-start(bf16[1296,128]{1,0:T(8,128)(2,1)S(1)} %get-tuple-element.22.most_ref), channel_id=1, source_target_pairs={{0,1},{1,2},{2,3},{4,5},{5,6},{6,7},{8,9},{9,10},{10,11},{12,13},{... | collective-permute-start | bytes 995336 | tf_op jit(solution)/shard_map/ppermute | solution.py:549
  20.4 1.3 %collective-permute-start.7 = (bf16[784,128]{1,0:T(8,128)(2,1)S(1)}, bf16[784,128]{1,0:T(8,128)(2,1)S(1)}, u32[]{:S(2)}, u32[]{:S(2)}) collective-permute-start(bf16[784,128]{1,0:T(8,128)(2,1)S(1)} %get-tuple-element.36), channel_id=1, source_target_pairs={{0,2},{1,3},{4,6},{5,7},{8,10},{9,11},{12,14},{13,15},{16,18},{17,... | collective-permute-start | bytes 602120 | tf_op jit(solution)/shard_map/ppermute | solution.py:549
  21.7 3.2 %products.1 = (bf16[16,256,256]{2,1,0:T(8,128)(2,1)S(1)}, bf16[2,256,256]{2,1,0:T(8,128)(2,1)S(1)}) custom-call(f32[64,128,128]{2,1,0:T(8,128)} %trans_ref.3), custom_call_target="tpu_custom_call" | custom-call | flops 1000000000 | tf_op jit(solution)/shard_map/products/pallas_call | solution.py:386
  24.8 0.0 collective-permute-done.3.halo_ref
  24.9 2.5 %outer_row.1 = (f32[16,1,256,128]{3,2,1,0:T(8,128)S(1)}, bf16[272,128]{1,0:T(8,128)(2,1)S(1)}, bf16[800,128]{1,0:T(8,128)(2,1)S(1)}) custom-call(bf16[16,256,128]{2,1,0:T(8,128)(2,1)S(1)} %collective-permute-done.3.halo_ref, f32[16,256,128]{2,1,0:T(8,128)S(1)} %get-tuple-element.27.part_ref, f32[256,128]{1,0:T(8,128)S(1)} %get-tuple-element.28.first_ref, ...), custom_call_target="tpu_custom_call" | custom-call | tf_op jit(solution)/shard_map/outer_row/pallas_call | solution.py:336
  27.4 1.3 %collective-permute-start.6 = (bf16[800,128]{1,0:T(8,128)(2,1)S(1)}, bf16[800,128]{1,0:T(8,128)(2,1)S(1)}, u32[]{:S(2)}, u32[]{:S(2)}) collective-permute-start(bf16[800,128]{1,0:T(8,128)(2,1)S(1)} %get-tuple-element.34), channel_id=1, source_target_pairs={{0,2},{1,3},{4,6},{5,7},{8,10},{9,11},{12,14},{13,15},{16,18},{17,... | collective-permute-start | bytes 614408 | tf_op jit(solution)/shard_map/ppermute | solution.py:549
  28.7 0.7 %collective-permute-start.5 = (bf16[272,128]{1,0:T(8,128)(2,1)S(1)}, bf16[272,128]{1,0:T(8,128)(2,1)S(1)}, u32[]{:S(2)}, u32[]{:S(2)}) collective-permute-start(bf16[272,128]{1,0:T(8,128)(2,1)S(1)} %get-tuple-element.30), channel_id=1, source_target_pairs={{0,3},{4,7},{8,11},{12,15},{16,19},{20,23},{24,27},{28,31},{32,35}... | collective-permute-start | bytes 208904 | tf_op jit(solution)/shard_map/ppermute | solution.py:549
  29.4 0.0 collective-permute-done.2.far_code
  29.4 10.2 %collective-permute-start.4 = (bf16[272,128]{1,0:T(8,128)(2,1)S(1)}, bf16[272,128]{1,0:T(8,128)(2,1)S(1)}, u32[]{:S(2)}, u32[]{:S(2)}) collective-permute-start(bf16[272,128]{1,0:T(8,128)(2,1)S(1)} %get-tuple-element.30), channel_id=1, source_target_pairs={{0,1},{1,2},{2,3},{4,5},{5,6},{6,7},{8,9},{9,10},{10,11},{12,13},{... | collective-permute-start | bytes 208904 | tf_op jit(solution)/shard_map/ppermute | solution.py:549
  39.6 0.0 collective-permute-done.1.near_code
  39.6 0.8 %ready.1 = (f32[5,256,128]{2,1,0:T(8,128)S(1)}, f32[5,256,128]{2,1,0:T(8,128)S(1)}) custom-call(bf16[1296,128]{1,0:T(8,128)(2,1)S(1)} %collective-permute-done.1.near_code, bf16[1296,128]{1,0:T(8,128)(2,1)S(1)} %collective-permute-done.2.far_code, f32[6,256,128]{2,1,0:T(8,128)S(1)} %get-tuple-element.23.keep_ref.refs_4_.refs_7_, ...), custom_call_target="tpu_custom_call" | custom-call | flops 1000000000 | bytes 2000000 | tf_op jit(solution)/shard_map/ready/pallas_call | solution.py:439
  40.4 0.0 collective-permute-done.7.refs_3_
  40.4 3.3 %spread1.1.refs_10_ = bf16[16,6,256,128]{3,2,1,0:T(8,128)(2,1)} custom-call(f32[5,256,128]{2,1,0:T(8,128)S(1)} %get-tuple-element.25.refs_0_, f32[5,256,128]{2,1,0:T(8,128)S(1)} %get-tuple-element.31.refs_1_.refs_2_, f32[16,5,256,128]{3,2,1,0:T(8,128)S(1)} %get-tuple-element.32.refs_2_.refs_4_, bf16[784,128]{1,0:T(8,128)(2,1)S(1)} %collective-permute-done.7.refs_3_, ...), custom_call_target="tpu_custom_call" | custom-call | flops 1000000000 | bytes 2000000 | tf_op jit(solution)/shard_map/spread1/pallas_call | solution.py:516
  43.7 0.0 collective-permute-done.5.refs_3_
  43.7 0.0 collective-permute-done.4.refs_1_
  43.7 0.0 collective-permute-done.6.refs_6_
  43.7 3.5 %spread2.1 = bf16[16,6,256,128]{3,2,1,0:T(8,128)(2,1)} custom-call(f32[5,256,128]{2,1,0:T(8,128)S(1)} %get-tuple-element.25.refs_0_, bf16[272,128]{1,0:T(8,128)(2,1)S(1)} %collective-permute-done.4.refs_1_, f32[5,256,128]{2,1,0:T(8,128)S(1)} %get-tuple-element.31.refs_1_.refs_2_, ...), custom_call_target="tpu_custom_call", output_to_operand_aliasing={{}: (10, {})} | custom-call | flops 1000000000 | bytes 2000000 | tf_op jit(solution)/shard_map/spread2/pallas_call | solution.py:516
Async XLA Ops:
  2.1 5.4 %collective-permute-start = (bf16[16,256,128]{2,1,0:T(8,128)(2,1)S(1)}, bf16[16,256,128]{2,1,0:T(8,128)(2,1)S(1)}, u32[]{:S(2)}, u32[]{:S(2)}) collective-permute-start(bf16[16,256,128]{2,1,0:T(8,128)(2,1)S(1)} %get-tuple-element.21), channel_id=1, source_target_pairs={{0,4},{8,12},{16,20},{24,28},{32,36},{40,44},{48,52},{56,60},{64,6... | collective-permute-start | bytes 3145736 | tf_op jit(solution)/shard_map/ppermute | solution.py:546
  2.9 21.9 %collective-permute-start.3 = (bf16[16,256,128]{2,1,0:T(8,128)(2,1)S(1)}, bf16[16,256,128]{2,1,0:T(8,128)(2,1)S(1)}, u32[]{:S(2)}, u32[]{:S(2)}) collective-permute-start(bf16[16,256,128]{2,1,0:T(8,128)(2,1)S(1)} %get-tuple-element.26), channel_id=1, source_target_pairs={{4,8},{12,16},{20,24},{28,32},{36,40},{44,48},{52,56},{60,64},{68,... | collective-permute-start | bytes 3145736 | tf_op jit(solution)/shard_map/ppermute | solution.py:545
  16.1 13.2 %collective-permute-start.2 = (bf16[1296,128]{1,0:T(8,128)(2,1)S(1)}, bf16[1296,128]{1,0:T(8,128)(2,1)S(1)}, u32[]{:S(2)}, u32[]{:S(2)}) collective-permute-start(bf16[1296,128]{1,0:T(8,128)(2,1)S(1)} %get-tuple-element.22.most_ref), channel_id=1, source_target_pairs={{0,3},{4,7},{8,11},{12,15},{16,19},{20,23},{24,27},{28,31},{32,35}... | collective-permute-start | bytes 995336 | tf_op jit(solution)/shard_map/ppermute | solution.py:549
  16.8 22.7 %collective-permute-start.1 = (bf16[1296,128]{1,0:T(8,128)(2,1)S(1)}, bf16[1296,128]{1,0:T(8,128)(2,1)S(1)}, u32[]{:S(2)}, u32[]{:S(2)}) collective-permute-start(bf16[1296,128]{1,0:T(8,128)(2,1)S(1)} %get-tuple-element.22.most_ref), channel_id=1, source_target_pairs={{0,1},{1,2},{2,3},{4,5},{5,6},{6,7},{8,9},{9,10},{10,11},{12,13},{... | collective-permute-start | bytes 995336 | tf_op jit(solution)/shard_map/ppermute | solution.py:549
  20.4 20.0 %collective-permute-start.7 = (bf16[784,128]{1,0:T(8,128)(2,1)S(1)}, bf16[784,128]{1,0:T(8,128)(2,1)S(1)}, u32[]{:S(2)}, u32[]{:S(2)}) collective-permute-start(bf16[784,128]{1,0:T(8,128)(2,1)S(1)} %get-tuple-element.36), channel_id=1, source_target_pairs={{0,2},{1,3},{4,6},{5,7},{8,10},{9,11},{12,14},{13,15},{16,18},{17,... | collective-permute-start | bytes 602120 | tf_op jit(solution)/shard_map/ppermute | solution.py:549
  27.4 16.3 %collective-permute-start.6 = (bf16[800,128]{1,0:T(8,128)(2,1)S(1)}, bf16[800,128]{1,0:T(8,128)(2,1)S(1)}, u32[]{:S(2)}, u32[]{:S(2)}) collective-permute-start(bf16[800,128]{1,0:T(8,128)(2,1)S(1)} %get-tuple-element.34), channel_id=1, source_target_pairs={{0,2},{1,3},{4,6},{5,7},{8,10},{9,11},{12,14},{13,15},{16,18},{17,... | collective-permute-start | bytes 614408 | tf_op jit(solution)/shard_map/ppermute | solution.py:549
  28.7 15.0 %collective-permute-start.5 = (bf16[272,128]{1,0:T(8,128)(2,1)S(1)}, bf16[272,128]{1,0:T(8,128)(2,1)S(1)}, u32[]{:S(2)}, u32[]{:S(2)}) collective-permute-start(bf16[272,128]{1,0:T(8,128)(2,1)S(1)} %get-tuple-element.30), channel_id=1, source_target_pairs={{0,3},{4,7},{8,11},{12,15},{16,19},{20,23},{24,27},{28,31},{32,35}... | collective-permute-start | bytes 208904 | tf_op jit(solution)/shard_map/ppermute | solution.py:549
  29.4 14.3 %collective-permute-start.4 = (bf16[272,128]{1,0:T(8,128)(2,1)S(1)}, bf16[272,128]{1,0:T(8,128)(2,1)S(1)}, u32[]{:S(2)}, u32[]{:S(2)}) collective-permute-start(bf16[272,128]{1,0:T(8,128)(2,1)S(1)} %get-tuple-element.30), channel_id=1, source_target_pairs={{0,1},{1,2},{2,3},{4,5},{5,6},{6,7},{8,9},{9,10},{10,11},{12,13},{... | collective-permute-start | bytes 208904 | tf_op jit(solution)/shard_map/ppermute | solution.py:549

commit v6 on v3

--- a/solution.py
+++ b/solution.py
@@ -163,7 +163,7 @@
 
 def inner_kernel(
     steps, rows,
-    prev_ref, halo_ref, init_ref, line_ref, trans_ref,
+    prev_ref, init_ref, line_ref, trans_ref,
     loc_ref, code_ref, part_ref, first_ref, keep_ref, rhs_ref,
     pbuf, ibuf, tbuf, even, odds, weight, state, rates_ref, psem, isem, tsem, rsem,
 ):
@@ -189,7 +189,7 @@
         keep_ref[q] = 1.0 - share
     grids = (even, odds)
     for grid in grids:
-        for i in range(rows + 1):
+        for i in range(rows):
             grid[i, 0:8] = jnp.zeros((8, bins), F32)
             grid[i, columns + 8 :] = jnp.zeros((8, bins), F32)
     for t in range(1, steps):
@@ -201,22 +201,19 @@
     for q in range(rows):
         value = ibuf[place(q, rows, odd)]
         value = jnp.where(block == 0, value, jnp.zeros_like(value))
-        if q == 0:
-            first_ref[...] = value
+        if q in (0, rows - 1):
+            first_ref[min(q, 1)] = value
         else:
             state[q - 1] = value
 
-    pieces = [(q, c) for q in range(1, rows) for c in range(0, columns, CHUNK)]
-
-    units = [(q, c) for q in range(rows + 1) for c in range(0, columns, CHUNK)]
+    pieces = [(q, c) for q in range(1, rows - 1) for c in range(0, columns, CHUNK)]
+
+    units = [(q, c) for q in range(rows) for c in range(0, columns, CHUNK)]
 
     def fill(t, unit, slot):
         q, c = unit
-        if q == rows:
-            value = halo_ref[t, c : c + CHUNK].astype(F32)
-        else:
-            value = pbuf[t, place(q, rows, odd), c : c + CHUNK].astype(F32)
-            value = (value * weight[q, c : c + CHUNK]).astype(BF16).astype(F32)
+        value = pbuf[t, place(q, rows, odd), c : c + CHUNK].astype(F32)
+        value = (value * weight[q, c : c + CHUNK]).astype(BF16).astype(F32)
         grids[slot][q, 8 + c : 8 + c + CHUNK] = value
 
     def sides(grid, q, c):
@@ -235,10 +232,12 @@
         loc_ref[t, q - 1, c : c + CHUNK] = value
 
     def beside(t, i, slot):
-        if i % rows == 0 and i // rows < columns // CHUNK:
-            c = i // rows * CHUNK
-            grid = grids[slot]
-            part_ref[t, c : c + CHUNK] = grid[1, 8 + c : 8 + c + CHUNK] + sides(grid, 0, c)
+        every = rows - 2
+        if i % every == 0:
+            c = i // every * CHUNK
+            grid, inside = grids[slot], slice(8 + c, 8 + c + CHUNK)
+            part_ref[t, 0, c : c + CHUNK] = grid[1, inside] + sides(grid, 0, c)
+            part_ref[t, 1, c : c + CHUNK] = grid[rows - 2, inside] + sides(grid, rows - 1, c)
         if isinstance(t, int) and t == steps - 1:
             return
         if i == 0:
@@ -256,7 +255,7 @@
     finish(loc_ref, code_ref, steps)
 
 
-def inner_rows(previous, halo, initial, rates, transitions):
+def inner_rows(previous, initial, rates, transitions):
     steps, rows, columns, bins = previous.shape
     anywhere = pl.BlockSpec(memory_space=pl.ANY)
     vmem = pl.BlockSpec(memory_space=pltpu.VMEM)
@@ -267,23 +266,23 @@
     return pl.pallas_call(
         functools.partial(inner_kernel, steps, rows),
         out_shape=[
-            pltpu.VMEM((steps, rows - 1, columns, bins), F32),
-            jax.ShapeDtypeStruct(((rows - 1) * columns + 16, bins), BF16),
-            pltpu.VMEM((steps, columns, bins), F32),
-            pltpu.VMEM((columns, bins), F32),
+            pltpu.VMEM((steps, rows - 2, columns, bins), F32),
+            jax.ShapeDtypeStruct(((rows - 2) * columns + 16, bins), BF16),
+            pltpu.VMEM((steps, 2, columns, bins), F32),
+            pltpu.VMEM((2, columns, bins), F32),
             pltpu.VMEM((rows, columns, bins), F32),
             pltpu.VMEM((steps, 2 * bins, 2 * bins), BF16),
         ],
-        in_specs=[anywhere, vmem, anywhere, anywhere, anywhere],
+        in_specs=[anywhere] * 4,
         out_specs=[vmem] * 6,
         scratch_shapes=[
             pltpu.VMEM((steps, rows, columns, bins), BF16),
             pltpu.VMEM((rows, columns, bins), F32),
             pltpu.VMEM((steps, bins, bins), F32),
-            pltpu.VMEM((rows + 1, columns + 16, bins), F32),
-            pltpu.VMEM((rows + 1, columns + 16, bins), F32),
+            pltpu.VMEM((rows, columns + 16, bins), F32),
+            pltpu.VMEM((rows, columns + 16, bins), F32),
             pltpu.VMEM((rows, columns, bins), F32),
-            pltpu.VMEM((rows - 1, columns, bins), F32),
+            pltpu.VMEM((rows - 2, columns, bins), F32),
             pltpu.VMEM((rows, columns), F32),
             pltpu.SemaphoreType.DMA((steps,)),
             pltpu.SemaphoreType.DMA,
@@ -297,52 +296,47 @@
             transcendentals=0,
         ),
         name="inner_rows",
-    )(previous, halo, initial, rates, transitions)
+    )(previous, initial, rates, transitions)
 
 
 def outer_kernel(
-    steps, halo_ref, part_ref, first_ref, keep_ref, rhs_ref, most_ref, loc_ref, code_ref, all_ref, state, sem
+    steps, outer_ref, inner_ref, part_ref, first_ref, keep_ref, rhs_ref, after_ref, loc_ref, code_ref, state
 ):
-    columns = first_ref.shape[0]
-    joined = most_ref.shape[0]
-    copy = pltpu.make_async_copy(most_ref, all_ref.at[pl.ds(0, joined)], sem)
-    copy.start()
+    columns = first_ref.shape[1]
+    last = keep_ref.shape[0] - 1
     state[...] = first_ref[...]
+    pieces = [(k, slice(c, c + CHUNK)) for c in range(0, columns, CHUNK) for k in range(2)]
 
     def left_of(t, i, _):
-        cells = slice(i * CHUNK, (i + 1) * CHUNK)
-        inflow = part_ref[t, cells] + halo_ref[t, cells].astype(F32)
-        return left(keep_ref[0, cells] * state[cells] + inflow)
+        k, cells = pieces[i]
+        inflow = part_ref[t, k, cells] + (outer_ref, inner_ref)[k][t, cells].astype(F32)
+        return left(keep_ref[k * last, cells] * state[k, cells] + inflow)
 
     def store(t, i, both):
-        cells = slice(i * CHUNK, (i + 1) * CHUNK)
-        state[cells] = loc_ref[t, 0, cells] = halves(both)
-
-    stream(steps, columns // CHUNK, lambda t: rhs_ref[t], left_of, store)
+        state[pieces[i]] = loc_ref[(t, *pieces[i])] = halves(both)
+
+    stream(steps, len(pieces), lambda t: rhs_ref[t], left_of, store)
     finish(loc_ref, code_ref, steps)
-    all_ref[joined:] = code_ref[...]
-    copy.wait()
-
-
-def outer_row(halo, part, first, keep, rhs, most):
-    steps, columns, bins = part.shape
+
+
+def outer_rows(outer, inner, part, first, keep, rhs, after):
+    steps, two, columns, bins = part.shape
     vmem = pl.BlockSpec(memory_space=pltpu.VMEM)
     return pl.pallas_call(
         functools.partial(outer_kernel, steps),
         out_shape=[
-            pltpu.VMEM((steps, 1, columns, bins), F32),
-            jax.ShapeDtypeStruct((columns + 16, bins), BF16),
-            jax.ShapeDtypeStruct((most.shape[0] + columns + 16, bins), BF16),
-        ],
-        in_specs=[vmem] * 6,
-        out_specs=[vmem] * 3,
-        scratch_shapes=[pltpu.VMEM((columns, bins), F32), pltpu.SemaphoreType.DMA],
+            pltpu.VMEM((steps, two, columns, bins), F32),
+            jax.ShapeDtypeStruct((two * columns + 16, bins), BF16),
+        ],
+        in_specs=[vmem] * 6 + [pl.BlockSpec(memory_space=pl.ANY)],
+        out_specs=[vmem] * 2,
+        scratch_shapes=[pltpu.VMEM((two, columns, bins), F32)],
         compiler_params=pltpu.CompilerParams(vmem_limit_bytes=4 * MIB),
         cost_estimate=pl.CostEstimate(
             flops=0, bytes_accessed=0, transcendentals=0
         ),
-        name="outer_row",
-    )(halo, part, first, keep, rhs, most)
+        name="outer_rows",
+    )(outer, inner, part, first, keep, rhs, after)
 
 
 def product_kernel(steps, trans_ref, prefix_ref, total_ref, work, sems):
@@ -391,7 +385,7 @@
         ],
         compiler_params=pltpu.CompilerParams(vmem_limit_bytes=16 * MIB),
         cost_estimate=pl.CostEstimate(
-            flops=0, bytes_accessed=0, transcendentals=0
+            flops=1000000000, bytes_accessed=0, transcendentals=0
         ),
         name="products",
     )(transitions)
@@ -437,7 +431,7 @@
         out_specs=[vmem] * 2,
         compiler_params=pltpu.CompilerParams(vmem_limit_bytes=4 * MIB),
         cost_estimate=pl.CostEstimate(
-            flops=4_000_000_000, bytes_accessed=8_000_000, transcendentals=0
+            flops=1000000000, bytes_accessed=2000000, transcendentals=0
         ),
         name="ready",
     )(near, far, keep, total)
@@ -445,20 +439,19 @@
 
 def spread_kernel(
     chunks, rows,
-    near1_ref, far1_ref, near0_code, far0_code, mid_ref, loc1_ref, loc0_ref, keep_ref, prefix_ref, total_ref,
+    near1_ref, far1_ref, near0_code, far0_code, mid1_ref, mid0_ref, loc1_ref, loc0_ref, keep_ref, prefix_ref, total_ref,
     out_ref,
     entering, power, near0_ref, far0_ref, stage, sems,
 ):
     odd = lax.rem(lax.axis_index("space"), 2)
     steps, _, columns, bins = stage.shape
     locs = (loc1_ref, loc0_ref)
-    pieces, at, scales = [], 0, []
+    mids = (mid1_ref, mid0_ref)
+    pieces, scales = [], []
     for k, calc in enumerate(chunks):
         for n, q in enumerate(calc):
-            pieces += [(k, n, q, c, at + c) for c in range(0, columns, CHUNK)]
-            at += columns
-        scales.append(scale_of(mid_ref, at))
-        at += 16
+            pieces += [(k, n, q, c, n * columns + c) for c in range(0, columns, CHUNK)]
+        scales.append(scale_of(mids[k], len(calc) * columns))
     count = len(pieces)
     nears, fars = (near1_ref, near0_ref), (far1_ref, far0_ref)
     ready_kernel(chunks[1], near0_code, far0_code, keep_ref, total_ref, near0_ref, far0_ref)
@@ -468,7 +461,7 @@
 
     def left_mid(_, i, slot):
         k, n, q, c, at = pieces[i]
-        return left(decode(mid_ref[at : at + CHUNK], scales[k]) + fars[k][n, c : c + CHUNK])
+        return left(decode(mids[k][at : at + CHUNK], scales[k]) + fars[k][n, c : c + CHUNK])
 
     def store_mid(_, i, both):
         k, n, _, c, _ = pieces[i]
@@ -492,20 +485,20 @@
         pltpu.make_async_copy(stage.at[t], out_ref.at[t], sems.at[t]).wait()
 
 
-def spread(chunks, near1, far1, near0, far0, mid, loc1, loc0, keep, prefix, total):
+def spread(chunks, near1, far1, near0, far0, mid1, mid0, loc1, loc0, keep, prefix, total):
     steps, _, columns, bins = loc1.shape
     rows = keep.shape[0]
     vmem = pl.BlockSpec(memory_space=pltpu.VMEM)
     return pl.pallas_call(
         functools.partial(spread_kernel, chunks, rows),
         out_shape=jax.ShapeDtypeStruct((steps, rows, columns, bins), BF16),
-        in_specs=[vmem] * 10,
+        in_specs=[vmem] * 11,
         out_specs=pl.BlockSpec(memory_space=pl.ANY),
         scratch_shapes=[
             pltpu.VMEM((rows, columns, 2 * bins), BF16),
             pltpu.VMEM((rows, columns, bins), F32),
-            pltpu.VMEM((1, columns, bins), F32),
-            pltpu.VMEM((1, columns, bins), F32),
+            pltpu.VMEM((2, columns, bins), F32),
+            pltpu.VMEM((2, columns, bins), F32),
             pltpu.VMEM((steps, rows, columns, bins), BF16),
             pltpu.SemaphoreType.DMA((steps,)),
         ],
@@ -516,7 +509,7 @@
             transcendentals=0,
         ),
         name="spread",
-    )(near1, far1, near0, far0, mid, loc1, loc0, keep, prefix, total)
+    )(near1, far1, near0, far0, mid1, mid0, loc1, loc0, keep, prefix, total)
 
 
 def local(previous, initial, rates, transitions):
@@ -531,15 +524,16 @@
     def send(code, hop):
         return lax.ppermute(code, "tm", [(i, i + hop) for i in range(blocks - hop)])
 
-    most, rest = tuple(range(1, rows)), (0,)
-    loc1, code1, part, first, keep, rhs = inner_rows(previous, inner, initial, rates, transitions)
-    near1, far1 = send(code1, 1), send(code1, 3)
-    loc0, code0, code = outer_row(outer, part, first, keep, rhs, code1)
-    mid, near0, far0 = send(code, 2), send(code0, 1), send(code0, 3)
+    most, rest = tuple(range(1, rows - 1)), (0, rows - 1)
+    loc1, code1, part, first, keep, rhs = inner_rows(previous, initial, rates, transitions)
+    near1, far1, mid1 = send(code1, 1), send(code1, 3), send(code1, 2)
     prefix, total = products(transitions, steps)
-    chunks = (most, rest)
+    loc0, code0 = outer_rows(outer, inner, part, first, keep, rhs, code1)
+    near0, far0, mid0 = send(code0, 1), send(code0, 3), send(code0, 2)
     ready1 = ready(most, near1, far1, keep, total)
-    return spread(chunks, *ready1, near0, far0, mid, loc1, loc0, keep, prefix, total)
+    return spread(
+        (most, rest), *ready1, near0, far0, mid1, mid0, loc1, loc0, keep, prefix, total
+    )
 
 
 def solution(mesh):

time: 46.8 us -> 50.9 us (1.088)
  the two profiles are of different devices: /device:TPU:14 before, /device:TPU:6 now
where the time goes in v6:
time: 50.9 us; the launch traced here: 50.6 us
  starting transfers between devices  26.2 us (51%)
  Pallas kernels  24.2 us (48%)
    ppermute x6, starting transfers between devices, send(): return lax.ppermute(code, 'tm', [(i, i + hop) for i in range(blocks - hop)])  18.6 us
    pallas_call x1, Pallas kernels, inner_rows(): pl.pallas_call(functools.partial(inner_kernel, steps, rows), out_shape=[p...  8.77 us
    ppermute x1, starting transfers between devices, local(): lax.ppermute(outer_edge, 'space', between + [(j, i) for i, j in between])  7.47 us
    pallas_call x1, Pallas kernels, spread(): pl.pallas_call(functools.partial(spread_kernel, chunks, rows), out_shape=...  6.73 us
    pallas_call x1, Pallas kernels, products(): pl.pallas_call(functools.partial(product_kernel, steps), out_shape=[pltpu...  3.54 us
    pallas_call x1, Pallas kernels, outer_rows(): pl.pallas_call(functools.partial(outer_kernel, steps), out_shape=[pltpu.V...  2.42 us
    pallas_call x1, Pallas kernels, edges(): pl.pallas_call(functools.partial(edge_kernel, steps, rows), out_shape=[ja...  2.13 us
  transfers between devices with their start and end apart: 8, of which 0 were waited for; matrix products, arithmetic and copies ran while one was open for 0% of the time, Pallas kernels for 30%

profile of v6, /device:TPU:6, one launch (start us, length us, event | category | flops | bytes accessed | tf_op | source)
XLA Modules:
  0.0 50.6 jit_solution(2787328751567751432)
XLA Ops:
  0.0 2.1 %edges.1 = (bf16[16,256,128]{2,1,0:T(8,128)(2,1)S(1)}, bf16[16,256,128]{2,1,0:T(8,128)(2,1)S(1)}) custom-call(bf16[16,6,256,128]{3,2,1,0:T(8,128)(2,1)} %prev_ref.3, f32[6,256]{1,0:T(8,128)} %line_ref.3), custom_call_target="tpu_custom_call" | custom-call | tf_op jit(solution)/shard_map/edges/pallas_call | solution.py:147
  2.1 7.5 %collective-permute-start.2 = (bf16[16,256,128]{2,1,0:T(8,128)(2,1)S(1)}, bf16[16,256,128]{2,1,0:T(8,128)(2,1)S(1)}, u32[]{:S(2)}, u32[]{:S(2)}) collective-permute-start(bf16[16,256,128]{2,1,0:T(8,128)(2,1)S(1)} %get-tuple-element.24), channel_id=1, source_target_pairs={{4,8},{12,16},{20,24},{28,32},{36,40},{44,48},{52,56},{60,64},{68,... | collective-permute-start | bytes 3145736 | tf_op jit(solution)/shard_map/ppermute | solution.py:521
  9.6 0.1 collective-permute-start.3
  9.7 8.8 %inner_rows.1 = (f32[16,4,256,128]{3,2,1,0:T(8,128)S(1)}, bf16[1040,128]{1,0:T(8,128)(2,1)S(1)}, f32[16,2,256,128]{3,2,1,0:T(8,128)S(1)}, f32[2,256,128]{2,1,0:T...) custom-call(bf16[16,6,256,128]{3,2,1,0:T(8,128)(2,1)} %prev_ref.3, f32[6,256,128]{2,1,0:T(8,128)} %init_ref.1, ...), custom_call_target="tpu_custom_call" | custom-call | flops 3221225472 | bytes 6291456 | tf_op jit(solution)/shard_map/inner_rows/pallas_call | solution.py:266
  18.5 3.5 %collective-permute-start = (bf16[1040,128]{1,0:T(8,128)(2,1)S(1)}, bf16[1040,128]{1,0:T(8,128)(2,1)S(1)}, u32[]{:S(2)}, u32[]{:S(2)}) collective-permute-start(bf16[1040,128]{1,0:T(8,128)(2,1)S(1)} %get-tuple-element.19.after_ref), channel_id=1, source_target_pairs={{0,1},{1,2},{2,3},{4,5},{5,6},{6,7},{8,9},{9,10},{10,11},{12,13},{... | collective-permute-start | bytes 798728 | tf_op jit(solution)/shard_map/ppermute | solution.py:525
  22.0 2.7 %collective-permute-start.1 = (bf16[1040,128]{1,0:T(8,128)(2,1)S(1)}, bf16[1040,128]{1,0:T(8,128)(2,1)S(1)}, u32[]{:S(2)}, u32[]{:S(2)}) collective-permute-start(bf16[1040,128]{1,0:T(8,128)(2,1)S(1)} %get-tuple-element.19.after_ref), channel_id=1, source_target_pairs={{0,3},{4,7},{8,11},{12,15},{16,19},{20,23},{24,27},{28,31},{32,35}... | collective-permute-start | bytes 798728 | tf_op jit(solution)/shard_map/ppermute | solution.py:525
  24.7 2.8 %collective-permute-start.6 = (bf16[1040,128]{1,0:T(8,128)(2,1)S(1)}, bf16[1040,128]{1,0:T(8,128)(2,1)S(1)}, u32[]{:S(2)}, u32[]{:S(2)}) collective-permute-start(bf16[1040,128]{1,0:T(8,128)(2,1)S(1)} %get-tuple-element.19.after_ref), channel_id=1, source_target_pairs={{0,2},{1,3},{4,6},{5,7},{8,10},{9,11},{12,14},{13,15},{16,18},{17,... | collective-permute-start | bytes 798728 | tf_op jit(solution)/shard_map/ppermute | solution.py:525
  27.5 0.0 collective-permute-done.2.outer_ref
  27.5 0.0 collective-permute-done.3.inner_ref
  27.5 2.4 %outer_rows.1 = (f32[16,2,256,128]{3,2,1,0:T(8,128)S(1)}, bf16[528,128]{1,0:T(8,128)(2,1)S(1)}) custom-call(bf16[16,256,128]{2,1,0:T(8,128)(2,1)S(1)} %collective-permute-done.2.outer_ref, bf16[16,256,128]{2,1,0:T(8,128)(2,1)S(1)} %collective-permute-done.3.inner_ref, f32[16,2,256,128]{3,2,1,0:T(8,128)S(1)} %get-tuple-element.26.part_ref, ...), custom_call_target="tpu_custom_call" | custom-call | tf_op jit(solution)/shard_map/outer_rows/pallas_call | solution.py:325
  30.0 1.3 %collective-permute-start.4 = (bf16[528,128]{1,0:T(8,128)(2,1)S(1)}, bf16[528,128]{1,0:T(8,128)(2,1)S(1)}, u32[]{:S(2)}, u32[]{:S(2)}) collective-permute-start(bf16[528,128]{1,0:T(8,128)(2,1)S(1)} %get-tuple-element.29), channel_id=1, source_target_pairs={{0,1},{1,2},{2,3},{4,5},{5,6},{6,7},{8,9},{9,10},{10,11},{12,13},{... | collective-permute-start | bytes 405512 | tf_op jit(solution)/shard_map/ppermute | solution.py:525
  31.3 1.3 %collective-permute-start.5 = (bf16[528,128]{1,0:T(8,128)(2,1)S(1)}, bf16[528,128]{1,0:T(8,128)(2,1)S(1)}, u32[]{:S(2)}, u32[]{:S(2)}) collective-permute-start(bf16[528,128]{1,0:T(8,128)(2,1)S(1)} %get-tuple-element.29), channel_id=1, source_target_pairs={{0,3},{4,7},{8,11},{12,15},{16,19},{20,23},{24,27},{28,31},{32,35}... | collective-permute-start | bytes 405512 | tf_op jit(solution)/shard_map/ppermute | solution.py:525
  32.6 0.0 collective-permute-done.near_code
  32.6 7.0 %collective-permute-start.7 = (bf16[528,128]{1,0:T(8,128)(2,1)S(1)}, bf16[528,128]{1,0:T(8,128)(2,1)S(1)}, u32[]{:S(2)}, u32[]{:S(2)}) collective-permute-start(bf16[528,128]{1,0:T(8,128)(2,1)S(1)} %get-tuple-element.29), channel_id=1, source_target_pairs={{0,2},{1,3},{4,6},{5,7},{8,10},{9,11},{12,14},{13,15},{16,18},{17,... | collective-permute-start | bytes 405512 | tf_op jit(solution)/shard_map/ppermute | solution.py:525
  39.6 3.5 %products.1 = (bf16[16,256,256]{2,1,0:T(8,128)(2,1)S(1)}, bf16[2,256,256]{2,1,0:T(8,128)(2,1)S(1)}) custom-call(f32[64,128,128]{2,1,0:T(8,128)} %trans_ref.3), custom_call_target="tpu_custom_call" | custom-call | flops 1000000000 | tf_op jit(solution)/shard_map/products/pallas_call | solution.py:374
  43.2 0.0 collective-permute-done.1.far_code
  43.2 0.6 %ready.1 = (f32[4,256,128]{2,1,0:T(8,128)S(1)}, f32[4,256,128]{2,1,0:T(8,128)S(1)}) custom-call(bf16[1040,128]{1,0:T(8,128)(2,1)S(1)} %collective-permute-done.near_code, bf16[1040,128]{1,0:T(8,128)(2,1)S(1)} %collective-permute-done.1.far_code, f32[6,256,128]{2,1,0:T(8,128)S(1)} %get-tuple-element.20.keep_ref, ...), custom_call_target="tpu_custom_call" | custom-call | flops 1000000000 | bytes 2000000 | tf_op jit(solution)/shard_map/ready/pallas_call | solution.py:427
  43.8 0.0 collective-permute-done.6.mid1_ref
  43.8 0.0 collective-permute-done.4.near0_code
  43.9 0.0 collective-permute-done.5.far0_code
  43.9 0.0 collective-permute-done.7.mid0_ref
  43.9 6.7 %spread.1 = bf16[16,6,256,128]{3,2,1,0:T(8,128)(2,1)} custom-call(f32[4,256,128]{2,1,0:T(8,128)S(1)} %get-tuple-element.22.near1_ref, f32[4,256,128]{2,1,0:T(8,128)S(1)} %get-tuple-element.23.far1_ref, bf16[528,128]{1,0:T(8,128)(2,1)S(1)} %collective-permute-done.4.near0_code, bf16[528,128]{1,0:T(8,128)(2,1)S(1)} %collective-permute-done.5.far0_code, ...), custom_call_target="tpu_custom_call" | custom-call | flops 3221225472 | bytes 6291456 | tf_op jit(solution)/shard_map/spread/pallas_call | solution.py:492
Async XLA Ops:
  2.1 25.4 %collective-permute-start.2 = (bf16[16,256,128]{2,1,0:T(8,128)(2,1)S(1)}, bf16[16,256,128]{2,1,0:T(8,128)(2,1)S(1)}, u32[]{:S(2)}, u32[]{:S(2)}) collective-permute-start(bf16[16,256,128]{2,1,0:T(8,128)(2,1)S(1)} %get-tuple-element.24), channel_id=1, source_target_pairs={{4,8},{12,16},{20,24},{28,32},{36,40},{44,48},{52,56},{60,64},{68,... | collective-permute-start | bytes 3145736 | tf_op jit(solution)/shard_map/ppermute | solution.py:521
  9.6 17.9 %collective-permute-start.3 = (bf16[16,256,128]{2,1,0:T(8,128)(2,1)S(1)}, bf16[16,256,128]{2,1,0:T(8,128)(2,1)S(1)}, u32[]{:S(2)}, u32[]{:S(2)}) collective-permute-start(bf16[16,256,128]{2,1,0:T(8,128)(2,1)S(1)} %get-tuple-element.25), channel_id=1, source_target_pairs={{0,4},{8,12},{16,20},{24,28},{32,36},{40,44},{48,52},{56,60},{64,6... | collective-permute-start | bytes 3145736 | tf_op jit(solution)/shard_map/ppermute | solution.py:522
  18.5 14.1 %collective-permute-start = (bf16[1040,128]{1,0:T(8,128)(2,1)S(1)}, bf16[1040,128]{1,0:T(8,128)(2,1)S(1)}, u32[]{:S(2)}, u32[]{:S(2)}) collective-permute-start(bf16[1040,128]{1,0:T(8,128)(2,1)S(1)} %get-tuple-element.19.after_ref), channel_id=1, source_target_pairs={{0,1},{1,2},{2,3},{4,5},{5,6},{6,7},{8,9},{9,10},{10,11},{12,13},{... | collective-permute-start | bytes 798728 | tf_op jit(solution)/shard_map/ppermute | solution.py:525
  22.0 21.2 %collective-permute-start.1 = (bf16[1040,128]{1,0:T(8,128)(2,1)S(1)}, bf16[1040,128]{1,0:T(8,128)(2,1)S(1)}, u32[]{:S(2)}, u32[]{:S(2)}) collective-permute-start(bf16[1040,128]{1,0:T(8,128)(2,1)S(1)} %get-tuple-element.19.after_ref), channel_id=1, source_target_pairs={{0,3},{4,7},{8,11},{12,15},{16,19},{20,23},{24,27},{28,31},{32,35}... | collective-permute-start | bytes 798728 | tf_op jit(solution)/shard_map/ppermute | solution.py:525
  24.7 19.1 %collective-permute-start.6 = (bf16[1040,128]{1,0:T(8,128)(2,1)S(1)}, bf16[1040,128]{1,0:T(8,128)(2,1)S(1)}, u32[]{:S(2)}, u32[]{:S(2)}) collective-permute-start(bf16[1040,128]{1,0:T(8,128)(2,1)S(1)} %get-tuple-element.19.after_ref), channel_id=1, source_target_pairs={{0,2},{1,3},{4,6},{5,7},{8,10},{9,11},{12,14},{13,15},{16,18},{17,... | collective-permute-start | bytes 798728 | tf_op jit(solution)/shard_map/ppermute | solution.py:525
  30.0 13.9 %collective-permute-start.4 = (bf16[528,128]{1,0:T(8,128)(2,1)S(1)}, bf16[528,128]{1,0:T(8,128)(2,1)S(1)}, u32[]{:S(2)}, u32[]{:S(2)}) collective-permute-start(bf16[528,128]{1,0:T(8,128)(2,1)S(1)} %get-tuple-element.29), channel_id=1, source_target_pairs={{0,1},{1,2},{2,3},{4,5},{5,6},{6,7},{8,9},{9,10},{10,11},{12,13},{... | collective-permute-start | bytes 405512 | tf_op jit(solution)/shard_map/ppermute | solution.py:525
  31.3 12.6 %collective-permute-start.5 = (bf16[528,128]{1,0:T(8,128)(2,1)S(1)}, bf16[528,128]{1,0:T(8,128)(2,1)S(1)}, u32[]{:S(2)}, u32[]{:S(2)}) collective-permute-start(bf16[528,128]{1,0:T(8,128)(2,1)S(1)} %get-tuple-element.29), channel_id=1, source_target_pairs={{0,3},{4,7},{8,11},{12,15},{16,19},{20,23},{24,27},{28,31},{32,35}... | collective-permute-start | bytes 405512 | tf_op jit(solution)/shard_map/ppermute | solution.py:525
  32.6 11.3 %collective-permute-start.7 = (bf16[528,128]{1,0:T(8,128)(2,1)S(1)}, bf16[528,128]{1,0:T(8,128)(2,1)S(1)}, u32[]{:S(2)}, u32[]{:S(2)}) collective-permute-start(bf16[528,128]{1,0:T(8,128)(2,1)S(1)} %get-tuple-element.29), channel_id=1, source_target_pairs={{0,2},{1,3},{4,6},{5,7},{8,10},{9,11},{12,14},{13,15},{16,18},{17,... | collective-permute-start | bytes 405512 | tf_op jit(solution)/shard_map/ppermute | solution.py:525

commit v7 on v3

--- a/solution.py
+++ b/solution.py
@@ -152,7 +152,7 @@
         scratch_shapes=[
             pltpu.VMEM((2, steps, columns, bins), BF16),
             pltpu.VMEM((rows, columns), F32),
-            pltpu.SemaphoreType.DMA((2, 4)),
+            pltpu.SemaphoreType.DMA((2, 8)),
             pltpu.SemaphoreType.DMA,
         ],
         compiler_params=pltpu.CompilerParams(vmem_limit_bytes=8 * MIB),

time: 46.8 us -> 47 us (level)
  no operation moved by 1% of the time
where the time goes in v7:
time: 47 us; the launch traced here: 46.8 us
  Pallas kernels  23.1 us (49%)
  starting transfers between devices  18.9 us (40%)
  waiting for transfers between devices  4.68 us (10%)
    ppermute x5, starting transfers between devices, send(): return lax.ppermute(code, 'tm', [(i, i + hop) for i in range(blocks - hop)])  10.6 us
    pallas_call x1, Pallas kernels, inner_rows(): pl.pallas_call(functools.partial(inner_kernel, steps, rows), out_shape=[p...  8.58 us
    ppermute x1, starting transfers between devices, local(): lax.ppermute(outer_edge, 'space', between + [(j, i) for i, j in between])  8.12 us
    pallas_call x1, Pallas kernels, spread(): pl.pallas_call(functools.partial(spread_kernel, chunks, rows), out_shape=...  5.71 us
    ppermute x5, waiting for transfers between devices, send(): return lax.ppermute(code, 'tm', [(i, i + hop) for i in range(blocks - hop)])  4.67 us
    pallas_call x1, Pallas kernels, products(): pl.pallas_call(functools.partial(product_kernel, steps), out_shape=[pltpu...  3.22 us
    pallas_call x1, Pallas kernels, outer_row(): pl.pallas_call(functools.partial(outer_kernel, steps), out_shape=[pltpu.V...  2.46 us
    pallas_call x1, Pallas kernels, edges(): pl.pallas_call(functools.partial(edge_kernel, steps, rows), out_shape=[ja...  2.37 us
  transfers between devices with their start and end apart: 7, of which 1 were waited for; matrix products, arithmetic and copies ran while one was open for 0% of the time, Pallas kernels for 32%

profile of v7, /device:TPU:14, one launch (start us, length us, event | category | flops | bytes accessed | tf_op | source)
XLA Modules:
  0.0 46.8 jit_solution(18159441410351253801)
XLA Ops:
  0.0 2.4 %edges.1 = (bf16[16,256,128]{2,1,0:T(8,128)(2,1)S(1)}, bf16[16,256,128]{2,1,0:T(8,128)(2,1)S(1)}) custom-call(bf16[16,6,256,128]{3,2,1,0:T(8,128)(2,1)} %prev_ref.3, f32[6,256]{1,0:T(8,128)} %line_ref.3), custom_call_target="tpu_custom_call" | custom-call | tf_op jit(solution)/shard_map/edges/pallas_call | solution.py:147
  2.4 0.1 collective-permute-start
  2.5 8.1 %collective-permute-start.3 = (bf16[16,256,128]{2,1,0:T(8,128)(2,1)S(1)}, bf16[16,256,128]{2,1,0:T(8,128)(2,1)S(1)}, u32[]{:S(2)}, u32[]{:S(2)}) collective-permute-start(bf16[16,256,128]{2,1,0:T(8,128)(2,1)S(1)} %get-tuple-element.26), channel_id=1, source_target_pairs={{4,8},{12,16},{20,24},{28,32},{36,40},{44,48},{52,56},{60,64},{68,... | collective-permute-start | bytes 3145736 | tf_op jit(solution)/shard_map/ppermute | solution.py:528
  10.6 0.0 collective-permute-done.halo_ref
  10.6 8.6 %inner_rows.1 = (f32[16,5,256,128]{3,2,1,0:T(8,128)S(1)}, bf16[1296,128]{1,0:T(8,128)(2,1)S(1)}, f32[16,256,128]{2,1,0:T(8,128)S(1)}, f32[256,128]{1,0:T(8,128)S...) custom-call(bf16[16,6,256,128]{3,2,1,0:T(8,128)(2,1)} %prev_ref.3, ...), custom_call_target="tpu_custom_call" | custom-call | flops 3221225472 | bytes 6291456 | tf_op jit(solution)/shard_map/inner_rows/pallas_call | solution.py:267
  19.2 0.7 %collective-permute-start.2 = (bf16[1296,128]{1,0:T(8,128)(2,1)S(1)}, bf16[1296,128]{1,0:T(8,128)(2,1)S(1)}, u32[]{:S(2)}, u32[]{:S(2)}) collective-permute-start(bf16[1296,128]{1,0:T(8,128)(2,1)S(1)} %get-tuple-element.21.most_ref), channel_id=1, source_target_pairs={{0,3},{4,7},{8,11},{12,15},{16,19},{20,23},{24,27},{28,31},{32,35}... | collective-permute-start | bytes 995336 | tf_op jit(solution)/shard_map/ppermute | solution.py:532
  19.9 3.5 %collective-permute-start.1 = (bf16[1296,128]{1,0:T(8,128)(2,1)S(1)}, bf16[1296,128]{1,0:T(8,128)(2,1)S(1)}, u32[]{:S(2)}, u32[]{:S(2)}) collective-permute-start(bf16[1296,128]{1,0:T(8,128)(2,1)S(1)} %get-tuple-element.21.most_ref), channel_id=1, source_target_pairs={{0,1},{1,2},{2,3},{4,5},{5,6},{6,7},{8,9},{9,10},{10,11},{12,13},{... | collective-permute-start | bytes 995336 | tf_op jit(solution)/shard_map/ppermute | solution.py:532
  23.4 0.0 collective-permute-done.3.halo_ref
  23.4 2.5 %outer_row.1 = (f32[16,1,256,128]{3,2,1,0:T(8,128)S(1)}, bf16[272,128]{1,0:T(8,128)(2,1)S(1)}, bf16[1568,128]{1,0:T(8,128)(2,1)S(1)}) custom-call(bf16[16,256,128]{2,1,0:T(8,128)(2,1)S(1)} %collective-permute-done.3.halo_ref, f32[16,256,128]{2,1,0:T(8,128)S(1)} %get-tuple-element.27.part_ref, f32[256,128]{1,0:T(8,128)S(1)} %get-tuple-element.28.first_ref, ...), custom_call_target="tpu_custom_call" | custom-call | tf_op jit(solution)/shard_map/outer_row/pallas_call | solution.py:330
  25.9 3.9 %collective-permute-start.6 = (bf16[1568,128]{1,0:T(8,128)(2,1)S(1)}, bf16[1568,128]{1,0:T(8,128)(2,1)S(1)}, u32[]{:S(2)}, u32[]{:S(2)}) collective-permute-start(bf16[1568,128]{1,0:T(8,128)(2,1)S(1)} %get-tuple-element.31), channel_id=1, source_target_pairs={{0,2},{1,3},{4,6},{5,7},{8,10},{9,11},{12,14},{13,15},{16,18},{17,... | collective-permute-start | bytes 1204232 | tf_op jit(solution)/shard_map/ppermute | solution.py:532
  29.8 3.2 %products.1 = (bf16[16,256,256]{2,1,0:T(8,128)(2,1)S(1)}, bf16[2,256,256]{2,1,0:T(8,128)(2,1)S(1)}) custom-call(f32[64,128,128]{2,1,0:T(8,128)} %trans_ref.3), custom_call_target="tpu_custom_call" | custom-call | tf_op jit(solution)/shard_map/products/pallas_call | solution.py:380
  33.0 0.7 %collective-permute-start.5 = (bf16[272,128]{1,0:T(8,128)(2,1)S(1)}, bf16[272,128]{1,0:T(8,128)(2,1)S(1)}, u32[]{:S(2)}, u32[]{:S(2)}) collective-permute-start(bf16[272,128]{1,0:T(8,128)(2,1)S(1)} %get-tuple-element.30), channel_id=1, source_target_pairs={{0,3},{4,7},{8,11},{12,15},{16,19},{20,23},{24,27},{28,31},{32,35}... | collective-permute-start | bytes 208904 | tf_op jit(solution)/shard_map/ppermute | solution.py:532
  33.7 1.9 %collective-permute-start.4 = (bf16[272,128]{1,0:T(8,128)(2,1)S(1)}, bf16[272,128]{1,0:T(8,128)(2,1)S(1)}, u32[]{:S(2)}, u32[]{:S(2)}) collective-permute-start(bf16[272,128]{1,0:T(8,128)(2,1)S(1)} %get-tuple-element.30), channel_id=1, source_target_pairs={{0,1},{1,2},{2,3},{4,5},{5,6},{6,7},{8,9},{9,10},{10,11},{12,13},{... | collective-permute-start | bytes 208904 | tf_op jit(solution)/shard_map/ppermute | solution.py:532
  35.6 0.0 collective-permute-done.2.far_code
  35.6 0.0 collective-permute-done.1.near_code
  35.6 0.8 %ready.1 = (f32[5,256,128]{2,1,0:T(8,128)S(1)}, f32[5,256,128]{2,1,0:T(8,128)S(1)}) custom-call(bf16[1296,128]{1,0:T(8,128)(2,1)S(1)} %collective-permute-done.1.near_code, bf16[1296,128]{1,0:T(8,128)(2,1)S(1)} %collective-permute-done.2.far_code, f32[6,256,128]{2,1,0:T(8,128)S(1)} %get-tuple-element.22.keep_ref, ...), custom_call_target="tpu_custom_call" | custom-call | flops 4000000000 | bytes 8000000 | tf_op jit(solution)/shard_map/ready/pallas_call | solution.py:433
  36.4 0.0 collective-permute-done.5.far0_code
  36.4 4.7 %collective-permute-done.4.near0_code = bf16[272,128]{1,0:T(8,128)(2,1)S(1)} collective-permute-done((bf16[272,128]{1,0:T(8,128)(2,1)S(1)}, bf16[272,128]{1,0:T(8,128)(2,1)S(1)}, u32[]{:S(2)}, u32[]{:S(2)}) %collective-permute-start.4) | collective-permute-done | bytes 69664 | tf_op jit(solution)/shard_map/ppermute | solution.py:532
  41.1 0.0 collective-permute-done.6.mid_ref
  41.1 5.7 %spread.1 = bf16[16,6,256,128]{3,2,1,0:T(8,128)(2,1)} custom-call(f32[5,256,128]{2,1,0:T(8,128)S(1)} %get-tuple-element.24.near1_ref, f32[5,256,128]{2,1,0:T(8,128)S(1)} %get-tuple-element.25.far1_ref, bf16[272,128]{1,0:T(8,128)(2,1)S(1)} %collective-permute-done.4.near0_code, bf16[272,128]{1,0:T(8,128)(2,1)S(1)} %collective-permute-done.5.far0_code, ...), custom_call_target="tpu_custom_call" | custom-call | flops 3221225472 | bytes 6291456 | tf_op jit(solution)/shard_map/spread/pallas_call | solution.py:499
Async XLA Ops:
  2.4 8.2 %collective-permute-start = (bf16[16,256,128]{2,1,0:T(8,128)(2,1)S(1)}, bf16[16,256,128]{2,1,0:T(8,128)(2,1)S(1)}, u32[]{:S(2)}, u32[]{:S(2)}) collective-permute-start(bf16[16,256,128]{2,1,0:T(8,128)(2,1)S(1)} %get-tuple-element.20), channel_id=1, source_target_pairs={{0,4},{8,12},{16,20},{24,28},{32,36},{40,44},{48,52},{56,60},{64,6... | collective-permute-start | bytes 3145736 | tf_op jit(solution)/shard_map/ppermute | solution.py:529
  2.5 20.9 %collective-permute-start.3 = (bf16[16,256,128]{2,1,0:T(8,128)(2,1)S(1)}, bf16[16,256,128]{2,1,0:T(8,128)(2,1)S(1)}, u32[]{:S(2)}, u32[]{:S(2)}) collective-permute-start(bf16[16,256,128]{2,1,0:T(8,128)(2,1)S(1)} %get-tuple-element.26), channel_id=1, source_target_pairs={{4,8},{12,16},{20,24},{28,32},{36,40},{44,48},{52,56},{60,64},{68,... | collective-permute-start | bytes 3145736 | tf_op jit(solution)/shard_map/ppermute | solution.py:528
  19.2 16.4 %collective-permute-start.2 = (bf16[1296,128]{1,0:T(8,128)(2,1)S(1)}, bf16[1296,128]{1,0:T(8,128)(2,1)S(1)}, u32[]{:S(2)}, u32[]{:S(2)}) collective-permute-start(bf16[1296,128]{1,0:T(8,128)(2,1)S(1)} %get-tuple-element.21.most_ref), channel_id=1, source_target_pairs={{0,3},{4,7},{8,11},{12,15},{16,19},{20,23},{24,27},{28,31},{32,35}... | collective-permute-start | bytes 995336 | tf_op jit(solution)/shard_map/ppermute | solution.py:532
  19.9 15.7 %collective-permute-start.1 = (bf16[1296,128]{1,0:T(8,128)(2,1)S(1)}, bf16[1296,128]{1,0:T(8,128)(2,1)S(1)}, u32[]{:S(2)}, u32[]{:S(2)}) collective-permute-start(bf16[1296,128]{1,0:T(8,128)(2,1)S(1)} %get-tuple-element.21.most_ref), channel_id=1, source_target_pairs={{0,1},{1,2},{2,3},{4,5},{5,6},{6,7},{8,9},{9,10},{10,11},{12,13},{... | collective-permute-start | bytes 995336 | tf_op jit(solution)/shard_map/ppermute | solution.py:532
  25.9 15.2 %collective-permute-start.6 = (bf16[1568,128]{1,0:T(8,128)(2,1)S(1)}, bf16[1568,128]{1,0:T(8,128)(2,1)S(1)}, u32[]{:S(2)}, u32[]{:S(2)}) collective-permute-start(bf16[1568,128]{1,0:T(8,128)(2,1)S(1)} %get-tuple-element.31), channel_id=1, source_target_pairs={{0,2},{1,3},{4,6},{5,7},{8,10},{9,11},{12,14},{13,15},{16,18},{17,... | collective-permute-start | bytes 1204232 | tf_op jit(solution)/shard_map/ppermute | solution.py:532
  33.0 3.4 %collective-permute-start.5 = (bf16[272,128]{1,0:T(8,128)(2,1)S(1)}, bf16[272,128]{1,0:T(8,128)(2,1)S(1)}, u32[]{:S(2)}, u32[]{:S(2)}) collective-permute-start(bf16[272,128]{1,0:T(8,128)(2,1)S(1)} %get-tuple-element.30), channel_id=1, source_target_pairs={{0,3},{4,7},{8,11},{12,15},{16,19},{20,23},{24,27},{28,31},{32,35}... | collective-permute-start | bytes 208904 | tf_op jit(solution)/shard_map/ppermute | solution.py:532
  33.7 7.4 %collective-permute-start.4 = (bf16[272,128]{1,0:T(8,128)(2,1)S(1)}, bf16[272,128]{1,0:T(8,128)(2,1)S(1)}, u32[]{:S(2)}, u32[]{:S(2)}) collective-permute-start(bf16[272,128]{1,0:T(8,128)(2,1)S(1)} %get-tuple-element.30), channel_id=1, source_target_pairs={{0,1},{1,2},{2,3},{4,5},{5,6},{6,7},{8,9},{9,10},{10,11},{12,13},{... | collective-permute-start | bytes 208904 | tf_op jit(solution)/shard_map/ppermute | solution.py:532
